TPU v7x, 128 devices: a whole 4x4x4 slice. The times are simulated.
128 devices in a mesh: group: 8 (over z, core), member: 16 (over y, x).
Axes of the slice: x: 4, y: 4, z: 4, core: 2. Of those that a mesh axis runs over, the one named last changes fastest.
Arguments:
- query_hidden: bfloat16 [16384, 4096], P(('group', 'member')), may hold values from -8 to 8
- passage_hidden: bfloat16 [16384, 4096], P(('group', 'member')), may hold values from -8 to 8
- norm_gain: float32 [4096], replicated, may hold values from 0.5 to 1.5
- query_weight: float32 [16384], P(('group', 'member')), may hold values from 0.5 to 6
- hneg_ids: int32 [16384, 2], P(('group', 'member')), may hold values from 0 to 16383, as said below
Outputs:
- loss_rows: float32 [16384], P(('group', 'member'))
- query_grad: bfloat16 [16384, 4096], P(('group', 'member'))
- passage_grad: bfloat16 [16384, 4096], P(('group', 'member'))
- gain_grad: float32 [4096], replicated
Inputs may be any that keep to these rules, and one draw needn't show every extreme that they name: `hneg_ids`: among the 256 ids of one device's queries, no owner device (id // 128) is named more than 4 times; one owner device, the same for all devices, is named exactly 4 times by every device. No id equals its own query's row.
All inputs are finite; a program needn't handle non-finite values.
Results may differ from a plain program's by a relative error of at most 0.015.
Values may be sent and summed in bfloat16 or wider, within the bound.
No kernel may reach another device: no remote copies, remote signals or barrier semaphores. Data moves between devices by JAX's collectives and lax.ppermute only.
A program may use at most 128 MiB of HBM per device.

v0:
```python
import math

import jax
import jax.numpy as jnp
from jax import lax
from jax.experimental import pallas as pl
from jax.experimental.pallas import tpu as pltpu
from jax.sharding import Mesh, PartitionSpec as P

EPSILON = 1e-06
SOFTMAX_TEMPER = 0.28
RING = 4
CAP = 4
GROUPS = ("z", "c")
ALL_AXES = ("z", "c", "y", "x")
VMEM_BYTES = 60 * 1024 * 1024
LOW = -1e30


def shift(value, axis, step):
    return lax.ppermute(value, axis, [(i, (i + step) % RING) for i in range(RING)])


def ring_gather(block, axis):
    half = block.shape[0] // 2
    low, high = block[:half], block[half:]
    up_low = shift(low, axis, -1)
    down_high = shift(high, axis, 1)
    up_high = shift(high, axis, -1)
    down_low = shift(low, axis, 1)
    far_low = shift(up_low, axis, -1)
    far_high = shift(down_high, axis, 1)
    return [up_low, up_high, far_low, far_high, down_low, down_high]


def ring_scatter(blocks, axis):
    low_1, high_1, low_2, high_2, low_3, high_3 = blocks
    passing_low = shift(low_2, axis, 1)
    passing_high = shift(high_2, axis, -1)
    from_below_high = shift(high_1, axis, 1)
    from_above_low = shift(low_3, axis, -1)
    wide = jnp.float32
    both_low = (low_1.astype(wide) + passing_low.astype(wide)).astype(jnp.bfloat16)
    both_high = (high_3.astype(wide) + passing_high.astype(wide)).astype(jnp.bfloat16)
    from_below_low = shift(both_low, axis, 1)
    from_above_high = shift(both_high, axis, -1)
    return [from_below_low, from_above_low], [from_below_high, from_above_high]


def all_sum(value, z_size):
    value = value + lax.ppermute(value, "c", [(0, 1), (1, 0)])
    for axis, size in (("x", RING), ("y", RING), ("z", z_size)):
        value = value + lax.ppermute(value, axis, [(i, i ^ 1) for i in range(size)])
        value = value + lax.ppermute(value, axis, [(i, size - 1 - i) for i in range(size)])
    return value


def group_rows(rows, group_count):
    blocks = rows.reshape(group_count, rows.shape[0] // group_count, rows.shape[1])
    return lax.all_to_all(blocks, GROUPS, 0, 0, tiled=True).reshape(rows.shape)


def group_table(table, group_count):
    z_count = group_count // 2
    z_place, c_place = lax.axis_index("z"), lax.axis_index("c")
    got = jnp.zeros_like(table)
    places = jnp.arange(group_count, dtype=jnp.int32)[:, None]
    for z_step in range(z_count):
        for c_step in range(2):
            to_group = ((z_place + z_step) % z_count) * 2 + (c_place ^ c_step)
            from_group = ((z_place + z_count - z_step) % z_count) * 2 + (c_place ^ c_step)
            row = jnp.sum(jnp.where(places == to_group, table, 0), axis=0, keepdims=True)
            if z_step or c_step:
                row = lax.ppermute(
                    row,
                    GROUPS,
                    [
                        (z * 2 + c, ((z + z_step) % z_count) * 2 + (c ^ c_step))
                        for z in range(z_count)
                        for c in range(2)
                    ],
                )
            got = got + jnp.where(places == from_group, row, 0)
    return got


def line_table(table):
    x_place = lax.axis_index("x")
    places = jnp.arange(RING, dtype=jnp.int32)[:, None]
    got = jnp.where(places == x_place, table, 0)
    for step in range(1, RING):
        chosen = places == (x_place + step) % RING
        row = jnp.sum(jnp.where(chosen, table, 0), axis=0, keepdims=True)
        row = shift(row, "x", step)
        got = got + jnp.where(places == (x_place + RING - step) % RING, row, 0)
    return got


def mxu(left, right, left_dim=1, right_dim=0):
    return lax.dot_general(
        left, right, (((left_dim,), (right_dim,)), ((), ())), preferred_element_type=jnp.float32
    )


def params(steps_kind="arbitrary"):
    return pltpu.CompilerParams(
        dimension_semantics=(steps_kind,), vmem_limit_bytes=VMEM_BYTES
    )


SMALL = pl.CostEstimate(flops=1, bytes_accessed=1, transcendentals=0)


def tile(width):
    return min(512, width)


def whole(shape):
    return pl.BlockSpec(shape, lambda i: (0,) * len(shape))


def columns(rows, width):
    return pl.BlockSpec((rows, tile(width)), lambda i: (0, i))


def joined(refs):
    blocks = [ref[...] for ref in refs]
    return blocks[0] if len(blocks) == 1 else jnp.concatenate(blocks, axis=0)


def inverse_norm(values):
    return lax.rsqrt(jnp.mean(values * values, axis=-1, keepdims=True) + EPSILON)


def embed(hidden, gain):
    def body(hidden_ref, gain_ref, out_ref):
        values = hidden_ref[...].astype(jnp.float32)
        unit_rows = values * inverse_norm(values)
        out_ref[...] = (unit_rows * gain_ref[...]).astype(jnp.bfloat16)

    rows, width = hidden.shape
    step = min(64, rows)
    block = pl.BlockSpec((step, width), lambda i: (i, 0))
    return pl.pallas_call(
        body,
        grid=(rows // step,),
        in_specs=[block, whole((1, width))],
        out_specs=block,
        out_shape=jax.ShapeDtypeStruct((rows, width), jnp.bfloat16),
        compiler_params=params(),
        cost_estimate=SMALL,
        name="embed",
    )(hidden, gain)


def finish(hidden, gain, terms, low_terms, high_terms):
    rows, width = hidden.shape
    half = rows // 2
    step = half // 2
    count, low_count = len(terms), len(low_terms)

    def body(hidden_ref, gain_ref, *refs):
        out_ref = refs[-1]
        upstream = refs[0][...].astype(jnp.float32)
        for ref in refs[1:count]:
            upstream += ref[...].astype(jnp.float32)

        def done(total):
            values = hidden_ref[...].astype(jnp.float32)
            inverse = inverse_norm(values)
            unit_rows = values * inverse
            scaled = total * gain_ref[...]
            inner = jnp.mean(scaled * unit_rows, axis=-1, keepdims=True)
            out_ref[...] = (inverse * (scaled - unit_rows * inner)).astype(jnp.bfloat16)

        def add(total, extra):
            for ref in extra:
                total += ref[...].astype(jnp.float32)
            return total

        if low_count:
            low_half = pl.program_id(0) < half // step

            @pl.when(low_half)
            def _():
                done(add(upstream, refs[count : count + low_count]))

            @pl.when(jnp.logical_not(low_half))
            def _():
                done(add(upstream, refs[count + low_count : -1]))

        else:
            done(upstream)

    block = pl.BlockSpec((step, width), lambda i: (i, 0))
    per_half = half // step
    low = pl.BlockSpec((step, width), lambda i: (jnp.minimum(i, per_half - 1), 0))
    high = pl.BlockSpec((step, width), lambda i: (jnp.maximum(i - per_half, 0), 0))
    return pl.pallas_call(
        body,
        grid=(rows // step,),
        in_specs=[block, whole((1, width))]
        + [block] * count
        + [low] * low_count
        + [high] * len(high_terms),
        out_specs=block,
        out_shape=jax.ShapeDtypeStruct((rows, width), jnp.bfloat16),
        compiler_params=params(),
        cost_estimate=SMALL,
        name="finish",
    )(hidden, gain, *terms, *low_terms, *high_terms)


def pick_rows(matrix, sources):
    width = sources[0].shape[1]

    def body(matrix_ref, *refs):
        refs[-1][...] = mxu(matrix_ref[...], joined(refs[:-1])).astype(jnp.bfloat16)

    return pl.pallas_call(
        body,
        grid=(width // tile(width),),
        in_specs=[whole(matrix.shape)] + [columns(s.shape[0], width) for s in sources],
        out_specs=columns(matrix.shape[0], width),
        out_shape=jax.ShapeDtypeStruct((matrix.shape[0], width), jnp.bfloat16),
        compiler_params=params(),
        cost_estimate=SMALL,
        name="pick_rows",
    )(matrix, *sources)


def line_scores(sources, queries, scale):
    width = queries.shape[1]
    steps = width // tile(width)

    def body(query_ref, *refs):
        step = pl.program_id(0)
        out_ref = refs[-1]

        @pl.when(step == 0)
        def _():
            out_ref[...] = jnp.zeros_like(out_ref)

        out_ref[...] += scale * mxu(joined(refs[:-1]), query_ref[...], 1, 1)

    out = (sum(s.shape[0] for s in sources), queries.shape[0])
    return pl.pallas_call(
        body,
        grid=(steps,),
        in_specs=[columns(queries.shape[0], width)]
        + [columns(s.shape[0], width) for s in sources],
        out_specs=whole(out),
        out_shape=jax.ShapeDtypeStruct(out, jnp.float32),
        compiler_params=params(),
        cost_estimate=SMALL,
        name="line_scores",
    )(queries, *sources)


def far_scores(near, far_rows, queries, asked_by, line, scale):
    width = queries.shape[1]
    query_count = queries.shape[0]
    steps = width // tile(width)
    near_slots = near.shape[0] - line

    def body(near_ref, mask_ref, rows_ref, query_ref, out_ref, log_ref):
        step = pl.program_id(0)

        @pl.when(step == 0)
        def _():
            out_ref[...] = jnp.zeros_like(out_ref)

        out_ref[...] += scale * mxu(rows_ref[...], query_ref[...], 1, 1)

        @pl.when(step == steps - 1)
        def _():
            inner = near_ref[:line, :]
            own = jnp.where(mask_ref[:near_slots, :] > 0, near_ref[line:, :], LOW)
            far = jnp.where(mask_ref[near_slots:, :] > 0, out_ref[...], LOW)
            parts = (inner, own, far)
            top = jnp.max(inner, axis=0, keepdims=True)
            for part in parts[1:]:
                top = jnp.maximum(top, jnp.max(part, axis=0, keepdims=True))
            total = jnp.zeros_like(top)
            for part in parts:
                total += jnp.sum(jnp.exp(part - top), axis=0, keepdims=True)
            log_ref[...] = top + jnp.log(total)

    return pl.pallas_call(
        body,
        grid=(steps,),
        in_specs=[
            whole(near.shape),
            whole(asked_by.shape),
            columns(far_rows.shape[0], width),
            columns(query_count, width),
        ],
        out_specs=[whole((far_rows.shape[0], query_count)), whole((1, query_count))],
        out_shape=[
            jax.ShapeDtypeStruct((far_rows.shape[0], query_count), jnp.float32),
            jax.ShapeDtypeStruct((1, query_count), jnp.float32),
        ],
        compiler_params=params(),
        cost_estimate=SMALL,
        name="far_scores",
    )(near, asked_by, far_rows, queries)


def query_side(near, far, asked_by, log_total, weight, target, queries, sources, line, scale):
    width = queries.shape[1]
    query_count = queries.shape[0]
    near_slots = near.shape[0] - line
    slot_count = asked_by.shape[0]
    count = len(sources)

    def body(near_ref, far_ref, mask_ref, log_ref, weight_ref, target_ref, query_ref, *refs):
        source_refs = refs[:count]
        part_ref, gain_ref, coeff_ref, slot_ref, positive_ref, turned_ref = refs[count:]

        @pl.when(pl.program_id(0) == 0)
        def _():
            log_row, weight_row = log_ref[...], weight_ref[...]
            inner = near_ref[:line, :]
            row_place = lax.broadcasted_iota(jnp.int32, inner.shape, 0)
            hit = row_place == target_ref[...]
            positive_ref[...] = jnp.sum(jnp.where(hit, inner, 0.0), axis=0, keepdims=True)
            inner_coeff = weight_row * (jnp.exp(inner - log_row) - jnp.where(hit, 1.0, 0.0))
            coeff_ref[...] = inner_coeff.astype(jnp.bfloat16)
            own = jnp.where(mask_ref[:near_slots, :] > 0, near_ref[line:, :], LOW)
            slots = jnp.where(mask_ref[near_slots:, :] > 0, far_ref[...], LOW)
            own_coeff = (weight_row * jnp.exp(own - log_row)).astype(jnp.bfloat16)
            far_coeff = (weight_row * jnp.exp(slots - log_row)).astype(jnp.bfloat16)
            ones = jnp.ones((8, query_count), jnp.bfloat16)
            slot_ref[:, :near_slots] = mxu(ones, own_coeff, 1, 1)
            slot_ref[:, near_slots:] = mxu(ones, far_coeff, 1, 1)
            turned_ref[:, :line] = jnp.transpose(inner_coeff).astype(jnp.bfloat16)
            turned_ref[:, line : line + near_slots] = jnp.transpose(
                own_coeff.astype(jnp.float32)
            ).astype(jnp.bfloat16)
            turned_ref[:, line + near_slots :] = jnp.transpose(
                far_coeff.astype(jnp.float32)
            ).astype(jnp.bfloat16)

        total = scale * mxu(turned_ref[...], joined(source_refs))
        part_ref[...] = total.astype(jnp.bfloat16)
        gain_ref[...] = jnp.sum(total * query_ref[...].astype(jnp.float32), axis=0, keepdims=True)

    row = whole((1, query_count))
    return pl.pallas_call(
        body,
        grid=(width // tile(width),),
        in_specs=[
            whole(near.shape),
            whole(far.shape),
            whole(asked_by.shape),
            row,
            row,
            row,
            columns(query_count, width),
        ]
        + [columns(s.shape[0], width) for s in sources],
        out_specs=[
            columns(query_count, width),
            columns(1, width),
            whole((line, query_count)),
            whole((8, slot_count)),
            row,
        ],
        out_shape=[
            jax.ShapeDtypeStruct((query_count, width), jnp.bfloat16),
            jax.ShapeDtypeStruct((1, width), jnp.float32),
            jax.ShapeDtypeStruct((line, query_count), jnp.bfloat16),
            jax.ShapeDtypeStruct((8, slot_count), jnp.float32),
            jax.ShapeDtypeStruct((1, query_count), jnp.float32),
        ],
        scratch_shapes=[pltpu.VMEM((query_count, line + slot_count), jnp.bfloat16)],
        compiler_params=params(),
        cost_estimate=SMALL,
        name="query_side",
    )(near, far, asked_by, log_total, weight, target, queries, *sources)


def passage_side(coeff, queries, put, arrived, scale, out_type, pieces):
    width = queries.shape[1]
    rows = coeff.shape[0] // pieces

    def body(coeff_ref, query_ref, put_ref, arrived_ref, *out_refs):
        total = mxu(coeff_ref[...], query_ref[...]) + mxu(put_ref[...], arrived_ref[...])
        total = scale * total
        for i, out_ref in enumerate(out_refs):
            out_ref[...] = total[i * rows : (i + 1) * rows].astype(out_type)

    return pl.pallas_call(
        body,
        grid=(width // tile(width),),
        in_specs=[
            whole(coeff.shape),
            columns(queries.shape[0], width),
            whole(put.shape),
            columns(arrived.shape[0], width),
        ],
        out_specs=[columns(rows, width)] * pieces,
        out_shape=[jax.ShapeDtypeStruct((rows, width), out_type)] * pieces,
        compiler_params=params(),
        cost_estimate=SMALL,
        name="passage_side",
    )(coeff, queries, put, arrived)


def on_device(query_hidden, passage_hidden, norm_gain, query_weight, hneg_ids):
    rows, width = query_hidden.shape
    neg_count = hneg_ids.shape[1]
    z_count = lax.axis_size("z")
    group_count = 2 * z_count
    line = RING * rows
    scale = 1.0 / (SOFTMAX_TEMPER * math.sqrt(width))
    y_place, x_place = lax.axis_index("y"), lax.axis_index("x")

    gain = norm_gain.reshape(1, width)
    p_emb = embed(passage_hidden, gain)
    p_far = ring_gather(p_emb, "y")

    flat_ids = hneg_ids.reshape(-1)
    id_count = rows * neg_count
    owners = flat_ids // rows
    local_row = flat_ids % rows
    number = jnp.arange(id_count, dtype=jnp.int32)
    same = (owners[:, None] == owners[None, :]) & (number[None, :] < number[:, None])
    rank = jnp.sum(same.astype(jnp.int32), axis=1)
    y_step = (owners // RING - y_place) % RING
    line_of = (owners // (RING * RING)) * RING + owners % RING
    slot = (line_of * RING + y_step) * CAP + rank
    slot_count = group_count * RING * RING * CAP
    hit = slot[None, :] == jnp.arange(slot_count, dtype=jnp.int32)[:, None]
    slot_row = jnp.sum(jnp.where(hit, local_row[None, :] + 1, 0), axis=1) - 1
    slot_query = jnp.sum(jnp.where(hit, number[None, :] // neg_count + 1, 0), axis=1)
    slot_row, p_emb = lax.optimization_barrier((slot_row, p_emb))
    asked = lax.all_to_all(
        slot_row.reshape(group_count * RING, RING * CAP), ("z", "c", "x"), 0, 0, tiled=True
    )
    asked = asked.reshape(group_count, RING, RING, CAP).transpose(0, 2, 1, 3)
    y_base = rows * jnp.arange(RING - 1, dtype=jnp.int32)
    asked_own = asked[:, 0].reshape(-1)
    asked_far = jnp.where(
        asked[:, 1:] < 0, -1, asked[:, 1:] + y_base[None, :, None, None]
    ).reshape(-1)
    place = jnp.arange(line, dtype=jnp.int32)
    pick_own = (asked_own[:, None] == place[None, :rows]).astype(jnp.bfloat16)
    pick_far = (asked_far[:, None] == place[None, : line - rows]).astype(jnp.bfloat16)
    hard_own = group_rows(pick_rows(pick_own, [p_emb]), group_count)

    q_emb = embed(query_hidden, gain)
    q_line = lax.all_gather(q_emb, "x", axis=0, tiled=True)

    hard_far = group_rows(pick_rows(pick_far, p_far), group_count)

    by_x = slot_query.reshape(group_count, RING, RING * CAP).transpose(1, 0, 2)
    asker = line_table(by_x.reshape(RING, -1)).reshape(RING, group_count, RING, CAP)
    x_base = rows * jnp.arange(RING, dtype=jnp.int32)
    asker = jnp.where(asker == 0, -1, asker - 1 + x_base[:, None, None, None])
    asker = asker.transpose(1, 2, 0, 3)
    asker_own = asker[:, 0].reshape(-1)
    asker_far = asker[:, 1:].reshape(-1)
    send_own = (asker_own[:, None] == place[None, :]).astype(jnp.bfloat16)
    send_far = (asker_far[:, None] == place[None, :]).astype(jnp.bfloat16)
    asked_by = jnp.concatenate([send_own, send_far], axis=0)
    leave_far = pick_rows(send_far, [q_line])
    leave_own = pick_rows(send_own, [q_line])
    q_line, leave_far, leave_own = lax.optimization_barrier((q_line, leave_far, leave_own))
    far_queries = group_rows(leave_far, group_count)
    own_queries = group_rows(leave_own, group_count)

    near = line_scores([p_emb, *p_far, hard_own], q_line, scale)
    far, part_log = far_scores(near, hard_far, q_line, asked_by, line, scale)
    part_log = part_log.reshape(RING, rows)
    own_place = jnp.arange(RING, dtype=jnp.int32)[:, None] == x_place
    own_weight = jnp.where(own_place, query_weight[None, :], 0.0)
    message = jnp.concatenate([part_log, own_weight], axis=0)
    messages = [message] + [shift(message, "x", step) for step in (1, 3, 2)]
    logs = [m[:RING] for m in messages]
    weight = sum(m[RING:] for m in messages).reshape(1, line)
    top = jnp.maximum(jnp.maximum(logs[0], logs[1]), jnp.maximum(logs[2], logs[3]))
    log_total = (top + jnp.log(sum(jnp.exp(part - top) for part in logs))).reshape(1, line)
    first_row = x_place * rows
    target = place[None, :] - first_row
    target = jnp.where((target >= 0) & (target < rows), target, -1)

    part, gain_part, coeff, slot_coeff, positive = query_side(
        near, far, asked_by, log_total, weight, target, q_line,
        [p_emb, *p_far, hard_own, hard_far], line, scale,
    )
    loss_rows = lax.dynamic_slice(log_total - positive, (0, first_row), (1, rows)).reshape(-1)

    gain_grad = all_sum(gain_part.reshape(-1, 128), z_count).reshape(-1)
    gain_grad = 2.0 * gain_grad / norm_gain

    query_up = lax.psum_scatter(part, "x", scatter_dimension=0, tiled=True)
    query_grad = finish(query_hidden, gain, [query_up], [], [])

    own_slots = asker_own.shape[0]
    slot_own = slot_coeff[0, :own_slots].reshape(group_count, -1)
    slot_far = slot_coeff[0, own_slots:].reshape(group_count, -1)
    got_coeff = group_table(jnp.concatenate([slot_own, slot_far], axis=1), group_count)
    per_group = own_slots // group_count
    coeff_in_own = got_coeff[:, :per_group].reshape(-1)
    coeff_in_far = got_coeff[:, per_group:].reshape(-1)
    put_far = jnp.where(
        place[: line - rows, None] == asked_far[None, :], coeff_in_far[None, :], 0.0
    ).astype(jnp.bfloat16)
    put_own = jnp.where(
        place[:rows, None] == asked_own[None, :], coeff_in_own[None, :], 0.0
    ).astype(jnp.bfloat16)
    far_part = passage_side(
        coeff[rows:], q_line, put_far, far_queries, scale, jnp.bfloat16, 2 * (RING - 1)
    )
    low_terms, high_terms = ring_scatter(far_part, "y")
    own_part = passage_side(coeff[:rows], q_line, put_own, own_queries, scale, jnp.float32, 1)[0]
    passage_grad = finish(passage_hidden, gain, [own_part], low_terms, high_terms)
    return (loss_rows, query_grad, passage_grad, gain_grad)


def solution(mesh):
    torus = Mesh(mesh.devices.reshape(-1, 2, RING, RING), ALL_AXES)
    return jax.shard_map(
        on_device,
        mesh=torus,
        in_specs=(
            P(ALL_AXES, None),
            P(ALL_AXES, None),
            P(),
            P(ALL_AXES),
            P(ALL_AXES, None),
        ),
        out_specs=(
            P(ALL_AXES),
            P(ALL_AXES, None),
            P(ALL_AXES, None),
            P(),
        ),
        check_vma=False,
    )
```

profile of v0, /device:TPU:0, one launch (start us, length us, event | category | flops | bytes accessed | tf_op | source)
XLA Modules:
  0.0 285.5 jit_solution(11727587723795962481)
XLA Ops:
  13.5 8.2 %all-to-all-start = ((s32[32,1,16]{2,1,0:T(1,128)}), s32[32,1,16]{2,1,0:T(1,128)S(1)}, u32[]{:S(2)}, u32[]{:S(2)}) async-start(s32[32,1,16]{2,1,0:T(1,128)} %bitcast.4), calls=%async_computation | async-start | bytes 32768 | tf_op jit(solution)/shard_map/all_to_all | solution.py:438
  30.2 5.8 %pick_rows.6 = bf16[128,4096]{1,0:T(8,128)(2,1)} custom-call(bf16[128,128]{1,0:T(8,128)(2,1)} %compare_convert_fusion.1.matrix_ref, bf16[128,4096]{1,0:T(8,128)(2,1)} %embed.3.refs_0_), custom_call_target="tpu_custom_call" | custom-call | flops 1 | bytes 1 | tf_op jit(solution)/shard_map/pick_rows/pallas_call | solution.py:220
  36.0 3.6 %all-to-all-start.1 = ((bf16[8,16,4096]{2,1,0:T(8,128)(2,1)}), bf16[8,16,4096]{2,1,0:T(8,128)(2,1)S(1)}, u32[]{:S(2)}, u32[]{:S(2)}) async-start(bf16[8,16,4096]{2,1,0:T(8,128)(2,1)} %bitcast.55), calls=%async_computation.1 | async-start | bytes 2097152 | tf_op jit(solution)/shard_map/all_to_all | solution.py:60
  47.3 8.0 %collective-permute-done.4.refs_2_.refs_1_ = bf16[64,4096]{1,0:T(8,128)(2,1)S(1)} collective-permute-done((bf16[64,4096]{1,0:T(8,128)(2,1)}, bf16[64,4096]{1,0:T(8,128)(2,1)S(1)}, u32[]{:S(2)}, u32[]{:S(2)}) %collective-permute-start.4) | collective-permute-done | bytes 524320 | tf_op jit(solution)/shard_map/ppermute | solution.py:21
  55.2 3.6 %collective-permute-done.8.refs_5_.refs_4_ = bf16[64,4096]{1,0:T(8,128)(2,1)S(1)} collective-permute-done((bf16[64,4096]{1,0:T(8,128)(2,1)}, bf16[64,4096]{1,0:T(8,128)(2,1)S(1)}, u32[]{:S(2)}, u32[]{:S(2)}) %collective-permute-start.8) | collective-permute-done | bytes 524320 | tf_op jit(solution)/shard_map/ppermute | solution.py:21
  58.9 6.9 %collective-permute-done.5.refs_3_.refs_2_ = bf16[64,4096]{1,0:T(8,128)(2,1)} collective-permute-done((bf16[64,4096]{1,0:T(8,128)(2,1)S(1)}, bf16[64,4096]{1,0:T(8,128)(2,1)}, u32[]{:S(2)}, u32[]{:S(2)}) %collective-permute-start.5) | collective-permute-done | bytes 524320 | tf_op jit(solution)/shard_map/ppermute | solution.py:21
  69.3 7.7 %pick_rows.7 = bf16[384,4096]{1,0:T(8,128)(2,1)} custom-call(bf16[384,384]{1,0:T(8,128)(2,1)} %compare_convert_fusion.matrix_ref, bf16[64,4096]{1,0:T(8,128)(2,1)} %copy-done.3, bf16[64,4096]{1,0:T(8,128)(2,1)} %copy-done.5, bf16[64,4096]{1,0:T(8,128)(2,1)} %collective-permute-done.5.refs_3_.refs_2_, ...), custom_call_target="tpu_custom_call" | custom-call | flops 1 | bytes 1 | tf_op jit(solution)/shard_map/pick_rows/pallas_call | solution.py:220
  78.0 4.5 %all-to-all-start.2 = ((bf16[8,48,4096]{2,1,0:T(8,128)(2,1)}), bf16[8,48,4096]{2,1,0:T(8,128)(2,1)S(1)}, u32[]{:S(2)}, u32[]{:S(2)}) async-start(bf16[8,48,4096]{2,1,0:T(8,128)(2,1)} %bitcast.50), calls=%async_computation.2 | async-start | bytes 6291456 | tf_op jit(solution)/shard_map/all_to_all | solution.py:60
  94.4 7.8 %pick_rows.4 = bf16[384,4096]{1,0:T(8,128)(2,1)} custom-call(bf16[384,512]{1,0:T(8,128)(2,1)} %copy-done.8, bf16[512,4096]{1,0:T(8,128)(2,1)} %all-gather.2.cloned.1.call-done.refs_0_.query_ref), custom_call_target="tpu_custom_call" | custom-call | flops 1 | bytes 1 | tf_op jit(solution)/shard_map/pick_rows/pallas_call | solution.py:220
  102.2 6.7 %pick_rows.5 = bf16[128,4096]{1,0:T(8,128)(2,1)} custom-call(bf16[128,512]{1,0:T(8,128)(2,1)} %copy-done.9, bf16[512,4096]{1,0:T(8,128)(2,1)} %all-gather.2.cloned.1.call-done.refs_0_.query_ref), custom_call_target="tpu_custom_call" | custom-call | flops 1 | bytes 1 | tf_op jit(solution)/shard_map/pick_rows/pallas_call | solution.py:220
  108.8 9.2 %line_scores.1.near_ref = f32[640,512]{1,0:T(8,128)} custom-call(bf16[512,4096]{1,0:T(8,128)(2,1)} %all-gather.2.cloned.1.call-done.refs_0_.query_ref, bf16[128,4096]{1,0:T(8,128)(2,1)} %embed.3.refs_0_, bf16[64,4096]{1,0:T(8,128)(2,1)} %copy-done.3, bf16[64,4096]{1,0:T(8,128)(2,1)} %copy-done.5, bf16[64,4096]{1,0:T(8,128)(2,1)} %collective-permute-done.5.refs_3_.refs_2_, ...), custom_call_target="tpu_custom_call" | custom-call | flops 1 | bytes 1 | tf_op jit(solution)/shard_map/line_scores/pallas_call | solution.py:247
  122.6 9.1 %far_scores.1 = (f32[384,512]{1,0:T(8,128)}, f32[1,512]{1,0:T(1,128)}) custom-call(f32[640,512]{1,0:T(8,128)} %line_scores.1.near_ref, bf16[512,512]{1,0:T(8,128)(2,1)} %pad_maximum_fusion.mask_ref, bf16[384,4096]{1,0:T(8,128)(2,1)} %bitcast.48, bf16[512,4096]{1,0:T(8,128)(2,1)} %all-gather.2.cloned.1.call-done.refs_0_.query_ref), custom_call_target="tpu_custom_call" | custom-call | flops 1 | bytes 1 | tf_op jit(solution)/shard_map/far_scores/pallas_call | solution.py:289
  141.6 13.0 %query_side.1 = (bf16[512,4096]{1,0:T(8,128)(2,1)}, f32[1,4096]{1,0:T(1,128)}, bf16[512,512]{1,0:T(8,128)(2,1)}, f32[8,512]{1,0:T(8,128)}, f32[1,512]{1,0:T(1,128)}) custom-call(f32[640,512]{1,0:T(8,128)} %line_scores.1.near_ref, f32[384,512]{1,0:T(8,128)} %get-tuple-element.26.far_ref, bf16[512,512]{1,0:T(8,128)(2,1)} %pad_maximum_fusion.mask_ref, ...), custom_call_target="tpu_custom_call" | custom-call | flops 1 | bytes 1 | tf_op jit(solution)/shard_map/query_side/pallas_call | solution.py:349
  154.6 3.8 %all-to-all-start.4 = ((bf16[8,48,4096]{2,1,0:T(8,128)(2,1)}), bf16[8,48,4096]{2,1,0:T(8,128)(2,1)S(1)}, u32[]{:S(2)}, u32[]{:S(2)}) async-start(bf16[8,48,4096]{2,1,0:T(8,128)(2,1)} %bitcast.30), calls=%async_computation.5 | async-start | bytes 6291456 | tf_op jit(solution)/shard_map/all_to_all | solution.py:60
  168.4 24.7 %collective-permute-done.13 = f32[1,64]{1,0:T(1,128)S(1)} collective-permute-done((f32[1,64]{1,0:T(1,128)S(1)}, f32[1,64]{1,0:T(1,128)S(1)}, u32[]{:S(2)}, u32[]{:S(2)}) %collective-permute-start.13) | collective-permute-done | bytes 288 | tf_op jit(solution)/shard_map/ppermute | solution.py:74
  201.1 8.8 %passage_side.3 = (bf16[64,4096]{1,0:T(8,128)(2,1)}, bf16[64,4096]{1,0:T(8,128)(2,1)}, bf16[64,4096]{1,0:T(8,128)(2,1)}, bf16[64,4096]{1,0:T(8,128)(2,1)}, bf16[...) custom-call(bf16[384,512]{1,0:T(8,128)(2,1)} %slice.85.coeff_ref, ...), custom_call_target="tpu_custom_call" | custom-call | flops 1 | bytes 1 | tf_op jit(solution)/shard_map/passage_side/pallas_call | solution.py:393
  211.7 3.7 %collective-permute-done.26 = f32[32,128]{1,0:T(8,128)S(1)} collective-permute-done((f32[32,128]{1,0:T(8,128)S(1)}, f32[32,128]{1,0:T(8,128)S(1)}, u32[]{:S(2)}, u32[]{:S(2)}) %collective-permute-start.26) | collective-permute-done | bytes 16416 | tf_op jit(solution)/shard_map/ppermute | solution.py:53
  215.9 4.5 %collective-permute-done.27 = f32[32,128]{1,0:T(8,128)S(1)} collective-permute-done((f32[32,128]{1,0:T(8,128)S(1)}, f32[32,128]{1,0:T(8,128)S(1)}, u32[]{:S(2)}, u32[]{:S(2)}) %collective-permute-start.27) | collective-permute-done | bytes 16416 | tf_op jit(solution)/shard_map/ppermute | solution.py:54
  225.2 3.6 %all-to-all-start.3 = ((bf16[8,16,4096]{2,1,0:T(8,128)(2,1)}), bf16[8,16,4096]{2,1,0:T(8,128)(2,1)S(1)}, u32[]{:S(2)}, u32[]{:S(2)}) async-start(bf16[8,16,4096]{2,1,0:T(8,128)(2,1)} %bitcast.56), calls=%async_computation.4 | async-start | bytes 2097152 | tf_op jit(solution)/shard_map/all_to_all | solution.py:60
  239.3 7.7 %collective-permute-done.19 = bf16[64,4096]{1,0:T(8,128)(2,1)S(1)} collective-permute-done((bf16[64,4096]{1,0:T(8,128)(2,1)}, bf16[64,4096]{1,0:T(8,128)(2,1)S(1)}, u32[]{:S(2)}, u32[]{:S(2)}) %collective-permute-start.19) | collective-permute-done | bytes 524320 | tf_op jit(solution)/shard_map/ppermute | solution.py:21
  257.5 7.2 %passage_side.2.refs_0_ = f32[128,4096]{1,0:T(8,128)} custom-call(bf16[128,512]{1,0:T(8,128)(2,1)} %slice.81.coeff_ref, bf16[512,4096]{1,0:T(8,128)(2,1)} %all-gather.2.cloned.1.call-done.refs_0_.query_ref, bf16[128,128]{1,0:T(8,128)(2,1)} %select_convert_fusion.1.put_ref, bf16[128,4096]{1,0:T(8,128)(2,1)} %bitcast.54), custom_call_target="tpu_custom_call" | custom-call | flops 1 | bytes 1 | tf_op jit(solution)/shard_map/passage_side/pallas_call | solution.py:393
  264.7 4.0 %collective-permute-done.20.refs_1_ = bf16[64,4096]{1,0:T(8,128)(2,1)S(1)} collective-permute-done((bf16[64,4096]{1,0:T(8,128)(2,1)}, bf16[64,4096]{1,0:T(8,128)(2,1)S(1)}, u32[]{:S(2)}, u32[]{:S(2)}) %collective-permute-start.20) | collective-permute-done | bytes 524320 | tf_op jit(solution)/shard_map/ppermute | solution.py:21
  269.5 5.0 %finish.3 = bf16[128,4096]{1,0:T(8,128)(2,1)} custom-call(bf16[128,4096]{1,0:T(8,128)(2,1)} %hidden_ref.7, f32[1,4096]{1,0:T(1,128)} %bitcast.59, f32[128,4096]{1,0:T(8,128)} %passage_side.2.refs_0_, bf16[64,4096]{1,0:T(8,128)(2,1)} %copy-done.14, bf16[64,4096]{1,0:T(8,128)(2,1)} %copy-done.11, bf16[64,4096]{1,0:T(8,128)(2,1)} %copy-done.12, ...), custom_call_target="tpu_custom_call" | custom-call | flops 1 | bytes 1 | tf_op jit(solution)/shard_map/finish/pallas_call | solution.py:199
  274.5 4.2 %finish.2 = bf16[128,4096]{1,0:T(8,128)(2,1)} custom-call(bf16[128,4096]{1,0:T(8,128)(2,1)} %hidden_ref.6, f32[1,4096]{1,0:T(1,128)} %bitcast.60, bf16[128,4096]{1,0:T(8,128)(2,1)} %reduce-scatter.2.cloned.1.call-done.refs_0_), custom_call_target="tpu_custom_call" | custom-call | flops 1 | bytes 1 | tf_op jit(solution)/shard_map/finish/pallas_call | solution.py:199
  (203 shorter events, 99.6 us)
Async XLA Ops:
  7.2 87.2 %all-gather.2.cloned.1.call-start = ((), (), s32[]{:S(2)}) async-start(), calls=%async_computation.6 | async-start | bytes 5242880 | tf_op jit(solution)/shard_map/all_gather | solution.py:453
  24.2 18.5 %collective-permute-start.3 = (bf16[64,4096]{1,0:T(8,128)(2,1)}, bf16[64,4096]{1,0:T(8,128)(2,1)S(1)}, u32[]{:S(2)}, u32[]{:S(2)}) collective-permute-start(bf16[64,4096]{1,0:T(8,128)(2,1)} %get-tuple-element.54), channel_id=1, source_target_pairs={{0,12},{4,0},{8,4},{12,8},{1,13},{5,1},{9,5},{13,9},{2,14},{6,2},{... | collective-permute-start | bytes 1572872 | tf_op jit(solution)/shard_map/ppermute | solution.py:21
  27.2 18.7 %collective-permute-start.6 = (bf16[64,4096]{1,0:T(8,128)(2,1)}, bf16[64,4096]{1,0:T(8,128)(2,1)S(1)}, u32[]{:S(2)}, u32[]{:S(2)}) collective-permute-start(bf16[64,4096]{1,0:T(8,128)(2,1)} %get-tuple-element.53), channel_id=1, source_target_pairs={{0,4},{4,8},{8,12},{12,0},{1,5},{5,9},{9,13},{13,1},{2,6},{6,10},{... | collective-permute-start | bytes 1572872 | tf_op jit(solution)/shard_map/ppermute | solution.py:21
  36.0 41.0 %all-to-all-start.1 = ((bf16[8,16,4096]{2,1,0:T(8,128)(2,1)}), bf16[8,16,4096]{2,1,0:T(8,128)(2,1)S(1)}, u32[]{:S(2)}, u32[]{:S(2)}) async-start(bf16[8,16,4096]{2,1,0:T(8,128)(2,1)} %bitcast.55), calls=%async_computation.1 | async-start | bytes 2097152 | tf_op jit(solution)/shard_map/all_to_all | solution.py:60
  39.6 15.7 %collective-permute-start.4 = (bf16[64,4096]{1,0:T(8,128)(2,1)}, bf16[64,4096]{1,0:T(8,128)(2,1)S(1)}, u32[]{:S(2)}, u32[]{:S(2)}) collective-permute-start(bf16[64,4096]{1,0:T(8,128)(2,1)} %get-tuple-element.53), channel_id=1, source_target_pairs={{0,12},{4,0},{8,4},{12,8},{1,13},{5,1},{9,5},{13,9},{2,14},{6,2},{... | collective-permute-start | bytes 1572872 | tf_op jit(solution)/shard_map/ppermute | solution.py:21
  42.7 16.2 %collective-permute-start.8 = (bf16[64,4096]{1,0:T(8,128)(2,1)}, bf16[64,4096]{1,0:T(8,128)(2,1)S(1)}, u32[]{:S(2)}, u32[]{:S(2)}) collective-permute-start(bf16[64,4096]{1,0:T(8,128)(2,1)} %get-tuple-element.54), channel_id=1, source_target_pairs={{0,4},{4,8},{8,12},{12,0},{1,5},{5,9},{9,13},{13,1},{2,6},{6,10},{... | collective-permute-start | bytes 1572872 | tf_op jit(solution)/shard_map/ppermute | solution.py:21
  42.7 23.1 %collective-permute-start.5 = (bf16[64,4096]{1,0:T(8,128)(2,1)S(1)}, bf16[64,4096]{1,0:T(8,128)(2,1)}, u32[]{:S(2)}, u32[]{:S(2)}) collective-permute-start(bf16[64,4096]{1,0:T(8,128)(2,1)S(1)} %collective-permute-done.3.refs_1_.refs_0_), channel_id=1, source_target_pairs={{0,12},{4,0},{8,4},{12,8},{1,13},{5,1},{9,5},{13,9},{2,14},{6,2},{... | collective-permute-start | bytes 1572872 | tf_op jit(solution)/shard_map/ppermute | solution.py:21
  45.9 23.4 %collective-permute-start.7 = (bf16[64,4096]{1,0:T(8,128)(2,1)S(1)}, bf16[64,4096]{1,0:T(8,128)(2,1)}, u32[]{:S(2)}, u32[]{:S(2)}) collective-permute-start(bf16[64,4096]{1,0:T(8,128)(2,1)S(1)} %collective-permute-done.6.refs_6_.refs_5_), channel_id=1, source_target_pairs={{0,4},{4,8},{8,12},{12,0},{1,5},{5,9},{9,13},{13,1},{2,6},{6,10},{... | collective-permute-start | bytes 1572872 | tf_op jit(solution)/shard_map/ppermute | solution.py:21
  78.0 42.9 %all-to-all-start.2 = ((bf16[8,48,4096]{2,1,0:T(8,128)(2,1)}), bf16[8,48,4096]{2,1,0:T(8,128)(2,1)S(1)}, u32[]{:S(2)}, u32[]{:S(2)}) async-start(bf16[8,48,4096]{2,1,0:T(8,128)(2,1)} %bitcast.50), calls=%async_computation.2 | async-start | bytes 6291456 | tf_op jit(solution)/shard_map/all_to_all | solution.py:60
  82.4 192.0 %reduce-scatter.2.cloned.1.call-start = ((), (), s32[]{:S(2)}) async-start(), calls=%async_computation.7 | async-start | bytes 5242880 | tf_op jit(solution)/shard_map/reduce_scatter | solution.py:497
  154.6 44.8 %all-to-all-start.4 = ((bf16[8,48,4096]{2,1,0:T(8,128)(2,1)}), bf16[8,48,4096]{2,1,0:T(8,128)(2,1)S(1)}, u32[]{:S(2)}, u32[]{:S(2)}) async-start(bf16[8,48,4096]{2,1,0:T(8,128)(2,1)} %bitcast.30), calls=%async_computation.5 | async-start | bytes 6291456 | tf_op jit(solution)/shard_map/all_to_all | solution.py:60
  160.5 32.6 %collective-permute-start.13 = (f32[1,64]{1,0:T(1,128)S(1)}, f32[1,64]{1,0:T(1,128)S(1)}, u32[]{:S(2)}, u32[]{:S(2)}) collective-permute-start(f32[1,64]{1,0:T(1,128)S(1)} %bitcast.86), channel_id=1, source_target_pairs={{0,32},{16,48},{32,64},{48,80},{64,96},{80,112},{96,0},{112,16},{1... | collective-permute-start | bytes 776 | tf_op jit(solution)/shard_map/ppermute | solution.py:74
  162.2 36.1 %collective-permute-start.14 = (f32[1,64]{1,0:T(1,128)S(1)}, f32[1,64]{1,0:T(1,128)S(1)}, u32[]{:S(2)}, u32[]{:S(2)}) collective-permute-start(f32[1,64]{1,0:T(1,128)S(1)} %bitcast.84), channel_id=1, source_target_pairs={{0,48},{16,32},{32,80},{48,64},{64,112},{80,96},{96,16},{112,0},{1... | collective-permute-start | bytes 776 | tf_op jit(solution)/shard_map/ppermute | solution.py:74
  163.4 35.0 %collective-permute-start.15 = (f32[1,64]{1,0:T(1,128)S(1)}, f32[1,64]{1,0:T(1,128)S(1)}, u32[]{:S(2)}, u32[]{:S(2)}) collective-permute-start(f32[1,64]{1,0:T(1,128)S(1)} %bitcast.83), channel_id=1, source_target_pairs={{0,64},{16,80},{32,96},{48,112},{64,0},{80,16},{96,32},{112,48},{1... | collective-permute-start | bytes 776 | tf_op jit(solution)/shard_map/ppermute | solution.py:74
  164.9 33.4 %collective-permute-start.16 = (f32[1,64]{1,0:T(1,128)S(1)}, f32[1,64]{1,0:T(1,128)S(1)}, u32[]{:S(2)}, u32[]{:S(2)}) collective-permute-start(f32[1,64]{1,0:T(1,128)S(1)} %bitcast.81), channel_id=1, source_target_pairs={{0,80},{16,64},{32,112},{48,96},{64,16},{80,0},{96,48},{112,32},{1... | collective-permute-start | bytes 776 | tf_op jit(solution)/shard_map/ppermute | solution.py:74
  166.7 31.7 %collective-permute-start.17 = (f32[1,64]{1,0:T(1,128)S(1)}, f32[1,64]{1,0:T(1,128)S(1)}, u32[]{:S(2)}, u32[]{:S(2)}) collective-permute-start(f32[1,64]{1,0:T(1,128)S(1)} %bitcast.79), channel_id=1, source_target_pairs={{0,96},{16,112},{32,0},{48,16},{64,32},{80,48},{96,64},{112,80},{1... | collective-permute-start | bytes 776 | tf_op jit(solution)/shard_map/ppermute | solution.py:74
  210.0 24.2 %collective-permute-start.23 = (bf16[64,4096]{1,0:T(8,128)(2,1)}, bf16[64,4096]{1,0:T(8,128)(2,1)S(1)}, u32[]{:S(2)}, u32[]{:S(2)}) collective-permute-start(bf16[64,4096]{1,0:T(8,128)(2,1)} %get-tuple-element.38), channel_id=1, source_target_pairs={{0,12},{4,0},{8,4},{12,8},{1,13},{5,1},{9,5},{13,9},{2,14},{6,2},{... | collective-permute-start | bytes 1572872 | tf_op jit(solution)/shard_map/ppermute | solution.py:21
  225.2 31.3 %all-to-all-start.3 = ((bf16[8,16,4096]{2,1,0:T(8,128)(2,1)}), bf16[8,16,4096]{2,1,0:T(8,128)(2,1)S(1)}, u32[]{:S(2)}, u32[]{:S(2)}) async-start(bf16[8,16,4096]{2,1,0:T(8,128)(2,1)} %bitcast.56), calls=%async_computation.4 | async-start | bytes 2097152 | tf_op jit(solution)/shard_map/all_to_all | solution.py:60
  230.1 20.7 %collective-permute-start.30 = (f32[32,128]{1,0:T(8,128)S(1)}, f32[32,128]{1,0:T(8,128)S(1)}, u32[]{:S(2)}, u32[]{:S(2)}) collective-permute-start(f32[32,128]{1,0:T(8,128)S(1)} %add.371), channel_id=1, source_target_pairs={{0,32},{32,0},{64,96},{96,64},{1,33},{33,1},{65,97},{97,65},{2,34}... | collective-permute-start | bytes 49160 | tf_op jit(solution)/shard_map/ppermute | solution.py:53
  230.8 16.2 %collective-permute-start.19 = (bf16[64,4096]{1,0:T(8,128)(2,1)}, bf16[64,4096]{1,0:T(8,128)(2,1)S(1)}, u32[]{:S(2)}, u32[]{:S(2)}) collective-permute-start(bf16[64,4096]{1,0:T(8,128)(2,1)} %get-tuple-element.34), channel_id=1, source_target_pairs={{0,4},{4,8},{8,12},{12,0},{1,5},{5,9},{9,13},{13,1},{2,6},{6,10},{... | collective-permute-start | bytes 1572872 | tf_op jit(solution)/shard_map/ppermute | solution.py:21
  232.1 32.5 %collective-permute-start.21 = (bf16[64,4096]{1,0:T(8,128)(2,1)}, bf16[64,4096]{1,0:T(8,128)(2,1)S(1)}, u32[]{:S(2)}, u32[]{:S(2)}) collective-permute-start(bf16[64,4096]{1,0:T(8,128)(2,1)} %get-tuple-element.35), channel_id=1, source_target_pairs={{0,12},{4,0},{8,4},{12,8},{1,13},{5,1},{9,5},{13,9},{2,14},{6,2},{... | collective-permute-start | bytes 1572872 | tf_op jit(solution)/shard_map/ppermute | solution.py:21
  234.0 30.6 %collective-permute-start.22 = (bf16[64,4096]{1,0:T(8,128)(2,1)}, bf16[64,4096]{1,0:T(8,128)(2,1)S(1)}, u32[]{:S(2)}, u32[]{:S(2)}) collective-permute-start(bf16[64,4096]{1,0:T(8,128)(2,1)} %get-tuple-element.36), channel_id=1, source_target_pairs={{0,4},{4,8},{8,12},{12,0},{1,5},{5,9},{9,13},{13,1},{2,6},{6,10},{... | collective-permute-start | bytes 1572872 | tf_op jit(solution)/shard_map/ppermute | solution.py:21
  236.1 28.5 %collective-permute-start.24 = (bf16[64,4096]{1,0:T(8,128)(2,1)}, bf16[64,4096]{1,0:T(8,128)(2,1)S(1)}, u32[]{:S(2)}, u32[]{:S(2)}) collective-permute-start(bf16[64,4096]{1,0:T(8,128)(2,1)} %add_convert_fusion), channel_id=1, source_target_pairs={{0,12},{4,0},{8,4},{12,8},{1,13},{5,1},{9,5},{13,9},{2,14},{6,2},{... | collective-permute-start | bytes 1572872 | tf_op jit(solution)/shard_map/ppermute | solution.py:21
  247.9 20.7 %collective-permute-start.20 = (bf16[64,4096]{1,0:T(8,128)(2,1)}, bf16[64,4096]{1,0:T(8,128)(2,1)S(1)}, u32[]{:S(2)}, u32[]{:S(2)}) collective-permute-start(bf16[64,4096]{1,0:T(8,128)(2,1)} %add_convert_fusion.1), channel_id=1, source_target_pairs={{0,4},{4,8},{8,12},{12,0},{1,5},{5,9},{9,13},{13,1},{2,6},{6,10},{... | collective-permute-start | bytes 1572872 | tf_op jit(solution)/shard_map/ppermute | solution.py:21
  (40 other events, 433.9 us)
Sparse Core Ops, SparseCore 0:
  10.2 50.6 all-gather.1
  154.7 42.0 reduce-scatter.1
where the time goes:
time: 288 us; the launch traced here: 286 us
  Pallas kernels  89.3 us (31%)
  waiting for transfers between devices  82.2 us (29%)
  starting transfers between devices  66.1 us (23%)
  local copies, waits for them, and re-layouts  18.1 us (6%)
  other arithmetic  15.2 us (5%)
  between operations  14.6 us (5%)
    ppermute x18, waiting for transfers between devices, shift(): lax.ppermute(value, axis, [(i, (i + step) % RING) for i in range(RING)])  37.1 us
    pallas_call x4, Pallas kernels, pick_rows(): pl.pallas_call(body, grid=(width // tile(width),), in_specs=[whole(matrix...  28 us
    ppermute x18, starting transfers between devices, shift(): lax.ppermute(value, axis, [(i, (i + step) % RING) for i in range(RING)])  25.4 us
    ppermute x7, waiting for transfers between devices, group_table(): lax.ppermute(row, GROUPS, [(z * 2 + c, (z + z_step) % z_count * 2 + (c ^...  24.7 us
    pallas_call x2, Pallas kernels, passage_side(): pl.pallas_call(body, grid=(width // tile(width),), in_specs=[whole(coeff....  16 us
    all_to_all x4, starting transfers between devices, group_rows(): return lax.all_to_all(blocks, GROUPS, 0, 0, tiled=True).reshape(rows.shape)  15.4 us
    pallas_call x1, Pallas kernels, query_side(): pl.pallas_call(body, grid=(width // tile(width),), in_specs=[whole(near.s...  13 us
    ppermute x7, starting transfers between devices, group_table(): lax.ppermute(row, GROUPS, [(z * 2 + c, (z + z_step) % z_count * 2 + (c ^...  11.5 us
  transfers between devices with their start and end apart: 39, of which 17 were waited for; matrix products, arithmetic and copies ran while one was open for 8% of the time, Pallas kernels for 21%

commit v1 on v0

--- a/solution.py
+++ b/solution.py
@@ -13,7 +13,7 @@
 CAP = 4
 GROUPS = ("z", "c")
 ALL_AXES = ("z", "c", "y", "x")
-VMEM_BYTES = 60 * 1024 * 1024
+MIB = 1024 * 1024
 LOW = -1e30
 
 
@@ -21,20 +21,19 @@
     return lax.ppermute(value, axis, [(i, (i + step) % RING) for i in range(RING)])
 
 
-def ring_gather(block, axis):
-    half = block.shape[0] // 2
-    low, high = block[:half], block[half:]
+def ring_gather(low, high, axis):
     up_low = shift(low, axis, -1)
     down_high = shift(high, axis, 1)
     up_high = shift(high, axis, -1)
     down_low = shift(low, axis, 1)
     far_low = shift(up_low, axis, -1)
     far_high = shift(down_high, axis, 1)
-    return [up_low, up_high, far_low, far_high, down_low, down_high]
-
-
-def ring_scatter(blocks, axis):
-    low_1, high_1, low_2, high_2, low_3, high_3 = blocks
+    return [up_low, up_high, down_low, down_high], [far_low, far_high]
+
+
+def ring_scatter(opposite, beside, axis):
+    low_2, high_2 = opposite
+    low_1, high_1, low_3, high_3 = beside
     passing_low = shift(low_2, axis, 1)
     passing_high = shift(high_2, axis, -1)
     from_below_high = shift(high_1, axis, 1)
@@ -44,12 +43,12 @@
     both_high = (high_3.astype(wide) + passing_high.astype(wide)).astype(jnp.bfloat16)
     from_below_low = shift(both_low, axis, 1)
     from_above_high = shift(both_high, axis, -1)
-    return [from_below_low, from_above_low], [from_below_high, from_above_high]
+    return [from_below_low, from_above_low], [from_below_high, from_above_high], both_high
 
 
 def all_sum(value, z_size):
     value = value + lax.ppermute(value, "c", [(0, 1), (1, 0)])
-    for axis, size in (("x", RING), ("y", RING), ("z", z_size)):
+    for axis, size in (("x", RING), ("z", z_size), ("y", RING)):
         value = value + lax.ppermute(value, axis, [(i, i ^ 1) for i in range(size)])
         value = value + lax.ppermute(value, axis, [(i, size - 1 - i) for i in range(size)])
     return value
@@ -102,17 +101,16 @@
     )
 
 
-def params(steps_kind="arbitrary"):
-    return pltpu.CompilerParams(
-        dimension_semantics=(steps_kind,), vmem_limit_bytes=VMEM_BYTES
-    )
+def params(mib):
+    return pltpu.CompilerParams(dimension_semantics=("arbitrary",), vmem_limit_bytes=mib * MIB)
 
 
 SMALL = pl.CostEstimate(flops=1, bytes_accessed=1, transcendentals=0)
+LARGE = pl.CostEstimate(flops=10**11, bytes_accessed=10**8, transcendentals=0)
 
 
 def tile(width):
-    return min(512, width)
+    return min(1024, width)
 
 
 def whole(shape):
@@ -132,22 +130,34 @@
     return lax.rsqrt(jnp.mean(values * values, axis=-1, keepdims=True) + EPSILON)
 
 
-def embed(hidden, gain):
-    def body(hidden_ref, gain_ref, out_ref):
+def embed(hidden, gain, pieces):
+    def body(hidden_ref, gain_ref, *out_refs):
         values = hidden_ref[...].astype(jnp.float32)
         unit_rows = values * inverse_norm(values)
-        out_ref[...] = (unit_rows * gain_ref[...]).astype(jnp.bfloat16)
+        rounded_rows = (unit_rows * gain_ref[...]).astype(jnp.bfloat16)
+        for i, out_ref in enumerate(out_refs):
+
+            @pl.when(pl.program_id(0) // per_piece == i)
+            def _(out_ref=out_ref):
+                out_ref[...] = rounded_rows
 
     rows, width = hidden.shape
-    step = min(64, rows)
+    step = min(32, rows // pieces)
+    per_piece = rows // pieces // step
     block = pl.BlockSpec((step, width), lambda i: (i, 0))
+
+    def piece(at):
+        return pl.BlockSpec(
+            (step, width), lambda i: (jnp.clip(i - at * per_piece, 0, per_piece - 1), 0)
+        )
+
     return pl.pallas_call(
         body,
         grid=(rows // step,),
         in_specs=[block, whole((1, width))],
-        out_specs=block,
-        out_shape=jax.ShapeDtypeStruct((rows, width), jnp.bfloat16),
-        compiler_params=params(),
+        out_specs=[piece(at) for at in range(pieces)],
+        out_shape=[jax.ShapeDtypeStruct((rows // pieces, width), jnp.bfloat16)] * pieces,
+        compiler_params=params(12),
         cost_estimate=SMALL,
         name="embed",
     )(hidden, gain)
@@ -205,7 +215,7 @@
         + [high] * len(high_terms),
         out_specs=block,
         out_shape=jax.ShapeDtypeStruct((rows, width), jnp.bfloat16),
-        compiler_params=params(),
+        compiler_params=params(16),
         cost_estimate=SMALL,
         name="finish",
     )(hidden, gain, *terms, *low_terms, *high_terms)
@@ -223,7 +233,7 @@
         in_specs=[whole(matrix.shape)] + [columns(s.shape[0], width) for s in sources],
         out_specs=columns(matrix.shape[0], width),
         out_shape=jax.ShapeDtypeStruct((matrix.shape[0], width), jnp.bfloat16),
-        compiler_params=params(),
+        compiler_params=params(16),
         cost_estimate=SMALL,
         name="pick_rows",
     )(matrix, *sources)
@@ -251,26 +261,28 @@
         + [columns(s.shape[0], width) for s in sources],
         out_specs=whole(out),
         out_shape=jax.ShapeDtypeStruct(out, jnp.float32),
-        compiler_params=params(),
+        compiler_params=params(20),
         cost_estimate=SMALL,
         name="line_scores",
     )(queries, *sources)
 
 
-def far_scores(near, far_rows, queries, asked_by, line, scale):
+def far_scores(near, sources, queries, asked_by, line, scale):
     width = queries.shape[1]
     query_count = queries.shape[0]
     steps = width // tile(width)
     near_slots = near.shape[0] - line
-
-    def body(near_ref, mask_ref, rows_ref, query_ref, out_ref, log_ref):
+    far_slots = asked_by.shape[0] - near_slots
+
+    def body(near_ref, mask_ref, query_ref, *refs):
+        out_ref, log_ref = refs[-2:]
         step = pl.program_id(0)
 
         @pl.when(step == 0)
         def _():
             out_ref[...] = jnp.zeros_like(out_ref)
 
-        out_ref[...] += scale * mxu(rows_ref[...], query_ref[...], 1, 1)
+        out_ref[...] += scale * mxu(joined(refs[:-2]), query_ref[...], 1, 1)
 
         @pl.when(step == steps - 1)
         def _():
@@ -292,18 +304,18 @@
         in_specs=[
             whole(near.shape),
             whole(asked_by.shape),
-            columns(far_rows.shape[0], width),
             columns(query_count, width),
-        ],
-        out_specs=[whole((far_rows.shape[0], query_count)), whole((1, query_count))],
+        ]
+        + [columns(s.shape[0], width) for s in sources],
+        out_specs=[whole((far_slots, query_count)), whole((1, query_count))],
         out_shape=[
-            jax.ShapeDtypeStruct((far_rows.shape[0], query_count), jnp.float32),
+            jax.ShapeDtypeStruct((far_slots, query_count), jnp.float32),
             jax.ShapeDtypeStruct((1, query_count), jnp.float32),
         ],
-        compiler_params=params(),
-        cost_estimate=SMALL,
+        compiler_params=params(28),
+        cost_estimate=LARGE,
         name="far_scores",
-    )(near, asked_by, far_rows, queries)
+    )(near, asked_by, queries, *sources)
 
 
 def query_side(near, far, asked_by, log_total, weight, target, queries, sources, line, scale):
@@ -312,10 +324,13 @@
     near_slots = near.shape[0] - line
     slot_count = asked_by.shape[0]
     count = len(sources)
+    rows = line // RING
+    cuts = (rows, 3 * rows)
 
     def body(near_ref, far_ref, mask_ref, log_ref, weight_ref, target_ref, query_ref, *refs):
         source_refs = refs[:count]
-        part_ref, gain_ref, coeff_ref, slot_ref, positive_ref, turned_ref = refs[count:]
+        part_ref, gain_ref, slot_ref, positive_ref = refs[count : count + 4]
+        coeff_refs, turned_ref = refs[count + 4 : -1], refs[-1]
 
         @pl.when(pl.program_id(0) == 0)
         def _():
@@ -325,7 +340,10 @@
             hit = row_place == target_ref[...]
             positive_ref[...] = jnp.sum(jnp.where(hit, inner, 0.0), axis=0, keepdims=True)
             inner_coeff = weight_row * (jnp.exp(inner - log_row) - jnp.where(hit, 1.0, 0.0))
-            coeff_ref[...] = inner_coeff.astype(jnp.bfloat16)
+            at = 0
+            for coeff_ref, size in zip(coeff_refs, cuts):
+                coeff_ref[...] = inner_coeff[at : at + size].astype(jnp.bfloat16)
+                at += size
             own = jnp.where(mask_ref[:near_slots, :] > 0, near_ref[line:, :], LOW)
             slots = jnp.where(mask_ref[near_slots:, :] > 0, far_ref[...], LOW)
             own_coeff = (weight_row * jnp.exp(own - log_row)).astype(jnp.bfloat16)
@@ -362,19 +380,19 @@
         out_specs=[
             columns(query_count, width),
             columns(1, width),
-            whole((line, query_count)),
             whole((8, slot_count)),
             row,
-        ],
+        ]
+        + [whole((size, query_count)) for size in cuts],
         out_shape=[
             jax.ShapeDtypeStruct((query_count, width), jnp.bfloat16),
             jax.ShapeDtypeStruct((1, width), jnp.float32),
-            jax.ShapeDtypeStruct((line, query_count), jnp.bfloat16),
             jax.ShapeDtypeStruct((8, slot_count), jnp.float32),
             jax.ShapeDtypeStruct((1, query_count), jnp.float32),
-        ],
+        ]
+        + [jax.ShapeDtypeStruct((size, query_count), jnp.bfloat16) for size in cuts],
         scratch_shapes=[pltpu.VMEM((query_count, line + slot_count), jnp.bfloat16)],
-        compiler_params=params(),
+        compiler_params=params(32),
         cost_estimate=SMALL,
         name="query_side",
     )(near, far, asked_by, log_total, weight, target, queries, *sources)
@@ -401,8 +419,8 @@
         ],
         out_specs=[columns(rows, width)] * pieces,
         out_shape=[jax.ShapeDtypeStruct((rows, width), out_type)] * pieces,
-        compiler_params=params(),
-        cost_estimate=SMALL,
+        compiler_params=params(20),
+        cost_estimate=LARGE if pieces > 1 else SMALL,
         name="passage_side",
     )(coeff, queries, put, arrived)
 
@@ -417,8 +435,8 @@
     y_place, x_place = lax.axis_index("y"), lax.axis_index("x")
 
     gain = norm_gain.reshape(1, width)
-    p_emb = embed(passage_hidden, gain)
-    p_far = ring_gather(p_emb, "y")
+    p_own = embed(passage_hidden, gain, 2)
+    p_mid, p_opp = ring_gather(*p_own, "y")
 
     flat_ids = hneg_ids.reshape(-1)
     id_count = rows * neg_count
@@ -434,35 +452,36 @@
     hit = slot[None, :] == jnp.arange(slot_count, dtype=jnp.int32)[:, None]
     slot_row = jnp.sum(jnp.where(hit, local_row[None, :] + 1, 0), axis=1) - 1
     slot_query = jnp.sum(jnp.where(hit, number[None, :] // neg_count + 1, 0), axis=1)
-    slot_row, p_emb = lax.optimization_barrier((slot_row, p_emb))
     asked = lax.all_to_all(
         slot_row.reshape(group_count * RING, RING * CAP), ("z", "c", "x"), 0, 0, tiled=True
     )
     asked = asked.reshape(group_count, RING, RING, CAP).transpose(0, 2, 1, 3)
-    y_base = rows * jnp.arange(RING - 1, dtype=jnp.int32)
+    place = jnp.arange(line, dtype=jnp.int32)
+    asked, _ = lax.optimization_barrier((asked, p_mid))
     asked_own = asked[:, 0].reshape(-1)
-    asked_far = jnp.where(
-        asked[:, 1:] < 0, -1, asked[:, 1:] + y_base[None, :, None, None]
-    ).reshape(-1)
-    place = jnp.arange(line, dtype=jnp.int32)
-    pick_own = (asked_own[:, None] == place[None, :rows]).astype(jnp.bfloat16)
-    pick_far = (asked_far[:, None] == place[None, : line - rows]).astype(jnp.bfloat16)
-    hard_own = group_rows(pick_rows(pick_own, [p_emb]), group_count)
-
-    q_emb = embed(query_hidden, gain)
+    above = jnp.where(asked[:, 3:] < 0, -1, asked[:, 3:] + rows)
+    opposite = jnp.where(asked[:, 2:3] < 0, -1, asked[:, 2:3] + 2 * rows)
+    asked_far = jnp.concatenate([asked[:, 1:2], above, opposite], axis=1).reshape(-1)
+
+    def one_hot(numbers, size):
+        return (numbers[:, None] == place[None, :size]).astype(jnp.bfloat16)
+
+    chosen_own = pick_rows(one_hot(asked_own, rows), p_own)
+    hard_own = group_rows(chosen_own, group_count)
+    chosen_far = pick_rows(one_hot(asked_far, 3 * rows), [*p_mid, *p_opp])
+    hard_far = group_rows(chosen_far, group_count)
+
+    q_emb = embed(query_hidden, gain, 1)[0]
     q_line = lax.all_gather(q_emb, "x", axis=0, tiled=True)
-
-    hard_far = group_rows(pick_rows(pick_far, p_far), group_count)
 
     by_x = slot_query.reshape(group_count, RING, RING * CAP).transpose(1, 0, 2)
     asker = line_table(by_x.reshape(RING, -1)).reshape(RING, group_count, RING, CAP)
     x_base = rows * jnp.arange(RING, dtype=jnp.int32)
     asker = jnp.where(asker == 0, -1, asker - 1 + x_base[:, None, None, None])
     asker = asker.transpose(1, 2, 0, 3)
-    asker_own = asker[:, 0].reshape(-1)
-    asker_far = asker[:, 1:].reshape(-1)
-    send_own = (asker_own[:, None] == place[None, :]).astype(jnp.bfloat16)
-    send_far = (asker_far[:, None] == place[None, :]).astype(jnp.bfloat16)
+    far_asker = jnp.concatenate([asker[:, 1:2], asker[:, 3:], asker[:, 2:3]], axis=1)
+    send_own = one_hot(asker[:, 0].reshape(-1), line)
+    send_far = one_hot(far_asker.reshape(-1), line)
     asked_by = jnp.concatenate([send_own, send_far], axis=0)
     leave_far = pick_rows(send_far, [q_line])
     leave_own = pick_rows(send_own, [q_line])
@@ -470,8 +489,8 @@
     far_queries = group_rows(leave_far, group_count)
     own_queries = group_rows(leave_own, group_count)
 
-    near = line_scores([p_emb, *p_far, hard_own], q_line, scale)
-    far, part_log = far_scores(near, hard_far, q_line, asked_by, line, scale)
+    near = line_scores([*p_own, *p_mid, *p_opp, hard_own], q_line, scale)
+    far, part_log = far_scores(near, [hard_far], q_line, asked_by, line, scale)
     part_log = part_log.reshape(RING, rows)
     own_place = jnp.arange(RING, dtype=jnp.int32)[:, None] == x_place
     own_weight = jnp.where(own_place, query_weight[None, :], 0.0)
@@ -485,36 +504,37 @@
     target = place[None, :] - first_row
     target = jnp.where((target >= 0) & (target < rows), target, -1)
 
-    part, gain_part, coeff, slot_coeff, positive = query_side(
+    part, gain_part, slot_coeff, positive, coeff_own, coeff_far = query_side(
         near, far, asked_by, log_total, weight, target, q_line,
-        [p_emb, *p_far, hard_own, hard_far], line, scale,
+        [*p_own, *p_mid, *p_opp, hard_own, hard_far], line, scale,
     )
     loss_rows = lax.dynamic_slice(log_total - positive, (0, first_row), (1, rows)).reshape(-1)
-
+    query_up = lax.psum_scatter(part, "x", scatter_dimension=0, tiled=True)
+    query_grad = finish(query_hidden, gain, [query_up], [], [])
+
+    own_end = group_count * RING * CAP
+    pieces = (
+        slot_coeff[0, :own_end].reshape(group_count, -1),
+        slot_coeff[0, own_end:].reshape(group_count, -1),
+    )
+    got_coeff = group_table(jnp.concatenate(pieces, axis=1), group_count)
+    first = RING * CAP
+
+    def put_rows(numbers, values, size):
+        return jnp.where(
+            place[:size, None] == numbers[None, :], values.reshape(-1)[None, :], 0.0
+        ).astype(jnp.bfloat16)
+
+    put_own = put_rows(asked_own, got_coeff[:, :first], rows)
+    put_far = put_rows(asked_far, got_coeff[:, first:], 3 * rows)
+    far_part = passage_side(coeff_far, q_line, put_far, far_queries, scale, jnp.bfloat16, 6)
+    low_terms, high_terms, passed = ring_scatter(far_part[4:], far_part[:4], "y")
+    gain_part, _ = lax.optimization_barrier((gain_part, passed))
     gain_grad = all_sum(gain_part.reshape(-1, 128), z_count).reshape(-1)
     gain_grad = 2.0 * gain_grad / norm_gain
 
-    query_up = lax.psum_scatter(part, "x", scatter_dimension=0, tiled=True)
-    query_grad = finish(query_hidden, gain, [query_up], [], [])
-
-    own_slots = asker_own.shape[0]
-    slot_own = slot_coeff[0, :own_slots].reshape(group_count, -1)
-    slot_far = slot_coeff[0, own_slots:].reshape(group_count, -1)
-    got_coeff = group_table(jnp.concatenate([slot_own, slot_far], axis=1), group_count)
-    per_group = own_slots // group_count
-    coeff_in_own = got_coeff[:, :per_group].reshape(-1)
-    coeff_in_far = got_coeff[:, per_group:].reshape(-1)
-    put_far = jnp.where(
-        place[: line - rows, None] == asked_far[None, :], coeff_in_far[None, :], 0.0
-    ).astype(jnp.bfloat16)
-    put_own = jnp.where(
-        place[:rows, None] == asked_own[None, :], coeff_in_own[None, :], 0.0
-    ).astype(jnp.bfloat16)
-    far_part = passage_side(
-        coeff[rows:], q_line, put_far, far_queries, scale, jnp.bfloat16, 2 * (RING - 1)
-    )
-    low_terms, high_terms = ring_scatter(far_part, "y")
-    own_part = passage_side(coeff[:rows], q_line, put_own, own_queries, scale, jnp.float32, 1)[0]
+    own_part = passage_side(coeff_own, q_line, put_own, own_queries, scale, jnp.float32, 1)[0]
+    own_part, query_grad = lax.optimization_barrier((own_part, query_grad))
     passage_grad = finish(passage_hidden, gain, [own_part], low_terms, high_terms)
     return (loss_rows, query_grad, passage_grad, gain_grad)
 

time: 288 us -> 250 us (0.87)
  Pallas kernels: 89.3 us -> 46.4 us
  local copies, waits for them, and re-layouts: 18.1 us -> 28.9 us
  waiting for transfers between devices: 82.2 us -> 74.1 us
  starting transfers between devices: 66.1 us -> 73.3 us
  other arithmetic: 15.2 us -> 10.5 us
    ppermute x7, waiting for transfers between devices: 24.7 us -> 1.3 us  [group_table(): lax.ppermute(row, GROUPS, [(z * 2 + c, (z + z_step) % z_count * 2 + (c ^...]
    unnamed x51 -> x135, local copies, waits for them, and re-layouts: 6.85 us -> 24.8 us
    pallas_call x4, Pallas kernels: 28 us -> 11.5 us  [pick_rows(): pl.pallas_call(body, grid=(width // tile(width),), in_specs=[whole(matrix...]
    ppermute x3, waiting for transfers between devices: 6.84 us -> 15.5 us  [all_sum(): value = value + lax.ppermute(value, axis, [(i, i ^ 1) for i in range(size)])]
    pallas_call x2, Pallas kernels: 16 us -> 8.26 us  [passage_side(): pl.pallas_call(body, grid=(width // tile(width),), in_specs=[whole(coeff....]
    slice x11 -> x6, local copies, waits for them, and re-layouts: 7.53 us -> 0.23 us  [the longest x2 0.11 us: on_device(): send_own = one_hot(asker[:, 0].reshape(-1), line)]
    all_to_all x1, waiting for transfers between devices: 1.81 us -> 7.24 us  [on_device(): lax.all_to_all(slot_row.reshape(group_count * RING, RING * CAP), ('z', 'c...]
    pallas_call x1, Pallas kernels: 9.1 us -> 3.67 us  [far_scores(): pl.pallas_call(body, grid=(steps,), in_specs=[whole(near.shape), whole(as...]
  transfers between devices with their start and end apart: 39 -> 39, of which waited for: 17 -> 15; matrix products, arithmetic and copies ran while one was open for 8% -> 6% of each run, Pallas kernels for 21% -> 16%
where the time goes in v1:
time: 250 us; the launch traced here: 248 us
  waiting for transfers between devices  74.1 us (30%)
  starting transfers between devices  73.3 us (29%)
  Pallas kernels  46.4 us (19%)
  local copies, waits for them, and re-layouts  28.9 us (12%)
  between operations  15 us (6%)
  other arithmetic  10.5 us (4%)
    ppermute x18, waiting for transfers between devices, shift(): lax.ppermute(value, axis, [(i, (i + step) % RING) for i in range(RING)])  34.7 us
    ppermute x18, starting transfers between devices, shift(): lax.ppermute(value, axis, [(i, (i + step) % RING) for i in range(RING)])  25.6 us
    unnamed x135, local copies, waits for them, and re-layouts  24.8 us
    all_to_all x4, starting transfers between devices, group_rows(): return lax.all_to_all(blocks, GROUPS, 0, 0, tiled=True).reshape(rows.shape)  19.6 us
    ppermute x3, waiting for transfers between devices, all_sum(): value = value + lax.ppermute(value, axis, [(i, i ^ 1) for i in range(size)])  15.5 us
    pallas_call x4, Pallas kernels, pick_rows(): pl.pallas_call(body, grid=(width // tile(width),), in_specs=[whole(matrix...  11.5 us
    ppermute x7, starting transfers between devices, group_table(): lax.ppermute(row, GROUPS, [(z * 2 + c, (z + z_step) % z_count * 2 + (c ^...  9.86 us
    pallas_call x2, Pallas kernels, passage_side(): pl.pallas_call(body, grid=(width // tile(width),), in_specs=[whole(coeff....  8.26 us
  transfers between devices with their start and end apart: 39, of which 15 were waited for; matrix products, arithmetic and copies ran while one was open for 6% of the time, Pallas kernels for 16%

profile of v1, /device:TPU:0, one launch (start us, length us, event | category | flops | bytes accessed | tf_op | source)
XLA Modules:
  0.0 248.2 jit_solution(3248089601092143129)
XLA Ops:
  18.8 8.2 %all-to-all-start = ((s32[32,1,16]{2,1,0:T(1,128)}), s32[32,1,16]{2,1,0:T(1,128)S(1)}, u32[]{:S(2)}, u32[]{:S(2)}) async-start(s32[32,1,16]{2,1,0:T(1,128)} %bitcast.4), calls=%async_computation | async-start | bytes 32768 | tf_op jit(solution)/shard_map/all_to_all | solution.py:455
  27.1 7.2 %all-to-all-done = s32[32,1,16]{2,1,0:T(1,128)S(1)} async-done(((s32[32,1,16]{2,1,0:T(1,128)}), s32[32,1,16]{2,1,0:T(1,128)S(1)}, u32[]{:S(2)}, u32[]{:S(2)}) %all-to-all-start) | async-done | bytes 2080 | tf_op jit(solution)/shard_map/all_to_all | solution.py:455
  34.5 3.9 %collective-permute-done.3.refs_2_.refs_0_ = bf16[64,4096]{1,0:T(8,128)(2,1)S(1)} collective-permute-done((bf16[64,4096]{1,0:T(8,128)(2,1)S(1)}, bf16[64,4096]{1,0:T(8,128)(2,1)S(1)}, u32[]{:S(2)}, u32[]{:S(2)}) %collective-permute-start.3) | collective-permute-done | bytes 524320 | tf_op jit(solution)/shard_map/ppermute | solution.py:21
  40.8 5.3 %all-to-all-start.1 = ((bf16[8,16,4096]{2,1,0:T(8,128)(2,1)}), bf16[8,16,4096]{2,1,0:T(8,128)(2,1)S(1)}, u32[]{:S(2)}, u32[]{:S(2)}) async-start(bf16[8,16,4096]{2,1,0:T(8,128)(2,1)} %bitcast.54), calls=%async_computation.1 | async-start | bytes 2097152 | tf_op jit(solution)/shard_map/all_to_all | solution.py:59
  46.2 3.0 %collective-permute-start.7 = (bf16[64,4096]{1,0:T(8,128)(2,1)S(1)}, bf16[64,4096]{1,0:T(8,128)(2,1)}, u32[]{:S(2)}, u32[]{:S(2)}) collective-permute-start(bf16[64,4096]{1,0:T(8,128)(2,1)S(1)} %collective-permute-done.3.refs_2_.refs_0_), channel_id=1, source_target_pairs={{0,12},{4,0},{8,4},{12,8},{1,13},{5,1},{9,5},{13,9},{2,14},{6,2},{... | collective-permute-start | bytes 1572872 | tf_op jit(solution)/shard_map/ppermute | solution.py:21
  49.7 11.3 %collective-permute-done.7.refs_6_.refs_4_ = bf16[64,4096]{1,0:T(8,128)(2,1)} collective-permute-done((bf16[64,4096]{1,0:T(8,128)(2,1)S(1)}, bf16[64,4096]{1,0:T(8,128)(2,1)}, u32[]{:S(2)}, u32[]{:S(2)}) %collective-permute-start.7) | collective-permute-done | bytes 524320 | tf_op jit(solution)/shard_map/ppermute | solution.py:21
  61.0 3.5 %collective-permute-done.8.refs_7_.refs_5_ = bf16[64,4096]{1,0:T(8,128)(2,1)} collective-permute-done((bf16[64,4096]{1,0:T(8,128)(2,1)S(1)}, bf16[64,4096]{1,0:T(8,128)(2,1)}, u32[]{:S(2)}, u32[]{:S(2)}) %collective-permute-start.8) | collective-permute-done | bytes 524320 | tf_op jit(solution)/shard_map/ppermute | solution.py:21
  64.5 5.1 %pick_rows.7 = bf16[384,4096]{1,0:T(8,128)(2,1)} custom-call(bf16[384,384]{1,0:T(8,128)(2,1)S(1)} %compare_convert_fusion.matrix_ref, bf16[64,4096]{1,0:T(8,128)(2,1)S(1)} %collective-permute-done.3.refs_2_.refs_0_, bf16[64,4096]{1,0:T(8,128)(2,1)S(1)} %collective-permute-done.4.refs_3_.refs_1_, bf16[64,4096]{1,0:T(8,128)(2,1)S(1)} %collective-permute-done.5.refs_4_.refs_2_, ...), custom_call_target="tpu_custom_call" | custom-call | flops 1 | bytes 1 | tf_op jit(solution)/shard_map/pick_rows/pallas_call | solution.py:230
  70.6 4.6 %all-to-all-start.2 = ((bf16[8,48,4096]{2,1,0:T(8,128)(2,1)}), bf16[8,48,4096]{2,1,0:T(8,128)(2,1)S(1)}, u32[]{:S(2)}, u32[]{:S(2)}) async-start(bf16[8,48,4096]{2,1,0:T(8,128)(2,1)} %bitcast.8), calls=%async_computation.2 | async-start | bytes 6291456 | tf_op jit(solution)/shard_map/all_to_all | solution.py:59
  99.4 5.2 %line_scores.1.near_ref = f32[640,512]{1,0:T(8,128)S(1)} custom-call(bf16[512,4096]{1,0:T(8,128)(2,1)S(1)} %copy-done.1, bf16[64,4096]{1,0:T(8,128)(2,1)S(1)} %copy-done.26, bf16[64,4096]{1,0:T(8,128)(2,1)S(1)} %copy-done.29, bf16[64,4096]{1,0:T(8,128)(2,1)S(1)} %copy-done.20, bf16[64,4096]{1,0:T(8,128)(2,1)S(1)} %copy-done.17, ...), custom_call_target="tpu_custom_call" | custom-call | flops 1 | bytes 1 | tf_op jit(solution)/shard_map/line_scores/pallas_call | solution.py:257
  105.7 8.0 %all-to-all-done.2 = bf16[8,48,4096]{2,1,0:T(8,128)(2,1)S(1)} async-done(((bf16[8,48,4096]{2,1,0:T(8,128)(2,1)}), bf16[8,48,4096]{2,1,0:T(8,128)(2,1)S(1)}, u32[]{:S(2)}, u32[]{:S(2)}) %all-to-all-start.2) | async-done | bytes 3145760 | tf_op jit(solution)/shard_map/all_to_all | solution.py:59
  113.6 4.5 %all-to-all-start.4 = ((bf16[8,48,4096]{2,1,0:T(8,128)(2,1)}), bf16[8,48,4096]{2,1,0:T(8,128)(2,1)}, u32[]{:S(2)}, u32[]{:S(2)}) async-start(bf16[8,48,4096]{2,1,0:T(8,128)(2,1)} %bitcast.50), calls=%async_computation.5 | async-start | bytes 6291456 | tf_op jit(solution)/shard_map/all_to_all | solution.py:59
  122.8 3.7 %far_scores.1 = (f32[384,512]{1,0:T(8,128)S(1)}, f32[1,512]{1,0:T(1,128)S(1)}) custom-call(f32[640,512]{1,0:T(8,128)S(1)} %copy-done.11, bf16[512,512]{1,0:T(8,128)(2,1)S(1)} %copy-done.39, bf16[512,4096]{1,0:T(8,128)(2,1)S(1)} %copy-done.2, bf16[384,4096]{1,0:T(8,128)(2,1)S(1)} %bitcast.48), custom_call_target="tpu_custom_call" | custom-call | flops 99999997952 | bytes 100000000 | tf_op jit(solution)/shard_map/far_scores/pallas_call | solution.py:301
  126.5 2.8 %collective-permute-start.10 = (f32[8,128]{1,0:T(8,128)S(1)}, f32[8,128]{1,0:T(8,128)S(1)}, u32[]{:S(2)}, u32[]{:S(2)}) collective-permute-start(f32[8,128]{1,0:T(8,128)S(1)} %pad_maximum_fusion.1), channel_id=1, source_target_pairs={{0,3},{1,0},{2,1},{3,2},{4,7},{5,4},{6,5},{7,6},{8,11},{9,8},{10,9... | collective-permute-start | bytes 12296 | tf_op jit(solution)/shard_map/ppermute | solution.py:21
  131.0 3.4 %collective-permute-done.11 = f32[8,128]{1,0:T(8,128)S(1)} collective-permute-done((f32[8,128]{1,0:T(8,128)S(1)}, f32[8,128]{1,0:T(8,128)S(1)}, u32[]{:S(2)}, u32[]{:S(2)}) %collective-permute-start.11) | collective-permute-done | bytes 4128 | tf_op jit(solution)/shard_map/ppermute | solution.py:21
  135.2 8.1 %query_side.1 = (bf16[512,4096]{1,0:T(8,128)(2,1)S(1)}, f32[1,4096]{1,0:T(1,128)S(1)}, f32[8,512]{1,0:T(8,128)S(1)}, f32[1,512]{1,0:T(1,128)S(1)}, bf16[128,512]...) custom-call(f32[640,512]{1,0:T(8,128)S(1)} %copy-done.12, f32[384,512]{1,0:T(8,128)S(1)} %get-tuple-element.32.far_ref, ...), custom_call_target="tpu_custom_call" | custom-call | flops 1 | bytes 1 | tf_op jit(solution)/shard_map/query_side/pallas_call | solution.py:367
  160.2 6.3 %passage_side.3 = (bf16[64,4096]{1,0:T(8,128)(2,1)S(1)}, bf16[64,4096]{1,0:T(8,128)(2,1)}, bf16[64,4096]{1,0:T(8,128)(2,1)}, bf16[64,4096]{1,0:T(8,128)(2,1)S(1)...) custom-call(bf16[384,512]{1,0:T(8,128)(2,1)S(1)} %copy-done.48, bf16[512,4096]{1,0:T(8,128)(2,1)S(1)} %copy-done.4, ...), custom_call_target="tpu_custom_call" | custom-call | flops 99999997952 | bytes 100000000 | tf_op jit(solution)/shard_map/passage_side/pallas_call | solution.py:411
  168.6 12.0 %collective-permute-done.23 = bf16[64,4096]{1,0:T(8,128)(2,1)S(1)} collective-permute-done((bf16[64,4096]{1,0:T(8,128)(2,1)S(1)}, bf16[64,4096]{1,0:T(8,128)(2,1)S(1)}, u32[]{:S(2)}, u32[]{:S(2)}) %collective-permute-start.23) | collective-permute-done | bytes 524320 | tf_op jit(solution)/shard_map/ppermute | solution.py:21
  193.0 5.3 %all-to-all-start.3 = ((bf16[8,16,4096]{2,1,0:T(8,128)(2,1)}), bf16[8,16,4096]{2,1,0:T(8,128)(2,1)S(1)}, u32[]{:S(2)}, u32[]{:S(2)}) async-start(bf16[8,16,4096]{2,1,0:T(8,128)(2,1)} %bitcast.28), calls=%async_computation.3 | async-start | bytes 2097152 | tf_op jit(solution)/shard_map/all_to_all | solution.py:59
  200.3 3.0 %collective-permute-start.24 = (bf16[64,4096]{1,0:T(8,128)(2,1)}, bf16[64,4096]{1,0:T(8,128)(2,1)}, u32[]{:S(2)}, u32[]{:S(2)}) collective-permute-start(bf16[64,4096]{1,0:T(8,128)(2,1)} %add_convert_fusion), channel_id=1, source_target_pairs={{0,12},{4,0},{8,4},{12,8},{1,13},{5,1},{9,5},{13,9},{2,14},{6,2},{... | collective-permute-start | bytes 1572872 | tf_op jit(solution)/shard_map/ppermute | solution.py:21
  203.2 3.3 %collective-permute-start.29 = (f32[32,128]{1,0:T(8,128)S(1)}, f32[32,128]{1,0:T(8,128)S(1)}, u32[]{:S(2)}, u32[]{:S(2)}) collective-permute-start(f32[32,128]{1,0:T(8,128)S(1)} %add.385), channel_id=1, source_target_pairs={{0,96},{32,64},{64,32},{96,0},{1,97},{33,65},{65,33},{97,1},{2,98}... | collective-permute-start | bytes 49160 | tf_op jit(solution)/shard_map/ppermute | solution.py:53
  207.5 3.5 %collective-permute-done.29 = f32[32,128]{1,0:T(8,128)S(1)} collective-permute-done((f32[32,128]{1,0:T(8,128)S(1)}, f32[32,128]{1,0:T(8,128)S(1)}, u32[]{:S(2)}, u32[]{:S(2)}) %collective-permute-start.29) | collective-permute-done | bytes 16416 | tf_op jit(solution)/shard_map/ppermute | solution.py:53
  211.6 12.8 %collective-permute-done.30 = f32[32,128]{1,0:T(8,128)S(1)} collective-permute-done((f32[32,128]{1,0:T(8,128)S(1)}, f32[32,128]{1,0:T(8,128)S(1)}, u32[]{:S(2)}, u32[]{:S(2)}) %collective-permute-start.30) | collective-permute-done | bytes 16416 | tf_op jit(solution)/shard_map/ppermute | solution.py:52
  237.0 4.4 %finish.3 = bf16[128,4096]{1,0:T(8,128)(2,1)} custom-call(bf16[128,4096]{1,0:T(8,128)(2,1)S(1)} %copy-done.38, f32[1,4096]{1,0:T(1,128)S(1)} %bitcast.58, f32[128,4096]{1,0:T(8,128)S(1)} %passage_side.2.refs_0_, bf16[64,4096]{1,0:T(8,128)(2,1)} %collective-permute-done.20.refs_1_, bf16[64,4096]{1,0:T(8,128)(2,1)} %collective-permute-done.21.refs_2_, ...), custom_call_target="tpu_custom_call" | custom-call | flops 1 | bytes 1 | tf_op jit(solution)/shard_map/finish/pallas_call | solution.py:209
  (283 shorter events, 94.9 us)
Async XLA Ops:
  7.2 82.7 %all-gather.2.cloned.1.call-start = ((), (), s32[]{:S(2)}) async-start(), calls=%async_computation.6 | async-start | bytes 5242880 | tf_op jit(solution)/shard_map/all_gather | solution.py:475
  12.0 26.4 %collective-permute-start.6 = (bf16[64,4096]{1,0:T(8,128)(2,1)S(1)}, bf16[64,4096]{1,0:T(8,128)(2,1)S(1)}, u32[]{:S(2)}, u32[]{:S(2)}) collective-permute-start(bf16[64,4096]{1,0:T(8,128)(2,1)S(1)} %get-tuple-element.29.refs_1_), channel_id=1, source_target_pairs={{0,4},{4,8},{8,12},{12,0},{1,5},{5,9},{9,13},{13,1},{2,6},{6,10},{... | collective-permute-start | bytes 1572872 | tf_op jit(solution)/shard_map/ppermute | solution.py:21
  13.8 24.6 %collective-permute-start.4 = (bf16[64,4096]{1,0:T(8,128)(2,1)S(1)}, bf16[64,4096]{1,0:T(8,128)(2,1)S(1)}, u32[]{:S(2)}, u32[]{:S(2)}) collective-permute-start(bf16[64,4096]{1,0:T(8,128)(2,1)S(1)} %get-tuple-element.29.refs_1_), channel_id=1, source_target_pairs={{0,12},{4,0},{8,4},{12,8},{1,13},{5,1},{9,5},{13,9},{2,14},{6,2},{... | collective-permute-start | bytes 1572872 | tf_op jit(solution)/shard_map/ppermute | solution.py:21
  15.3 23.0 %collective-permute-start.3 = (bf16[64,4096]{1,0:T(8,128)(2,1)S(1)}, bf16[64,4096]{1,0:T(8,128)(2,1)S(1)}, u32[]{:S(2)}, u32[]{:S(2)}) collective-permute-start(bf16[64,4096]{1,0:T(8,128)(2,1)S(1)} %get-tuple-element.28.refs_0_), channel_id=1, source_target_pairs={{0,12},{4,0},{8,4},{12,8},{1,13},{5,1},{9,5},{13,9},{2,14},{6,2},{... | collective-permute-start | bytes 1572872 | tf_op jit(solution)/shard_map/ppermute | solution.py:21
  17.2 21.2 %collective-permute-start.5 = (bf16[64,4096]{1,0:T(8,128)(2,1)S(1)}, bf16[64,4096]{1,0:T(8,128)(2,1)S(1)}, u32[]{:S(2)}, u32[]{:S(2)}) collective-permute-start(bf16[64,4096]{1,0:T(8,128)(2,1)S(1)} %get-tuple-element.28.refs_0_), channel_id=1, source_target_pairs={{0,4},{4,8},{8,12},{12,0},{1,5},{5,9},{9,13},{13,1},{2,6},{6,10},{... | collective-permute-start | bytes 1572872 | tf_op jit(solution)/shard_map/ppermute | solution.py:21
  18.8 15.5 %all-to-all-start = ((s32[32,1,16]{2,1,0:T(1,128)}), s32[32,1,16]{2,1,0:T(1,128)S(1)}, u32[]{:S(2)}, u32[]{:S(2)}) async-start(s32[32,1,16]{2,1,0:T(1,128)} %bitcast.4), calls=%async_computation | async-start | bytes 32768 | tf_op jit(solution)/shard_map/all_to_all | solution.py:455
  40.8 28.8 %all-to-all-start.1 = ((bf16[8,16,4096]{2,1,0:T(8,128)(2,1)}), bf16[8,16,4096]{2,1,0:T(8,128)(2,1)S(1)}, u32[]{:S(2)}, u32[]{:S(2)}) async-start(bf16[8,16,4096]{2,1,0:T(8,128)(2,1)} %bitcast.54), calls=%async_computation.1 | async-start | bytes 2097152 | tf_op jit(solution)/shard_map/all_to_all | solution.py:59
  46.2 14.9 %collective-permute-start.7 = (bf16[64,4096]{1,0:T(8,128)(2,1)S(1)}, bf16[64,4096]{1,0:T(8,128)(2,1)}, u32[]{:S(2)}, u32[]{:S(2)}) collective-permute-start(bf16[64,4096]{1,0:T(8,128)(2,1)S(1)} %collective-permute-done.3.refs_2_.refs_0_), channel_id=1, source_target_pairs={{0,12},{4,0},{8,4},{12,8},{1,13},{5,1},{9,5},{13,9},{2,14},{6,2},{... | collective-permute-start | bytes 1572872 | tf_op jit(solution)/shard_map/ppermute | solution.py:21
  49.2 15.4 %collective-permute-start.8 = (bf16[64,4096]{1,0:T(8,128)(2,1)S(1)}, bf16[64,4096]{1,0:T(8,128)(2,1)}, u32[]{:S(2)}, u32[]{:S(2)}) collective-permute-start(bf16[64,4096]{1,0:T(8,128)(2,1)S(1)} %collective-permute-done.6.refs_5_.refs_3_), channel_id=1, source_target_pairs={{0,4},{4,8},{8,12},{12,0},{1,5},{5,9},{9,13},{13,1},{2,6},{6,10},{... | collective-permute-start | bytes 1572872 | tf_op jit(solution)/shard_map/ppermute | solution.py:21
  70.6 43.0 %all-to-all-start.2 = ((bf16[8,48,4096]{2,1,0:T(8,128)(2,1)}), bf16[8,48,4096]{2,1,0:T(8,128)(2,1)S(1)}, u32[]{:S(2)}, u32[]{:S(2)}) async-start(bf16[8,48,4096]{2,1,0:T(8,128)(2,1)} %bitcast.8), calls=%async_computation.2 | async-start | bytes 6291456 | tf_op jit(solution)/shard_map/all_to_all | solution.py:59
  75.5 8.9 %collective-permute-start = (s32[1,128]{1,0:T(1,128)S(1)}, s32[1,128]{1,0:T(1,128)S(1)}, u32[]{:S(2)}, u32[]{:S(2)}) collective-permute-start(s32[1,128]{1,0:T(1,128)S(1)} %broadcast_in_dim.366), channel_id=1, source_target_pairs={{0,1},{1,2},{2,3},{3,0},{4,5},{5,6},{6,7},{7,4},{8,9},{9,10},{10,1... | collective-permute-start | bytes 1544 | tf_op jit(solution)/shard_map/ppermute | solution.py:21
  77.1 8.7 %collective-permute-start.1 = (s32[1,128]{1,0:T(1,128)S(1)}, s32[1,128]{1,0:T(1,128)S(1)}, u32[]{:S(2)}, u32[]{:S(2)}) collective-permute-start(s32[1,128]{1,0:T(1,128)S(1)} %broadcast_in_dim.371), channel_id=1, source_target_pairs={{0,2},{1,3},{2,0},{3,1},{4,6},{5,7},{6,4},{7,5},{8,10},{9,11},{10,... | collective-permute-start | bytes 1544 | tf_op jit(solution)/shard_map/ppermute | solution.py:21
  113.6 44.4 %all-to-all-start.4 = ((bf16[8,48,4096]{2,1,0:T(8,128)(2,1)}), bf16[8,48,4096]{2,1,0:T(8,128)(2,1)}, u32[]{:S(2)}, u32[]{:S(2)}) async-start(bf16[8,48,4096]{2,1,0:T(8,128)(2,1)} %bitcast.50), calls=%async_computation.5 | async-start | bytes 6291456 | tf_op jit(solution)/shard_map/all_to_all | solution.py:59
  118.1 115.1 %reduce-scatter.2.cloned.1.call-start = ((), (), s32[]{:S(2)}) async-start(), calls=%async_computation.7 | async-start | bytes 5242880 | tf_op jit(solution)/shard_map/reduce_scatter | solution.py:512
  166.5 14.0 %collective-permute-start.23 = (bf16[64,4096]{1,0:T(8,128)(2,1)S(1)}, bf16[64,4096]{1,0:T(8,128)(2,1)S(1)}, u32[]{:S(2)}, u32[]{:S(2)}) collective-permute-start(bf16[64,4096]{1,0:T(8,128)(2,1)S(1)} %get-tuple-element.47), channel_id=1, source_target_pairs={{0,12},{4,0},{8,4},{12,8},{1,13},{5,1},{9,5},{13,9},{2,14},{6,2},{... | collective-permute-start | bytes 1572872 | tf_op jit(solution)/shard_map/ppermute | solution.py:21
  167.1 39.5 %collective-permute-start.19 = (bf16[64,4096]{1,0:T(8,128)(2,1)S(1)}, bf16[64,4096]{1,0:T(8,128)(2,1)S(1)}, u32[]{:S(2)}, u32[]{:S(2)}) collective-permute-start(bf16[64,4096]{1,0:T(8,128)(2,1)S(1)} %get-tuple-element.43), channel_id=1, source_target_pairs={{0,4},{4,8},{8,12},{12,0},{1,5},{5,9},{9,13},{13,1},{2,6},{6,10},{... | collective-permute-start | bytes 1572872 | tf_op jit(solution)/shard_map/ppermute | solution.py:21
  192.4 10.8 %collective-permute-start.28 = (f32[32,128]{1,0:T(8,128)S(1)}, f32[32,128]{1,0:T(8,128)S(1)}, u32[]{:S(2)}, u32[]{:S(2)}) collective-permute-start(f32[32,128]{1,0:T(8,128)S(1)} %add.384), channel_id=1, source_target_pairs={{0,32},{32,0},{64,96},{96,64},{1,33},{33,1},{65,97},{97,65},{2,34}... | collective-permute-start | bytes 49160 | tf_op jit(solution)/shard_map/ppermute | solution.py:52
  193.0 33.3 %all-to-all-start.3 = ((bf16[8,16,4096]{2,1,0:T(8,128)(2,1)}), bf16[8,16,4096]{2,1,0:T(8,128)(2,1)S(1)}, u32[]{:S(2)}, u32[]{:S(2)}) async-start(bf16[8,16,4096]{2,1,0:T(8,128)(2,1)} %bitcast.28), calls=%async_computation.3 | async-start | bytes 2097152 | tf_op jit(solution)/shard_map/all_to_all | solution.py:59
  198.2 38.7 %collective-permute-start.21 = (bf16[64,4096]{1,0:T(8,128)(2,1)}, bf16[64,4096]{1,0:T(8,128)(2,1)}, u32[]{:S(2)}, u32[]{:S(2)}) collective-permute-start(bf16[64,4096]{1,0:T(8,128)(2,1)} %get-tuple-element.44), channel_id=1, source_target_pairs={{0,12},{4,0},{8,4},{12,8},{1,13},{5,1},{9,5},{13,9},{2,14},{6,2},{... | collective-permute-start | bytes 1572872 | tf_op jit(solution)/shard_map/ppermute | solution.py:21
  200.0 37.0 %collective-permute-start.22 = (bf16[64,4096]{1,0:T(8,128)(2,1)}, bf16[64,4096]{1,0:T(8,128)(2,1)}, u32[]{:S(2)}, u32[]{:S(2)}) collective-permute-start(bf16[64,4096]{1,0:T(8,128)(2,1)} %get-tuple-element.45), channel_id=1, source_target_pairs={{0,4},{4,8},{8,12},{12,0},{1,5},{5,9},{9,13},{13,1},{2,6},{6,10},{... | collective-permute-start | bytes 1572872 | tf_op jit(solution)/shard_map/ppermute | solution.py:21
  200.3 36.7 %collective-permute-start.24 = (bf16[64,4096]{1,0:T(8,128)(2,1)}, bf16[64,4096]{1,0:T(8,128)(2,1)}, u32[]{:S(2)}, u32[]{:S(2)}) collective-permute-start(bf16[64,4096]{1,0:T(8,128)(2,1)} %add_convert_fusion), channel_id=1, source_target_pairs={{0,12},{4,0},{8,4},{12,8},{1,13},{5,1},{9,5},{13,9},{2,14},{6,2},{... | collective-permute-start | bytes 1572872 | tf_op jit(solution)/shard_map/ppermute | solution.py:21
  207.4 29.5 %collective-permute-start.20 = (bf16[64,4096]{1,0:T(8,128)(2,1)}, bf16[64,4096]{1,0:T(8,128)(2,1)}, u32[]{:S(2)}, u32[]{:S(2)}) collective-permute-start(bf16[64,4096]{1,0:T(8,128)(2,1)} %add_convert_fusion.1), channel_id=1, source_target_pairs={{0,4},{4,8},{8,12},{12,0},{1,5},{5,9},{9,13},{13,1},{2,6},{6,10},{... | collective-permute-start | bytes 1572872 | tf_op jit(solution)/shard_map/ppermute | solution.py:21
  211.0 13.4 %collective-permute-start.30 = (f32[32,128]{1,0:T(8,128)S(1)}, f32[32,128]{1,0:T(8,128)S(1)}, u32[]{:S(2)}, u32[]{:S(2)}) collective-permute-start(f32[32,128]{1,0:T(8,128)S(1)} %add.386), channel_id=1, source_target_pairs={{0,4},{4,0},{8,12},{12,8},{1,5},{5,1},{9,13},{13,9},{2,6},{6,2},{1... | collective-permute-start | bytes 49160 | tf_op jit(solution)/shard_map/ppermute | solution.py:52
  224.4 8.3 %collective-permute-start.31 = (f32[32,128]{1,0:T(8,128)S(1)}, f32[32,128]{1,0:T(8,128)S(1)}, u32[]{:S(2)}, u32[]{:S(2)}) collective-permute-start(f32[32,128]{1,0:T(8,128)S(1)} %add.387), channel_id=1, source_target_pairs={{0,12},{4,8},{8,4},{12,0},{1,13},{5,9},{9,5},{13,1},{2,14},{6,10},... | collective-permute-start | bytes 49160 | tf_op jit(solution)/shard_map/ppermute | solution.py:53
  (82 other events, 832.7 us)
Sparse Core Ops, SparseCore 0:
  11.3 50.8 all-gather.1
  156.5 43.8 reduce-scatter.1

commit v2 on v1

--- a/solution.py
+++ b/solution.py
@@ -21,36 +21,12 @@
     return lax.ppermute(value, axis, [(i, (i + step) % RING) for i in range(RING)])
 
 
-def ring_gather(low, high, axis):
-    up_low = shift(low, axis, -1)
-    down_high = shift(high, axis, 1)
-    up_high = shift(high, axis, -1)
-    down_low = shift(low, axis, 1)
-    far_low = shift(up_low, axis, -1)
-    far_high = shift(down_high, axis, 1)
-    return [up_low, up_high, down_low, down_high], [far_low, far_high]
-
-
-def ring_scatter(opposite, beside, axis):
-    low_2, high_2 = opposite
-    low_1, high_1, low_3, high_3 = beside
-    passing_low = shift(low_2, axis, 1)
-    passing_high = shift(high_2, axis, -1)
-    from_below_high = shift(high_1, axis, 1)
-    from_above_low = shift(low_3, axis, -1)
-    wide = jnp.float32
-    both_low = (low_1.astype(wide) + passing_low.astype(wide)).astype(jnp.bfloat16)
-    both_high = (high_3.astype(wide) + passing_high.astype(wide)).astype(jnp.bfloat16)
-    from_below_low = shift(both_low, axis, 1)
-    from_above_high = shift(both_high, axis, -1)
-    return [from_below_low, from_above_low], [from_below_high, from_above_high], both_high
-
-
-def all_sum(value, z_size):
-    value = value + lax.ppermute(value, "c", [(0, 1), (1, 0)])
-    for axis, size in (("x", RING), ("z", z_size), ("y", RING)):
+def axes_sum(value, axes):
+    for axis in axes:
+        size = lax.axis_size(axis)
         value = value + lax.ppermute(value, axis, [(i, i ^ 1) for i in range(size)])
-        value = value + lax.ppermute(value, axis, [(i, size - 1 - i) for i in range(size)])
+        if size > 2:
+            value = value + lax.ppermute(value, axis, [(i, size - 1 - i) for i in range(size)])
     return value
 
 
@@ -130,98 +106,56 @@
     return lax.rsqrt(jnp.mean(values * values, axis=-1, keepdims=True) + EPSILON)
 
 
-def embed(hidden, gain, pieces):
-    def body(hidden_ref, gain_ref, *out_refs):
+def embed(hidden, gain):
+    def body(hidden_ref, gain_ref, out_ref):
         values = hidden_ref[...].astype(jnp.float32)
         unit_rows = values * inverse_norm(values)
-        rounded_rows = (unit_rows * gain_ref[...]).astype(jnp.bfloat16)
-        for i, out_ref in enumerate(out_refs):
-
-            @pl.when(pl.program_id(0) // per_piece == i)
-            def _(out_ref=out_ref):
-                out_ref[...] = rounded_rows
+        out_ref[...] = (unit_rows * gain_ref[...]).astype(jnp.bfloat16)
 
     rows, width = hidden.shape
-    step = min(32, rows // pieces)
-    per_piece = rows // pieces // step
+    step = rows // 4
     block = pl.BlockSpec((step, width), lambda i: (i, 0))
-
-    def piece(at):
-        return pl.BlockSpec(
-            (step, width), lambda i: (jnp.clip(i - at * per_piece, 0, per_piece - 1), 0)
-        )
-
     return pl.pallas_call(
         body,
         grid=(rows // step,),
         in_specs=[block, whole((1, width))],
-        out_specs=[piece(at) for at in range(pieces)],
-        out_shape=[jax.ShapeDtypeStruct((rows // pieces, width), jnp.bfloat16)] * pieces,
+        out_specs=block,
+        out_shape=jax.ShapeDtypeStruct((rows, width), jnp.bfloat16),
         compiler_params=params(12),
         cost_estimate=SMALL,
         name="embed",
     )(hidden, gain)
 
 
-def finish(hidden, gain, terms, low_terms, high_terms):
+def finish(hidden, gain, terms):
     rows, width = hidden.shape
-    half = rows // 2
-    step = half // 2
-    count, low_count = len(terms), len(low_terms)
+    step = rows // 4
 
     def body(hidden_ref, gain_ref, *refs):
-        out_ref = refs[-1]
-        upstream = refs[0][...].astype(jnp.float32)
-        for ref in refs[1:count]:
-            upstream += ref[...].astype(jnp.float32)
-
-        def done(total):
-            values = hidden_ref[...].astype(jnp.float32)
-            inverse = inverse_norm(values)
-            unit_rows = values * inverse
-            scaled = total * gain_ref[...]
-            inner = jnp.mean(scaled * unit_rows, axis=-1, keepdims=True)
-            out_ref[...] = (inverse * (scaled - unit_rows * inner)).astype(jnp.bfloat16)
-
-        def add(total, extra):
-            for ref in extra:
-                total += ref[...].astype(jnp.float32)
-            return total
-
-        if low_count:
-            low_half = pl.program_id(0) < half // step
-
-            @pl.when(low_half)
-            def _():
-                done(add(upstream, refs[count : count + low_count]))
-
-            @pl.when(jnp.logical_not(low_half))
-            def _():
-                done(add(upstream, refs[count + low_count : -1]))
-
-        else:
-            done(upstream)
+        total = refs[0][...].astype(jnp.float32)
+        for ref in refs[1:-1]:
+            total += ref[...].astype(jnp.float32)
+        values = hidden_ref[...].astype(jnp.float32)
+        inverse = inverse_norm(values)
+        unit_rows = values * inverse
+        scaled = total * gain_ref[...]
+        inner = jnp.mean(scaled * unit_rows, axis=-1, keepdims=True)
+        refs[-1][...] = (inverse * (scaled - unit_rows * inner)).astype(jnp.bfloat16)
 
     block = pl.BlockSpec((step, width), lambda i: (i, 0))
-    per_half = half // step
-    low = pl.BlockSpec((step, width), lambda i: (jnp.minimum(i, per_half - 1), 0))
-    high = pl.BlockSpec((step, width), lambda i: (jnp.maximum(i - per_half, 0), 0))
     return pl.pallas_call(
         body,
         grid=(rows // step,),
-        in_specs=[block, whole((1, width))]
-        + [block] * count
-        + [low] * low_count
-        + [high] * len(high_terms),
+        in_specs=[block, whole((1, width))] + [block] * len(terms),
         out_specs=block,
         out_shape=jax.ShapeDtypeStruct((rows, width), jnp.bfloat16),
         compiler_params=params(16),
         cost_estimate=SMALL,
         name="finish",
-    )(hidden, gain, *terms, *low_terms, *high_terms)
-
-
-def pick_rows(matrix, sources):
+    )(hidden, gain, *terms)
+
+
+def pick_rows(matrix, sources, cost=SMALL):
     width = sources[0].shape[1]
 
     def body(matrix_ref, *refs):
@@ -234,9 +168,35 @@
         out_specs=columns(matrix.shape[0], width),
         out_shape=jax.ShapeDtypeStruct((matrix.shape[0], width), jnp.bfloat16),
         compiler_params=params(16),
-        cost_estimate=SMALL,
+        cost_estimate=cost,
         name="pick_rows",
     )(matrix, *sources)
+
+
+def pick_into(matrix, sources, shape, at, held=None):
+    width = sources[0].shape[1]
+    groups = shape[0]
+    size = matrix.shape[0] // groups
+
+    def body(matrix_ref, *refs):
+        picked = mxu(matrix_ref[...], joined(refs[: len(sources)])).astype(jnp.bfloat16)
+        refs[-1][...] = picked.reshape(groups, size, picked.shape[1])
+
+    place = pl.BlockSpec((groups, size, tile(width)), lambda i: (0, at // size, i))
+    more = () if held is None else (held,)
+    return pl.pallas_call(
+        body,
+        grid=(width // tile(width),),
+        in_specs=[whole(matrix.shape)]
+        + [columns(s.shape[0], width) for s in sources]
+        + [pl.BlockSpec(memory_space=pl.ANY)] * len(more),
+        out_specs=place,
+        out_shape=jax.ShapeDtypeStruct(shape, jnp.bfloat16),
+        input_output_aliases={1 + len(sources): 0} if more else {},
+        compiler_params=params(16),
+        cost_estimate=SMALL,
+        name="pick_into",
+    )(matrix, *sources, *more)
 
 
 def line_scores(sources, queries, scale):
@@ -435,8 +395,9 @@
     y_place, x_place = lax.axis_index("y"), lax.axis_index("x")
 
     gain = norm_gain.reshape(1, width)
-    p_own = embed(passage_hidden, gain, 2)
-    p_mid, p_opp = ring_gather(*p_own, "y")
+    p_own = embed(passage_hidden, gain)
+    p_mid = [shift(p_own, "y", -1), shift(p_own, "y", 1)]
+    p_opp = shift(p_own, "y", 2)
 
     flat_ids = hneg_ids.reshape(-1)
     id_count = rows * neg_count
@@ -457,21 +418,26 @@
     )
     asked = asked.reshape(group_count, RING, RING, CAP).transpose(0, 2, 1, 3)
     place = jnp.arange(line, dtype=jnp.int32)
-    asked, _ = lax.optimization_barrier((asked, p_mid))
+    asked, _ = lax.optimization_barrier((asked, p_mid[0]))
     asked_own = asked[:, 0].reshape(-1)
     above = jnp.where(asked[:, 3:] < 0, -1, asked[:, 3:] + rows)
+    asked_mid = jnp.concatenate([asked[:, 1:2], above], axis=1)
     opposite = jnp.where(asked[:, 2:3] < 0, -1, asked[:, 2:3] + 2 * rows)
-    asked_far = jnp.concatenate([asked[:, 1:2], above, opposite], axis=1).reshape(-1)
+    asked_far = jnp.concatenate([asked_mid, opposite], axis=1).reshape(-1)
 
     def one_hot(numbers, size):
         return (numbers[:, None] == place[None, :size]).astype(jnp.bfloat16)
 
-    chosen_own = pick_rows(one_hot(asked_own, rows), p_own)
-    hard_own = group_rows(chosen_own, group_count)
-    chosen_far = pick_rows(one_hot(asked_far, 3 * rows), [*p_mid, *p_opp])
-    hard_far = group_rows(chosen_far, group_count)
-
-    q_emb = embed(query_hidden, gain, 1)[0]
+    hard_own = group_rows(pick_rows(one_hot(asked_own, rows), [p_own]), group_count)
+    per_owner = RING * CAP
+    shape = (group_count, 3 * per_owner, width)
+    chosen = pick_into(one_hot(asked_mid.reshape(-1), 2 * rows), p_mid, shape, 0)
+    chosen = pick_into(
+        one_hot(asked[:, 2].reshape(-1), rows), [p_opp], shape, 2 * per_owner, chosen
+    )
+    hard_far = group_rows(chosen.reshape(-1, width), group_count)
+
+    q_emb = embed(query_hidden, gain)
     q_line = lax.all_gather(q_emb, "x", axis=0, tiled=True)
 
     by_x = slot_query.reshape(group_count, RING, RING * CAP).transpose(1, 0, 2)
@@ -489,7 +455,7 @@
     far_queries = group_rows(leave_far, group_count)
     own_queries = group_rows(leave_own, group_count)
 
-    near = line_scores([*p_own, *p_mid, *p_opp, hard_own], q_line, scale)
+    near = line_scores([p_own, *p_mid, p_opp, hard_own], q_line, scale)
     far, part_log = far_scores(near, [hard_far], q_line, asked_by, line, scale)
     part_log = part_log.reshape(RING, rows)
     own_place = jnp.arange(RING, dtype=jnp.int32)[:, None] == x_place
@@ -506,11 +472,11 @@
 
     part, gain_part, slot_coeff, positive, coeff_own, coeff_far = query_side(
         near, far, asked_by, log_total, weight, target, q_line,
-        [*p_own, *p_mid, *p_opp, hard_own, hard_far], line, scale,
+        [p_own, *p_mid, p_opp, hard_own, hard_far], line, scale,
     )
     loss_rows = lax.dynamic_slice(log_total - positive, (0, first_row), (1, rows)).reshape(-1)
     query_up = lax.psum_scatter(part, "x", scatter_dimension=0, tiled=True)
-    query_grad = finish(query_hidden, gain, [query_up], [], [])
+    query_grad = finish(query_hidden, gain, [query_up])
 
     own_end = group_count * RING * CAP
     pieces = (
@@ -527,15 +493,17 @@
 
     put_own = put_rows(asked_own, got_coeff[:, :first], rows)
     put_far = put_rows(asked_far, got_coeff[:, first:], 3 * rows)
-    far_part = passage_side(coeff_far, q_line, put_far, far_queries, scale, jnp.bfloat16, 6)
-    low_terms, high_terms, passed = ring_scatter(far_part[4:], far_part[:4], "y")
-    gain_part, _ = lax.optimization_barrier((gain_part, passed))
-    gain_grad = all_sum(gain_part.reshape(-1, 128), z_count).reshape(-1)
-    gain_grad = 2.0 * gain_grad / norm_gain
+    above, below, far = passage_side(
+        coeff_far, q_line, put_far, far_queries, scale, jnp.bfloat16, 3
+    )
+    arrived = [shift(above, "y", 1), shift(below, "y", -1), shift(far, "y", 2)]
+    gain_part, own_queries = lax.optimization_barrier((gain_part, own_queries))
+    gain_part = axes_sum(gain_part.reshape(-1, 128), ("c", "x", "z", "y"))
+    gain_grad = 2.0 * gain_part.reshape(-1) / norm_gain
 
     own_part = passage_side(coeff_own, q_line, put_own, own_queries, scale, jnp.float32, 1)[0]
     own_part, query_grad = lax.optimization_barrier((own_part, query_grad))
-    passage_grad = finish(passage_hidden, gain, [own_part], low_terms, high_terms)
+    passage_grad = finish(passage_hidden, gain, [own_part, *arrived])
     return (loss_rows, query_grad, passage_grad, gain_grad)
 
 

time: 250 us -> 275 us (1.10)
  waiting for transfers between devices: 74.1 us -> 94.7 us
  local copies, waits for them, and re-layouts: 28.9 us -> 44.1 us
  starting transfers between devices: 73.3 us -> 61.2 us
  Pallas kernels: 46.4 us -> 49.2 us
    unnamed x135 -> x117, local copies, waits for them, and re-layouts: 24.8 us -> 39.4 us
    ppermute x7, waiting for transfers between devices: 22.9 us -> 37.1 us  [the longest x4 29.1 us: axes_sum(): value = value + lax.ppermute(value, axis, [(i, i ^ 1) for i in range(size)])]
    ppermute x18 -> x12, starting transfers between devices: 25.6 us -> 19.2 us  [shift(): lax.ppermute(value, axis, [(i, (i + step) % RING) for i in range(RING)])]
    pallas_call x0 -> x2, Pallas kernels: none -> 6.39 us  [pick_into(): pl.pallas_call(body, grid=(width // tile(width),), in_specs=[whole(matrix...]
    pallas_call x4 -> x3, Pallas kernels: 11.5 us -> 6.42 us  [pick_rows(): pl.pallas_call(body, grid=(width // tile(width),), in_specs=[whole(matrix...]
    all_to_all x4, waiting for transfers between devices: 7.99 us -> 11.3 us  [group_rows(): return lax.all_to_all(blocks, GROUPS, 0, 0, tiled=True).reshape(rows.shape)]
    ppermute x18 -> x12, waiting for transfers between devices: 34.7 us -> 37.3 us  [shift(): lax.ppermute(value, axis, [(i, (i + step) % RING) for i in range(RING)])]
  transfers between devices with their start and end apart: 39 -> 33, of which waited for: 15 -> 18; matrix products, arithmetic and copies ran while one was open for 6% -> 5% of each run, Pallas kernels for 16% -> 16%
where the time goes in v2:
time: 275 us; the launch traced here: 273 us
  waiting for transfers between devices  94.7 us (34%)
  starting transfers between devices  61.2 us (22%)
  Pallas kernels  49.2 us (18%)
  local copies, waits for them, and re-layouts  44.1 us (16%)
  between operations  14.7 us (5%)
  other arithmetic  9.28 us (3%)
    unnamed x117, local copies, waits for them, and re-layouts  39.4 us
    ppermute x12, waiting for transfers between devices, shift(): lax.ppermute(value, axis, [(i, (i + step) % RING) for i in range(RING)])  37.3 us
    ppermute x4, waiting for transfers between devices, axes_sum(): value = value + lax.ppermute(value, axis, [(i, i ^ 1) for i in range(size)])  29.1 us
    ppermute x12, starting transfers between devices, shift(): lax.ppermute(value, axis, [(i, (i + step) % RING) for i in range(RING)])  19.2 us
    all_to_all x4, starting transfers between devices, group_rows(): return lax.all_to_all(blocks, GROUPS, 0, 0, tiled=True).reshape(rows.shape)  17.8 us
    all_to_all x4, waiting for transfers between devices, group_rows(): return lax.all_to_all(blocks, GROUPS, 0, 0, tiled=True).reshape(rows.shape)  11.3 us
    pallas_call x2, Pallas kernels, passage_side(): pl.pallas_call(body, grid=(width // tile(width),), in_specs=[whole(coeff....  8.45 us
    ppermute x7, starting transfers between devices, group_table(): lax.ppermute(row, GROUPS, [(z * 2 + c, (z + z_step) % z_count * 2 + (c ^...  8.36 us
  transfers between devices with their start and end apart: 33, of which 18 were waited for; matrix products, arithmetic and copies ran while one was open for 5% of the time, Pallas kernels for 16%

profile of v2, /device:TPU:0, one launch (start us, length us, event | category | flops | bytes accessed | tf_op | source)
XLA Modules:
  0.0 273.0 jit_solution(16258410750582278331)
XLA Ops:
  11.9 3.2 %collective-permute-start.3 = (bf16[128,4096]{1,0:T(8,128)(2,1)S(1)}, bf16[128,4096]{1,0:T(8,128)(2,1)S(1)}, u32[]{:S(2)}, u32[]{:S(2)}) collective-permute-start(bf16[128,4096]{1,0:T(8,128)(2,1)S(1)} %embed.3.refs_0_), channel_id=1, source_target_pairs={{0,12},{4,0},{8,4},{12,8},{1,13},{5,1},{9,5},{13,9},{2,14},{6,2},{... | collective-permute-start | bytes 3145736 | tf_op jit(solution)/shard_map/ppermute | solution.py:21
  16.5 8.2 %all-to-all-start = ((s32[32,1,16]{2,1,0:T(1,128)}), s32[32,1,16]{2,1,0:T(1,128)S(1)}, u32[]{:S(2)}, u32[]{:S(2)}) async-start(s32[32,1,16]{2,1,0:T(1,128)} %bitcast.4), calls=%async_computation | async-start | bytes 32768 | tf_op jit(solution)/shard_map/all_to_all | solution.py:416
  26.4 5.6 %all-to-all-done = s32[32,1,16]{2,1,0:T(1,128)S(1)} async-done(((s32[32,1,16]{2,1,0:T(1,128)}), s32[32,1,16]{2,1,0:T(1,128)S(1)}, u32[]{:S(2)}, u32[]{:S(2)}) %all-to-all-start) | async-done | bytes 2080 | tf_op jit(solution)/shard_map/all_to_all | solution.py:416
  32.1 27.9 %collective-permute-done.3.refs_1_.refs_0_ = bf16[128,4096]{1,0:T(8,128)(2,1)S(1)} collective-permute-done((bf16[128,4096]{1,0:T(8,128)(2,1)S(1)}, bf16[128,4096]{1,0:T(8,128)(2,1)S(1)}, u32[]{:S(2)}, u32[]{:S(2)}) %collective-permute-start.3) | collective-permute-done | bytes 1048608 | tf_op jit(solution)/shard_map/ppermute | solution.py:21
  63.3 5.3 %all-to-all-start.1 = ((bf16[8,16,4096]{2,1,0:T(8,128)(2,1)}), bf16[8,16,4096]{2,1,0:T(8,128)(2,1)S(1)}, u32[]{:S(2)}, u32[]{:S(2)}) async-start(bf16[8,16,4096]{2,1,0:T(8,128)(2,1)} %bitcast.53), calls=%async_computation.1 | async-start | bytes 2097152 | tf_op jit(solution)/shard_map/all_to_all | solution.py:35
  69.1 5.1 %collective-permute-done.4.refs_2_.refs_1_ = bf16[128,4096]{1,0:T(8,128)(2,1)} collective-permute-done((bf16[128,4096]{1,0:T(8,128)(2,1)S(1)}, bf16[128,4096]{1,0:T(8,128)(2,1)}, u32[]{:S(2)}, u32[]{:S(2)}) %collective-permute-start.4) | collective-permute-done | bytes 1048608 | tf_op jit(solution)/shard_map/ppermute | solution.py:21
  75.4 4.2 %pick_into.2.refs_1_ = bf16[8,48,4096]{2,1,0:T(8,128)(2,1)} custom-call(bf16[256,256]{1,0:T(8,128)(2,1)S(1)} %compare_convert_fusion.matrix_ref, bf16[128,4096]{1,0:T(8,128)(2,1)S(1)} %copy-done.8, bf16[128,4096]{1,0:T(8,128)(2,1)} %collective-permute-done.4.refs_2_.refs_1_), custom_call_target="tpu_custom_call" | custom-call | flops 1 | bytes 1 | tf_op jit(solution)/shard_map/pick_into/pallas_call | solution.py:187
  84.6 4.5 %all-to-all-start.2 = ((bf16[8,48,4096]{2,1,0:T(8,128)(2,1)}), bf16[8,48,4096]{2,1,0:T(8,128)(2,1)}, u32[]{:S(2)}, u32[]{:S(2)}) async-start(bf16[8,48,4096]{2,1,0:T(8,128)(2,1)} %pick_into.3), calls=%async_computation.2 | async-start | bytes 6291456 | tf_op jit(solution)/shard_map/all_to_all | solution.py:35
  113.5 5.0 %line_scores.1.near_ref = f32[640,512]{1,0:T(8,128)S(1)} custom-call(bf16[512,4096]{1,0:T(8,128)(2,1)S(1)} %copy-done.1, bf16[128,4096]{1,0:T(8,128)(2,1)S(1)} %embed.3.refs_0_, bf16[128,4096]{1,0:T(8,128)(2,1)S(1)} %copy-done.9, bf16[128,4096]{1,0:T(8,128)(2,1)} %collective-permute-done.4.refs_2_.refs_1_, ...), custom_call_target="tpu_custom_call" | custom-call | flops 1 | bytes 1 | tf_op jit(solution)/shard_map/line_scores/pallas_call | solution.py:217
  119.5 7.9 %all-to-all-done.2 = bf16[8,48,4096]{2,1,0:T(8,128)(2,1)} async-done(((bf16[8,48,4096]{2,1,0:T(8,128)(2,1)}), bf16[8,48,4096]{2,1,0:T(8,128)(2,1)}, u32[]{:S(2)}, u32[]{:S(2)}) %all-to-all-start.2) | async-done | bytes 3145760 | tf_op jit(solution)/shard_map/all_to_all | solution.py:35
  127.5 4.5 %all-to-all-start.4 = ((bf16[8,48,4096]{2,1,0:T(8,128)(2,1)}), bf16[8,48,4096]{2,1,0:T(8,128)(2,1)}, u32[]{:S(2)}, u32[]{:S(2)}) async-start(bf16[8,48,4096]{2,1,0:T(8,128)(2,1)} %bitcast.49), calls=%async_computation.5 | async-start | bytes 6291456 | tf_op jit(solution)/shard_map/all_to_all | solution.py:35
  136.5 5.1 %far_scores.1 = (f32[384,512]{1,0:T(8,128)S(1)}, f32[1,512]{1,0:T(1,128)S(1)}) custom-call(f32[640,512]{1,0:T(8,128)S(1)} %copy-done.12, bf16[512,512]{1,0:T(8,128)(2,1)S(1)} %copy-done.22, bf16[512,4096]{1,0:T(8,128)(2,1)S(1)} %copy-done.2, bf16[384,4096]{1,0:T(8,128)(2,1)} %bitcast.8.refs_0_.refs_5_), custom_call_target="tpu_custom_call" | custom-call | flops 99999997952 | bytes 100000000 | tf_op jit(solution)/shard_map/far_scores/pallas_call | solution.py:261
  142.6 3.0 %collective-permute-start.8 = (f32[8,128]{1,0:T(8,128)S(1)}, f32[8,128]{1,0:T(8,128)S(1)}, u32[]{:S(2)}, u32[]{:S(2)}) collective-permute-start(f32[8,128]{1,0:T(8,128)S(1)} %pad_maximum_fusion.1), channel_id=1, source_target_pairs={{0,2},{1,3},{2,0},{3,1},{4,6},{5,7},{6,4},{7,5},{8,10},{9,11},{10,... | collective-permute-start | bytes 12296 | tf_op jit(solution)/shard_map/ppermute | solution.py:21
  158.6 8.2 %query_side.1 = (bf16[512,4096]{1,0:T(8,128)(2,1)S(1)}, f32[1,4096]{1,0:T(1,128)S(1)}, f32[8,512]{1,0:T(8,128)S(1)}, f32[1,512]{1,0:T(1,128)S(1)}, bf16[128,512]...) custom-call(f32[640,512]{1,0:T(8,128)S(1)} %copy-done.13, f32[384,512]{1,0:T(8,128)S(1)} %copy-done.28, ...), custom_call_target="tpu_custom_call" | custom-call | flops 1 | bytes 1 | tf_op jit(solution)/shard_map/query_side/pallas_call | solution.py:327
  174.3 3.3 %collective-permute-start.12 = (f32[1,64]{1,0:T(1,128)S(1)}, f32[1,64]{1,0:T(1,128)S(1)}, u32[]{:S(2)}, u32[]{:S(2)}) collective-permute-start(f32[1,64]{1,0:T(1,128)S(1)} %bitcast.78), channel_id=1, source_target_pairs={{0,64},{16,80},{32,96},{48,112},{64,0},{80,16},{96,32},{112,48},{1... | collective-permute-start | bytes 776 | tf_op jit(solution)/shard_map/ppermute | solution.py:49
  182.8 3.6 %all-to-all-start.3 = ((bf16[8,16,4096]{2,1,0:T(8,128)(2,1)}), bf16[8,16,4096]{2,1,0:T(8,128)(2,1)S(1)}, u32[]{:S(2)}, u32[]{:S(2)}) async-start(bf16[8,16,4096]{2,1,0:T(8,128)(2,1)} %bitcast.27), calls=%async_computation.3 | async-start | bytes 2097152 | tf_op jit(solution)/shard_map/all_to_all | solution.py:35
  186.4 3.0 %copy-done.4 = bf16[512,4096]{1,0:T(8,128)(2,1)S(1)} copy-done((bf16[512,4096]{1,0:T(8,128)(2,1)S(1)}, bf16[512,4096]{1,0:T(8,128)(2,1)}, u32[]{:S(2)}) %copy-start.4) | copy-done | bytes 4194328
  190.3 6.5 %passage_side.3 = (bf16[128,4096]{1,0:T(8,128)(2,1)}, bf16[128,4096]{1,0:T(8,128)(2,1)}, bf16[128,4096]{1,0:T(8,128)(2,1)}) custom-call(bf16[384,512]{1,0:T(8,128)(2,1)S(1)} %copy-done.35, bf16[512,4096]{1,0:T(8,128)(2,1)S(1)} %copy-done.4, bf16[384,384]{1,0:T(8,128)(2,1)S(1)} %select_convert_fusion.put_ref, bf16[384,4096]{1,0:T(8,128)(2,1)} %bitcast.30.arrived_ref), custom_call_target="tpu_custom_call" | custom-call | flops 99999997952 | bytes 100000000 | tf_op jit(solution)/shard_map/passage_side/pallas_call | solution.py:371
  196.8 3.3 %collective-permute-start.17 = (bf16[128,4096]{1,0:T(8,128)(2,1)}, bf16[128,4096]{1,0:T(8,128)(2,1)}, u32[]{:S(2)}, u32[]{:S(2)}) collective-permute-start(bf16[128,4096]{1,0:T(8,128)(2,1)} %get-tuple-element.39), channel_id=1, source_target_pairs={{0,12},{4,0},{8,4},{12,8},{1,13},{5,1},{9,5},{13,9},{2,14},{6,2},{... | collective-permute-start | bytes 3145736 | tf_op jit(solution)/shard_map/ppermute | solution.py:21
  204.4 4.2 %collective-permute-done.20 = f32[32,128]{1,0:T(8,128)S(1)} collective-permute-done((f32[32,128]{1,0:T(8,128)S(1)}, f32[32,128]{1,0:T(8,128)S(1)}, u32[]{:S(2)}, u32[]{:S(2)}) %collective-permute-start.20) | collective-permute-done | bytes 16416 | tf_op jit(solution)/shard_map/ppermute | solution.py:27
  208.7 5.5 %collective-permute-done.21 = f32[32,128]{1,0:T(8,128)S(1)} collective-permute-done((f32[32,128]{1,0:T(8,128)S(1)}, f32[32,128]{1,0:T(8,128)S(1)}, u32[]{:S(2)}, u32[]{:S(2)}) %collective-permute-start.21) | collective-permute-done | bytes 16416 | tf_op jit(solution)/shard_map/ppermute | solution.py:29
  224.2 21.1 %collective-permute-done.24 = f32[32,128]{1,0:T(8,128)S(1)} collective-permute-done((f32[32,128]{1,0:T(8,128)S(1)}, f32[32,128]{1,0:T(8,128)S(1)}, u32[]{:S(2)}, u32[]{:S(2)}) %collective-permute-start.24) | collective-permute-done | bytes 16416 | tf_op jit(solution)/shard_map/ppermute | solution.py:27
  245.3 3.3 %collective-permute-start.25 = (f32[32,128]{1,0:T(8,128)S(1)}, f32[32,128]{1,0:T(8,128)S(1)}, u32[]{:S(2)}, u32[]{:S(2)}) collective-permute-start(f32[32,128]{1,0:T(8,128)S(1)} %add.379), channel_id=1, source_target_pairs={{0,12},{4,8},{8,4},{12,0},{1,13},{5,9},{9,5},{13,1},{2,14},{6,10},... | collective-permute-start | bytes 49160 | tf_op jit(solution)/shard_map/ppermute | solution.py:29
  261.8 4.4 %finish.3 = bf16[128,4096]{1,0:T(8,128)(2,1)} custom-call(bf16[128,4096]{1,0:T(8,128)(2,1)S(1)} %copy-done.17, f32[1,4096]{1,0:T(1,128)S(1)} %bitcast.57, f32[128,4096]{1,0:T(8,128)S(1)} %passage_side.2.refs_0_, bf16[128,4096]{1,0:T(8,128)(2,1)} %collective-permute-done.16.refs_1_, bf16[128,4096]{1,0:T(8,128)(2,1)} %collective-permute-done.17.refs_2_, ...), custom_call_target="tpu_custom_call" | custom-call | flops 1 | bytes 1 | tf_op jit(solution)/shard_map/finish/pallas_call | solution.py:146
  (259 shorter events, 102.8 us)
Async XLA Ops:
  7.2 96.1 %all-gather.2.cloned.1.call-start = ((), (), s32[]{:S(2)}) async-start(), calls=%async_computation.6 | async-start | bytes 5242880 | tf_op jit(solution)/shard_map/all_gather | solution.py:441
  11.9 48.1 %collective-permute-start.3 = (bf16[128,4096]{1,0:T(8,128)(2,1)S(1)}, bf16[128,4096]{1,0:T(8,128)(2,1)S(1)}, u32[]{:S(2)}, u32[]{:S(2)}) collective-permute-start(bf16[128,4096]{1,0:T(8,128)(2,1)S(1)} %embed.3.refs_0_), channel_id=1, source_target_pairs={{0,12},{4,0},{8,4},{12,8},{1,13},{5,1},{9,5},{13,9},{2,14},{6,2},{... | collective-permute-start | bytes 3145736 | tf_op jit(solution)/shard_map/ppermute | solution.py:21
  16.5 15.4 %all-to-all-start = ((s32[32,1,16]{2,1,0:T(1,128)}), s32[32,1,16]{2,1,0:T(1,128)S(1)}, u32[]{:S(2)}, u32[]{:S(2)}) async-start(s32[32,1,16]{2,1,0:T(1,128)} %bitcast.4), calls=%async_computation | async-start | bytes 32768 | tf_op jit(solution)/shard_map/all_to_all | solution.py:416
  24.7 54.9 %collective-permute-start.5 = (bf16[128,4096]{1,0:T(8,128)(2,1)S(1)}, bf16[128,4096]{1,0:T(8,128)(2,1)S(1)}, u32[]{:S(2)}, u32[]{:S(2)}) collective-permute-start(bf16[128,4096]{1,0:T(8,128)(2,1)S(1)} %embed.3.refs_0_), channel_id=1, source_target_pairs={{0,8},{4,12},{8,0},{12,4},{1,9},{5,13},{9,1},{13,5},{2,10},{6,14},... | collective-permute-start | bytes 3145736 | tf_op jit(solution)/shard_map/ppermute | solution.py:21
  25.4 48.8 %collective-permute-start.4 = (bf16[128,4096]{1,0:T(8,128)(2,1)S(1)}, bf16[128,4096]{1,0:T(8,128)(2,1)}, u32[]{:S(2)}, u32[]{:S(2)}) collective-permute-start(bf16[128,4096]{1,0:T(8,128)(2,1)S(1)} %embed.3.refs_0_), channel_id=1, source_target_pairs={{0,4},{4,8},{8,12},{12,0},{1,5},{5,9},{9,13},{13,1},{2,6},{6,10},{... | collective-permute-start | bytes 3145736 | tf_op jit(solution)/shard_map/ppermute | solution.py:21
  63.3 21.3 %all-to-all-start.1 = ((bf16[8,16,4096]{2,1,0:T(8,128)(2,1)}), bf16[8,16,4096]{2,1,0:T(8,128)(2,1)S(1)}, u32[]{:S(2)}, u32[]{:S(2)}) async-start(bf16[8,16,4096]{2,1,0:T(8,128)(2,1)} %bitcast.53), calls=%async_computation.1 | async-start | bytes 2097152 | tf_op jit(solution)/shard_map/all_to_all | solution.py:35
  84.6 42.9 %all-to-all-start.2 = ((bf16[8,48,4096]{2,1,0:T(8,128)(2,1)}), bf16[8,48,4096]{2,1,0:T(8,128)(2,1)}, u32[]{:S(2)}, u32[]{:S(2)}) async-start(bf16[8,48,4096]{2,1,0:T(8,128)(2,1)} %pick_into.3), calls=%async_computation.2 | async-start | bytes 6291456 | tf_op jit(solution)/shard_map/all_to_all | solution.py:35
  89.3 10.8 %collective-permute-start.2 = (s32[1,128]{1,0:T(1,128)S(1)}, s32[1,128]{1,0:T(1,128)S(1)}, u32[]{:S(2)}, u32[]{:S(2)}) collective-permute-start(s32[1,128]{1,0:T(1,128)S(1)} %broadcast_in_dim.377), channel_id=1, source_target_pairs={{0,3},{1,0},{2,1},{3,2},{4,7},{5,4},{6,5},{7,6},{8,11},{9,8},{10,9... | collective-permute-start | bytes 1544 | tf_op jit(solution)/shard_map/ppermute | solution.py:21
  92.2 7.0 %collective-permute-start.1 = (s32[1,128]{1,0:T(1,128)S(1)}, s32[1,128]{1,0:T(1,128)S(1)}, u32[]{:S(2)}, u32[]{:S(2)}) collective-permute-start(s32[1,128]{1,0:T(1,128)S(1)} %broadcast_in_dim.372), channel_id=1, source_target_pairs={{0,2},{1,3},{2,0},{3,1},{4,6},{5,7},{6,4},{7,5},{8,10},{9,11},{10,... | collective-permute-start | bytes 1544 | tf_op jit(solution)/shard_map/ppermute | solution.py:21
  127.5 55.3 %all-to-all-start.4 = ((bf16[8,48,4096]{2,1,0:T(8,128)(2,1)}), bf16[8,48,4096]{2,1,0:T(8,128)(2,1)}, u32[]{:S(2)}, u32[]{:S(2)}) async-start(bf16[8,48,4096]{2,1,0:T(8,128)(2,1)} %bitcast.49), calls=%async_computation.5 | async-start | bytes 6291456 | tf_op jit(solution)/shard_map/all_to_all | solution.py:35
  131.9 123.7 %reduce-scatter.2.cloned.1.call-start = ((), (), s32[]{:S(2)}) async-start(), calls=%async_computation.7 | async-start | bytes 5242880 | tf_op jit(solution)/shard_map/reduce_scatter | solution.py:478
  142.6 5.4 %collective-permute-start.8 = (f32[8,128]{1,0:T(8,128)S(1)}, f32[8,128]{1,0:T(8,128)S(1)}, u32[]{:S(2)}, u32[]{:S(2)}) collective-permute-start(f32[8,128]{1,0:T(8,128)S(1)} %pad_maximum_fusion.1), channel_id=1, source_target_pairs={{0,2},{1,3},{2,0},{3,1},{4,6},{5,7},{6,4},{7,5},{8,10},{9,11},{10,... | collective-permute-start | bytes 12296 | tf_op jit(solution)/shard_map/ppermute | solution.py:21
  170.6 7.0 %collective-permute-start.15 = (f32[1,64]{1,0:T(1,128)S(1)}, f32[1,64]{1,0:T(1,128)S(1)}, u32[]{:S(2)}, u32[]{:S(2)}) collective-permute-start(f32[1,64]{1,0:T(1,128)S(1)} %bitcast.83), channel_id=1, source_target_pairs={{0,112},{16,96},{32,16},{48,0},{64,48},{80,32},{96,80},{112,64},{1... | collective-permute-start | bytes 776 | tf_op jit(solution)/shard_map/ppermute | solution.py:49
  172.2 6.6 %collective-permute-start.14 = (f32[1,64]{1,0:T(1,128)S(1)}, f32[1,64]{1,0:T(1,128)S(1)}, u32[]{:S(2)}, u32[]{:S(2)}) collective-permute-start(f32[1,64]{1,0:T(1,128)S(1)} %bitcast.82), channel_id=1, source_target_pairs={{0,96},{16,112},{32,0},{48,16},{64,32},{80,48},{96,64},{112,80},{1... | collective-permute-start | bytes 776 | tf_op jit(solution)/shard_map/ppermute | solution.py:49
  173.9 5.2 %collective-permute-start.13 = (f32[1,64]{1,0:T(1,128)S(1)}, f32[1,64]{1,0:T(1,128)S(1)}, u32[]{:S(2)}, u32[]{:S(2)}) collective-permute-start(f32[1,64]{1,0:T(1,128)S(1)} %bitcast.79), channel_id=1, source_target_pairs={{0,80},{16,64},{32,112},{48,96},{64,16},{80,0},{96,48},{112,32},{1... | collective-permute-start | bytes 776 | tf_op jit(solution)/shard_map/ppermute | solution.py:49
  174.3 5.0 %collective-permute-start.12 = (f32[1,64]{1,0:T(1,128)S(1)}, f32[1,64]{1,0:T(1,128)S(1)}, u32[]{:S(2)}, u32[]{:S(2)}) collective-permute-start(f32[1,64]{1,0:T(1,128)S(1)} %bitcast.78), channel_id=1, source_target_pairs={{0,64},{16,80},{32,96},{48,112},{64,0},{80,16},{96,32},{112,48},{1... | collective-permute-start | bytes 776 | tf_op jit(solution)/shard_map/ppermute | solution.py:49
  182.8 19.5 %all-to-all-start.3 = ((bf16[8,16,4096]{2,1,0:T(8,128)(2,1)}), bf16[8,16,4096]{2,1,0:T(8,128)(2,1)S(1)}, u32[]{:S(2)}, u32[]{:S(2)}) async-start(bf16[8,16,4096]{2,1,0:T(8,128)(2,1)} %bitcast.27), calls=%async_computation.3 | async-start | bytes 2097152 | tf_op jit(solution)/shard_map/all_to_all | solution.py:35
  196.8 63.7 %collective-permute-start.16 = (bf16[128,4096]{1,0:T(8,128)(2,1)}, bf16[128,4096]{1,0:T(8,128)(2,1)}, u32[]{:S(2)}, u32[]{:S(2)}) collective-permute-start(bf16[128,4096]{1,0:T(8,128)(2,1)} %get-tuple-element.38), channel_id=1, source_target_pairs={{0,4},{4,8},{8,12},{12,0},{1,5},{5,9},{9,13},{13,1},{2,6},{6,10},{... | collective-permute-start | bytes 3145736 | tf_op jit(solution)/shard_map/ppermute | solution.py:21
  196.8 63.7 %collective-permute-start.17 = (bf16[128,4096]{1,0:T(8,128)(2,1)}, bf16[128,4096]{1,0:T(8,128)(2,1)}, u32[]{:S(2)}, u32[]{:S(2)}) collective-permute-start(bf16[128,4096]{1,0:T(8,128)(2,1)} %get-tuple-element.39), channel_id=1, source_target_pairs={{0,12},{4,0},{8,4},{12,8},{1,13},{5,1},{9,5},{13,9},{2,14},{6,2},{... | collective-permute-start | bytes 3145736 | tf_op jit(solution)/shard_map/ppermute | solution.py:21
  200.2 60.4 %collective-permute-start.18 = (bf16[128,4096]{1,0:T(8,128)(2,1)}, bf16[128,4096]{1,0:T(8,128)(2,1)}, u32[]{:S(2)}, u32[]{:S(2)}) collective-permute-start(bf16[128,4096]{1,0:T(8,128)(2,1)} %get-tuple-element.40), channel_id=1, source_target_pairs={{0,8},{4,12},{8,0},{12,4},{1,9},{5,13},{9,1},{13,5},{2,10},{6,14},... | collective-permute-start | bytes 3145736 | tf_op jit(solution)/shard_map/ppermute | solution.py:21
  208.7 5.5 %collective-permute-start.21 = (f32[32,128]{1,0:T(8,128)S(1)}, f32[32,128]{1,0:T(8,128)S(1)}, u32[]{:S(2)}, u32[]{:S(2)}) collective-permute-start(f32[32,128]{1,0:T(8,128)S(1)} %add.375), channel_id=1, source_target_pairs={{0,3},{1,2},{2,1},{3,0},{4,7},{5,6},{6,5},{7,4},{8,11},{9,10},{10,... | collective-permute-start | bytes 49160 | tf_op jit(solution)/shard_map/ppermute | solution.py:29
  217.9 4.9 %collective-permute-start.23 = (f32[32,128]{1,0:T(8,128)S(1)}, f32[32,128]{1,0:T(8,128)S(1)}, u32[]{:S(2)}, u32[]{:S(2)}) collective-permute-start(f32[32,128]{1,0:T(8,128)S(1)} %add.377), channel_id=1, source_target_pairs={{0,96},{32,64},{64,32},{96,0},{1,97},{33,65},{65,33},{97,1},{2,98}... | collective-permute-start | bytes 49160 | tf_op jit(solution)/shard_map/ppermute | solution.py:29
  222.8 22.4 %collective-permute-start.24 = (f32[32,128]{1,0:T(8,128)S(1)}, f32[32,128]{1,0:T(8,128)S(1)}, u32[]{:S(2)}, u32[]{:S(2)}) collective-permute-start(f32[32,128]{1,0:T(8,128)S(1)} %add.378), channel_id=1, source_target_pairs={{0,4},{4,0},{8,12},{12,8},{1,5},{5,1},{9,13},{13,9},{2,6},{6,2},{1... | collective-permute-start | bytes 49160 | tf_op jit(solution)/shard_map/ppermute | solution.py:27
  245.3 9.7 %collective-permute-start.25 = (f32[32,128]{1,0:T(8,128)S(1)}, f32[32,128]{1,0:T(8,128)S(1)}, u32[]{:S(2)}, u32[]{:S(2)}) collective-permute-start(f32[32,128]{1,0:T(8,128)S(1)} %add.379), channel_id=1, source_target_pairs={{0,12},{4,8},{8,4},{12,0},{1,13},{5,9},{9,5},{13,1},{2,14},{6,10},... | collective-permute-start | bytes 49160 | tf_op jit(solution)/shard_map/ppermute | solution.py:29
  (67 other events, 487.5 us)
Sparse Core Ops, SparseCore 0:
  11.2 50.8 all-gather.1
  179.1 46.6 reduce-scatter.1

commit v3 on v1

--- a/solution.py
+++ b/solution.py
@@ -21,19 +21,20 @@
     return lax.ppermute(value, axis, [(i, (i + step) % RING) for i in range(RING)])
 
 
-def ring_gather(low, high, axis):
+def ring_pieces(block, axis):
+    half = block.shape[0] // 2
+    low, high = block[:half], block[half:]
     up_low = shift(low, axis, -1)
     down_high = shift(high, axis, 1)
     up_high = shift(high, axis, -1)
     down_low = shift(low, axis, 1)
     far_low = shift(up_low, axis, -1)
     far_high = shift(down_high, axis, 1)
-    return [up_low, up_high, down_low, down_high], [far_low, far_high]
-
-
-def ring_scatter(opposite, beside, axis):
-    low_2, high_2 = opposite
-    low_1, high_1, low_3, high_3 = beside
+    return [low, high, up_low, up_high, down_low, down_high, far_low, far_high]
+
+
+def ring_scatter(blocks, axis):
+    low_1, high_1, low_3, high_3, low_2, high_2 = blocks
     passing_low = shift(low_2, axis, 1)
     passing_high = shift(high_2, axis, -1)
     from_below_high = shift(high_1, axis, 1)
@@ -46,11 +47,12 @@
     return [from_below_low, from_above_low], [from_below_high, from_above_high], both_high
 
 
-def all_sum(value, z_size):
-    value = value + lax.ppermute(value, "c", [(0, 1), (1, 0)])
-    for axis, size in (("x", RING), ("z", z_size), ("y", RING)):
+def axes_sum(value, axes):
+    for axis in axes:
+        size = lax.axis_size(axis)
         value = value + lax.ppermute(value, axis, [(i, i ^ 1) for i in range(size)])
-        value = value + lax.ppermute(value, axis, [(i, size - 1 - i) for i in range(size)])
+        if size > 2:
+            value = value + lax.ppermute(value, axis, [(i, size - 1 - i) for i in range(size)])
     return value
 
 
@@ -130,33 +132,21 @@
     return lax.rsqrt(jnp.mean(values * values, axis=-1, keepdims=True) + EPSILON)
 
 
-def embed(hidden, gain, pieces):
-    def body(hidden_ref, gain_ref, *out_refs):
+def embed(hidden, gain):
+    def body(hidden_ref, gain_ref, out_ref):
         values = hidden_ref[...].astype(jnp.float32)
         unit_rows = values * inverse_norm(values)
-        rounded_rows = (unit_rows * gain_ref[...]).astype(jnp.bfloat16)
-        for i, out_ref in enumerate(out_refs):
-
-            @pl.when(pl.program_id(0) // per_piece == i)
-            def _(out_ref=out_ref):
-                out_ref[...] = rounded_rows
+        out_ref[...] = (unit_rows * gain_ref[...]).astype(jnp.bfloat16)
 
     rows, width = hidden.shape
-    step = min(32, rows // pieces)
-    per_piece = rows // pieces // step
+    step = rows // 4
     block = pl.BlockSpec((step, width), lambda i: (i, 0))
-
-    def piece(at):
-        return pl.BlockSpec(
-            (step, width), lambda i: (jnp.clip(i - at * per_piece, 0, per_piece - 1), 0)
-        )
-
     return pl.pallas_call(
         body,
         grid=(rows // step,),
         in_specs=[block, whole((1, width))],
-        out_specs=[piece(at) for at in range(pieces)],
-        out_shape=[jax.ShapeDtypeStruct((rows // pieces, width), jnp.bfloat16)] * pieces,
+        out_specs=block,
+        out_shape=jax.ShapeDtypeStruct((rows, width), jnp.bfloat16),
         compiler_params=params(12),
         cost_estimate=SMALL,
         name="embed",
@@ -221,7 +211,7 @@
     )(hidden, gain, *terms, *low_terms, *high_terms)
 
 
-def pick_rows(matrix, sources):
+def pick_rows(matrix, sources, cost=SMALL):
     width = sources[0].shape[1]
 
     def body(matrix_ref, *refs):
@@ -234,9 +224,34 @@
         out_specs=columns(matrix.shape[0], width),
         out_shape=jax.ShapeDtypeStruct((matrix.shape[0], width), jnp.bfloat16),
         compiler_params=params(16),
-        cost_estimate=SMALL,
+        cost_estimate=cost,
         name="pick_rows",
     )(matrix, *sources)
+
+
+def in_order(pieces, x_place):
+    half, width = pieces[0].shape
+
+    def body(place_ref, *refs):
+        out_ref = refs[-1]
+        for i, ref in enumerate(refs[:-1]):
+            step = (0, 1, RING - 1, 2)[i // 2]
+            block = lax.rem(place_ref[0] + step, RING)
+            first = pl.multiple_of((2 * block + i % 2) * half, half)
+            out_ref[pl.ds(first, half), :] = ref[...]
+
+    rows = half * len(pieces)
+    return pl.pallas_call(
+        body,
+        grid=(width // tile(width),),
+        in_specs=[pl.BlockSpec(memory_space=pltpu.SMEM)]
+        + [columns(half, width) for _ in pieces],
+        out_specs=columns(rows, width),
+        out_shape=jax.ShapeDtypeStruct((rows, width), jnp.bfloat16),
+        compiler_params=params(12),
+        cost_estimate=SMALL,
+        name="in_order",
+    )(x_place.reshape(1), *pieces)
 
 
 def line_scores(sources, queries, scale):
@@ -318,19 +333,19 @@
     )(near, asked_by, queries, *sources)
 
 
-def query_side(near, far, asked_by, log_total, weight, target, queries, sources, line, scale):
+def query_side(near, far, asked_by, log_total, weight, target, y_place, queries, sources, line, scale):
     width = queries.shape[1]
     query_count = queries.shape[0]
     near_slots = near.shape[0] - line
     slot_count = asked_by.shape[0]
     count = len(sources)
     rows = line // RING
-    cuts = (rows, 3 * rows)
-
-    def body(near_ref, far_ref, mask_ref, log_ref, weight_ref, target_ref, query_ref, *refs):
+    cuts = ((0,), (1, 3, 2))
+
+    def body(near_ref, far_ref, mask_ref, log_ref, weight_ref, target_ref, place_ref, query_ref, *refs):
         source_refs = refs[:count]
         part_ref, gain_ref, slot_ref, positive_ref = refs[count : count + 4]
-        coeff_refs, turned_ref = refs[count + 4 : -1], refs[-1]
+        coeff_refs, (turned_ref, kept_ref) = refs[count + 4 : -2], refs[-2:]
 
         @pl.when(pl.program_id(0) == 0)
         def _():
@@ -340,10 +355,12 @@
             hit = row_place == target_ref[...]
             positive_ref[...] = jnp.sum(jnp.where(hit, inner, 0.0), axis=0, keepdims=True)
             inner_coeff = weight_row * (jnp.exp(inner - log_row) - jnp.where(hit, 1.0, 0.0))
-            at = 0
-            for coeff_ref, size in zip(coeff_refs, cuts):
-                coeff_ref[...] = inner_coeff[at : at + size].astype(jnp.bfloat16)
-                at += size
+            kept_ref[...] = inner_coeff.astype(jnp.bfloat16)
+            for coeff_ref, cut in zip(coeff_refs, cuts):
+                for i, step in enumerate(cut):
+                    block = lax.rem(place_ref[0] + step, RING)
+                    first = pl.multiple_of(block * rows, rows)
+                    coeff_ref[i * rows : (i + 1) * rows] = kept_ref[pl.ds(first, rows), :]
             own = jnp.where(mask_ref[:near_slots, :] > 0, near_ref[line:, :], LOW)
             slots = jnp.where(mask_ref[near_slots:, :] > 0, far_ref[...], LOW)
             own_coeff = (weight_row * jnp.exp(own - log_row)).astype(jnp.bfloat16)
@@ -374,6 +391,7 @@
             row,
             row,
             row,
+            pl.BlockSpec(memory_space=pltpu.SMEM),
             columns(query_count, width),
         ]
         + [columns(s.shape[0], width) for s in sources],
@@ -383,19 +401,22 @@
             whole((8, slot_count)),
             row,
         ]
-        + [whole((size, query_count)) for size in cuts],
+        + [whole((rows * len(cut), query_count)) for cut in cuts],
         out_shape=[
             jax.ShapeDtypeStruct((query_count, width), jnp.bfloat16),
             jax.ShapeDtypeStruct((1, width), jnp.float32),
             jax.ShapeDtypeStruct((8, slot_count), jnp.float32),
             jax.ShapeDtypeStruct((1, query_count), jnp.float32),
         ]
-        + [jax.ShapeDtypeStruct((size, query_count), jnp.bfloat16) for size in cuts],
-        scratch_shapes=[pltpu.VMEM((query_count, line + slot_count), jnp.bfloat16)],
+        + [jax.ShapeDtypeStruct((rows * len(cut), query_count), jnp.bfloat16) for cut in cuts],
+        scratch_shapes=[
+            pltpu.VMEM((query_count, line + slot_count), jnp.bfloat16),
+            pltpu.VMEM((line, query_count), jnp.bfloat16),
+        ],
         compiler_params=params(32),
         cost_estimate=SMALL,
         name="query_side",
-    )(near, far, asked_by, log_total, weight, target, queries, *sources)
+    )(near, far, asked_by, log_total, weight, target, y_place, queries, *sources)
 
 
 def passage_side(coeff, queries, put, arrived, scale, out_type, pieces):
@@ -435,8 +456,9 @@
     y_place, x_place = lax.axis_index("y"), lax.axis_index("x")
 
     gain = norm_gain.reshape(1, width)
-    p_own = embed(passage_hidden, gain, 2)
-    p_mid, p_opp = ring_gather(*p_own, "y")
+    p_own = embed(passage_hidden, gain)
+    p_line = lax.all_gather(p_own, "y", axis=0, tiled=True)
+    q_pieces = ring_pieces(embed(query_hidden, gain), "x")
 
     flat_ids = hneg_ids.reshape(-1)
     id_count = rows * neg_count
@@ -452,27 +474,31 @@
     hit = slot[None, :] == jnp.arange(slot_count, dtype=jnp.int32)[:, None]
     slot_row = jnp.sum(jnp.where(hit, local_row[None, :] + 1, 0), axis=1) - 1
     slot_query = jnp.sum(jnp.where(hit, number[None, :] // neg_count + 1, 0), axis=1)
+    slot_row, p_own = lax.optimization_barrier((slot_row, p_own))
     asked = lax.all_to_all(
         slot_row.reshape(group_count * RING, RING * CAP), ("z", "c", "x"), 0, 0, tiled=True
     )
     asked = asked.reshape(group_count, RING, RING, CAP).transpose(0, 2, 1, 3)
+    asked, _ = lax.optimization_barrier((asked, q_pieces[2:6]))
     place = jnp.arange(line, dtype=jnp.int32)
-    asked, _ = lax.optimization_barrier((asked, p_mid))
     asked_own = asked[:, 0].reshape(-1)
-    above = jnp.where(asked[:, 3:] < 0, -1, asked[:, 3:] + rows)
-    opposite = jnp.where(asked[:, 2:3] < 0, -1, asked[:, 2:3] + 2 * rows)
-    asked_far = jnp.concatenate([asked[:, 1:2], above, opposite], axis=1).reshape(-1)
+    far_steps = [1, RING - 1, 2]
+    asked_far = jnp.stack([asked[:, step] for step in far_steps], axis=1)
+
+    def numbered(blocks):
+        blocks = jnp.stack(blocks).astype(jnp.int32)[None, :, None, None]
+        return jnp.where(asked_far < 0, -1, asked_far + rows * blocks).reshape(-1)
+
+    asked_line = numbered([(y_place + step) % RING for step in far_steps])
+    asked_far = numbered([jnp.int32(i) for i in range(RING - 1)])
 
     def one_hot(numbers, size):
         return (numbers[:, None] == place[None, :size]).astype(jnp.bfloat16)
 
-    chosen_own = pick_rows(one_hot(asked_own, rows), p_own)
-    hard_own = group_rows(chosen_own, group_count)
-    chosen_far = pick_rows(one_hot(asked_far, 3 * rows), [*p_mid, *p_opp])
-    hard_far = group_rows(chosen_far, group_count)
-
-    q_emb = embed(query_hidden, gain, 1)[0]
-    q_line = lax.all_gather(q_emb, "x", axis=0, tiled=True)
+    hard_own = group_rows(pick_rows(one_hot(asked_own, rows), [p_own]), group_count)
+    hard_far = group_rows(pick_rows(one_hot(asked_line, line), [p_line]), group_count)
+
+    q_line = in_order(q_pieces, x_place)
 
     by_x = slot_query.reshape(group_count, RING, RING * CAP).transpose(1, 0, 2)
     asker = line_table(by_x.reshape(RING, -1)).reshape(RING, group_count, RING, CAP)
@@ -489,7 +515,7 @@
     far_queries = group_rows(leave_far, group_count)
     own_queries = group_rows(leave_own, group_count)
 
-    near = line_scores([*p_own, *p_mid, *p_opp, hard_own], q_line, scale)
+    near = line_scores([p_line, hard_own], q_line, scale)
     far, part_log = far_scores(near, [hard_far], q_line, asked_by, line, scale)
     part_log = part_log.reshape(RING, rows)
     own_place = jnp.arange(RING, dtype=jnp.int32)[:, None] == x_place
@@ -502,11 +528,11 @@
     log_total = (top + jnp.log(sum(jnp.exp(part - top) for part in logs))).reshape(1, line)
     first_row = x_place * rows
     target = place[None, :] - first_row
-    target = jnp.where((target >= 0) & (target < rows), target, -1)
+    target = jnp.where((target >= 0) & (target < rows), target + y_place * rows, -1)
 
     part, gain_part, slot_coeff, positive, coeff_own, coeff_far = query_side(
-        near, far, asked_by, log_total, weight, target, q_line,
-        [*p_own, *p_mid, *p_opp, hard_own, hard_far], line, scale,
+        near, far, asked_by, log_total, weight, target, y_place.reshape(1), q_line,
+        [p_line, hard_own, hard_far], line, scale,
     )
     loss_rows = lax.dynamic_slice(log_total - positive, (0, first_row), (1, rows)).reshape(-1)
     query_up = lax.psum_scatter(part, "x", scatter_dimension=0, tiled=True)
@@ -528,10 +554,11 @@
     put_own = put_rows(asked_own, got_coeff[:, :first], rows)
     put_far = put_rows(asked_far, got_coeff[:, first:], 3 * rows)
     far_part = passage_side(coeff_far, q_line, put_far, far_queries, scale, jnp.bfloat16, 6)
-    low_terms, high_terms, passed = ring_scatter(far_part[4:], far_part[:4], "y")
-    gain_part, _ = lax.optimization_barrier((gain_part, passed))
-    gain_grad = all_sum(gain_part.reshape(-1, 128), z_count).reshape(-1)
-    gain_grad = 2.0 * gain_grad / norm_gain
+    low_terms, high_terms, sent = ring_scatter(far_part, "y")
+    gain_part, own_queries = lax.optimization_barrier((gain_part, own_queries))
+    gain_part = axes_sum(gain_part.reshape(-1, 128), ("c", "x", "z"))
+    gain_part, _ = lax.optimization_barrier((gain_part, sent))
+    gain_grad = 2.0 * axes_sum(gain_part, ("y",)).reshape(-1) / norm_gain
 
     own_part = passage_side(coeff_own, q_line, put_own, own_queries, scale, jnp.float32, 1)[0]
     own_part, query_grad = lax.optimization_barrier((own_part, query_grad))

time: 250 us -> 269 us (1.076)
  waiting for transfers between devices: 74.1 us -> 92.1 us
  starting transfers between devices: 73.3 us -> 58.4 us
  local copies, waits for them, and re-layouts: 28.9 us -> 42.8 us
  Pallas kernels: 46.4 us -> 50.5 us
    unnamed x135 -> x99, local copies, waits for them, and re-layouts: 24.8 us -> 38.3 us
    all_gather x1, waiting for transfers between devices: 0.01 us -> 10.4 us  [on_device(): p_line = lax.all_gather(p_own, 'y', axis=0, tiled=True)]
    all_to_all x1, waiting for transfers between devices: 7.24 us -> 16.9 us  [on_device(): lax.all_to_all(slot_row.reshape(group_count * RING, RING * CAP), ('z', 'c...]
    ppermute x7, starting transfers between devices: 9.89 us -> 1.99 us  [the longest x3 1.4 us: axes_sum(): lax.ppermute(value, axis, [(i, size - 1 - i) for i in range(size)])]
    all_to_all x4, starting transfers between devices: 19.6 us -> 16.2 us  [group_rows(): return lax.all_to_all(blocks, GROUPS, 0, 0, tiled=True).reshape(rows.shape)]
    all_to_all x4, waiting for transfers between devices: 7.99 us -> 4.75 us  [group_rows(): return lax.all_to_all(blocks, GROUPS, 0, 0, tiled=True).reshape(rows.shape)]
    pallas_call x4, Pallas kernels: 11.5 us -> 14.5 us  [pick_rows(): pl.pallas_call(body, grid=(width // tile(width),), in_specs=[whole(matrix...]
  transfers between devices with their start and end apart: 39 -> 39, of which waited for: 15 -> 17; matrix products, arithmetic and copies ran while one was open for 6% -> 5% of each run, Pallas kernels for 16% -> 17%
where the time goes in v3:
time: 269 us; the launch traced here: 267 us
  waiting for transfers between devices  92.1 us (34%)
  starting transfers between devices  58.4 us (22%)
  Pallas kernels  50.5 us (19%)
  local copies, waits for them, and re-layouts  42.8 us (16%)
  between operations  14.7 us (5%)
  other arithmetic  8.84 us (3%)
    unnamed x99, local copies, waits for them, and re-layouts  38.3 us
    ppermute x18, waiting for transfers between devices, shift(): lax.ppermute(value, axis, [(i, (i + step) % RING) for i in range(RING)])  34.4 us
    ppermute x18, starting transfers between devices, shift(): lax.ppermute(value, axis, [(i, (i + step) % RING) for i in range(RING)])  26 us
    all_to_all x1, waiting for transfers between devices, on_device(): lax.all_to_all(slot_row.reshape(group_count * RING, RING * CAP), ('z', 'c...  16.9 us
    ppermute x4, waiting for transfers between devices, axes_sum(): value = value + lax.ppermute(value, axis, [(i, i ^ 1) for i in range(size)])  16.9 us
    all_to_all x4, starting transfers between devices, group_rows(): return lax.all_to_all(blocks, GROUPS, 0, 0, tiled=True).reshape(rows.shape)  16.2 us
    pallas_call x4, Pallas kernels, pick_rows(): pl.pallas_call(body, grid=(width // tile(width),), in_specs=[whole(matrix...  14.5 us
    all_gather x1, waiting for transfers between devices, on_device(): p_line = lax.all_gather(p_own, 'y', axis=0, tiled=True)  10.4 us
  transfers between devices with their start and end apart: 39, of which 17 were waited for; matrix products, arithmetic and copies ran while one was open for 5% of the time, Pallas kernels for 17%

profile of v3, /device:TPU:0, one launch (start us, length us, event | category | flops | bytes accessed | tf_op | source)
XLA Modules:
  0.0 267.4 jit_solution(18149215830151098193)
XLA Ops:
  20.1 5.8 %all-to-all-start = ((s32[32,1,16]{2,1,0:T(1,128)}), s32[32,1,16]{2,1,0:T(1,128)S(1)}, u32[]{:S(2)}, u32[]{:S(2)}) async-start(s32[32,1,16]{2,1,0:T(1,128)} %bitcast.5), calls=%async_computation | async-start | bytes 32768 | tf_op jit(solution)/shard_map/all_to_all | solution.py:478
  25.9 16.9 %all-to-all-done = s32[32,1,16]{2,1,0:T(1,128)S(1)} async-done(((s32[32,1,16]{2,1,0:T(1,128)}), s32[32,1,16]{2,1,0:T(1,128)S(1)}, u32[]{:S(2)}, u32[]{:S(2)}) %all-to-all-start) | async-done | bytes 2080 | tf_op jit(solution)/shard_map/all_to_all | solution.py:478
  43.5 4.0 %pick_rows.6 = bf16[128,4096]{1,0:T(8,128)(2,1)} custom-call(bf16[128,128]{1,0:T(8,128)(2,1)S(1)} %compare_convert_fusion.matrix_ref, bf16[128,4096]{1,0:T(8,128)(2,1)} %embed.3.refs_0_), custom_call_target="tpu_custom_call" | custom-call | flops 1 | bytes 1 | tf_op jit(solution)/shard_map/pick_rows/pallas_call | solution.py:220
  47.5 3.6 %all-to-all-start.1 = ((bf16[8,16,4096]{2,1,0:T(8,128)(2,1)}), bf16[8,16,4096]{2,1,0:T(8,128)(2,1)S(1)}, u32[]{:S(2)}, u32[]{:S(2)}) async-start(bf16[8,16,4096]{2,1,0:T(8,128)(2,1)} %bitcast.7), calls=%async_computation.1 | async-start | bytes 2097152 | tf_op jit(solution)/shard_map/all_to_all | solution.py:61
  51.8 10.4 %all-gather.2.cloned.1.call-done.refs_0_ = bf16[512,4096]{1,0:T(8,128)(2,1)} async-done(((bf16[128,4096]{1,0:T(8,128)(2,1)}), bf16[512,4096]{1,0:T(8,128)(2,1)}) %all-gather.2.cloned.1.call-update) | async-done | bytes 4194320 | tf_op jit(solution)/shard_map/all_gather | solution.py:460
  64.3 3.9 %pick_rows.7 = bf16[384,4096]{1,0:T(8,128)(2,1)} custom-call(bf16[384,512]{1,0:T(8,128)(2,1)S(1)} %fusion.1.matrix_ref, bf16[512,4096]{1,0:T(8,128)(2,1)S(1)} %copy-done.5), custom_call_target="tpu_custom_call" | custom-call | flops 1 | bytes 1 | tf_op jit(solution)/shard_map/pick_rows/pallas_call | solution.py:220
  69.2 4.6 %all-to-all-start.2 = ((bf16[8,48,4096]{2,1,0:T(8,128)(2,1)}), bf16[8,48,4096]{2,1,0:T(8,128)(2,1)S(1)}, u32[]{:S(2)}, u32[]{:S(2)}) async-start(bf16[8,48,4096]{2,1,0:T(8,128)(2,1)} %bitcast.12), calls=%async_computation.2 | async-start | bytes 6291456 | tf_op jit(solution)/shard_map/all_to_all | solution.py:61
  78.9 3.7 %collective-permute-done.6 = s32[1,128]{1,0:T(1,128)S(1)} collective-permute-done((s32[1,128]{1,0:T(1,128)S(1)}, s32[1,128]{1,0:T(1,128)S(1)}, u32[]{:S(2)}, u32[]{:S(2)}) %collective-permute-start.6) | collective-permute-done | bytes 544 | tf_op jit(solution)/shard_map/ppermute | solution.py:21
  86.2 3.2 %collective-permute-start.4 = (bf16[64,4096]{1,0:T(8,128)(2,1)}, bf16[64,4096]{1,0:T(8,128)(2,1)}, u32[]{:S(2)}, u32[]{:S(2)}) collective-permute-start(bf16[64,4096]{1,0:T(8,128)(2,1)} %copy-done.36), channel_id=1, source_target_pairs={{0,3},{1,0},{2,1},{3,2},{4,7},{5,4},{6,5},{7,6},{8,11},{9,8},{10,9... | collective-permute-start | bytes 1572872 | tf_op jit(solution)/shard_map/ppermute | solution.py:21
  89.9 10.7 %collective-permute-done.5.refs_7_ = bf16[64,4096]{1,0:T(8,128)(2,1)} collective-permute-done((bf16[64,4096]{1,0:T(8,128)(2,1)}, bf16[64,4096]{1,0:T(8,128)(2,1)}, u32[]{:S(2)}, u32[]{:S(2)}) %collective-permute-start.5) | collective-permute-done | bytes 524320 | tf_op jit(solution)/shard_map/ppermute | solution.py:21
  113.2 3.8 %pick_rows.4 = bf16[384,4096]{1,0:T(8,128)(2,1)} custom-call(bf16[384,512]{1,0:T(8,128)(2,1)S(1)} %fusion.matrix_ref, bf16[512,4096]{1,0:T(8,128)(2,1)S(1)} %in_order.1.refs_0_.query_ref), custom_call_target="tpu_custom_call" | custom-call | flops 1 | bytes 1 | tf_op jit(solution)/shard_map/pick_rows/pallas_call | solution.py:220
  117.0 4.3 %line_scores.1.near_ref = f32[640,512]{1,0:T(8,128)S(1)} custom-call(bf16[512,4096]{1,0:T(8,128)(2,1)S(1)} %in_order.1.refs_0_.query_ref, bf16[512,4096]{1,0:T(8,128)(2,1)S(1)} %copy-done.6, bf16[128,4096]{1,0:T(8,128)(2,1)S(1)} %bitcast.55), custom_call_target="tpu_custom_call" | custom-call | flops 1 | bytes 1 | tf_op jit(solution)/shard_map/line_scores/pallas_call | solution.py:272
  122.4 4.5 %all-to-all-start.4 = ((bf16[8,48,4096]{2,1,0:T(8,128)(2,1)}), bf16[8,48,4096]{2,1,0:T(8,128)(2,1)}, u32[]{:S(2)}, u32[]{:S(2)}) async-start(bf16[8,48,4096]{2,1,0:T(8,128)(2,1)} %bitcast.35), calls=%async_computation.5 | async-start | bytes 6291456 | tf_op jit(solution)/shard_map/all_to_all | solution.py:61
  131.5 3.7 %far_scores.1 = (f32[384,512]{1,0:T(8,128)S(1)}, f32[1,512]{1,0:T(1,128)S(1)}) custom-call(f32[640,512]{1,0:T(8,128)S(1)} %copy-done.12, bf16[512,512]{1,0:T(8,128)(2,1)S(1)} %copy-done.21, bf16[512,4096]{1,0:T(8,128)(2,1)S(1)} %copy-done.1, bf16[384,4096]{1,0:T(8,128)(2,1)S(1)} %bitcast.53), custom_call_target="tpu_custom_call" | custom-call | flops 99999997952 | bytes 100000000 | tf_op jit(solution)/shard_map/far_scores/pallas_call | solution.py:316
  153.1 7.5 %query_side.1 = (bf16[512,4096]{1,0:T(8,128)(2,1)S(1)}, f32[1,4096]{1,0:T(1,128)S(1)}, f32[8,512]{1,0:T(8,128)S(1)}, f32[1,512]{1,0:T(1,128)S(1)}, bf16[128,512]...) custom-call(f32[640,512]{1,0:T(8,128)S(1)} %copy-done.13, f32[384,512]{1,0:T(8,128)S(1)} %copy-done.29, ...), custom_call_target="tpu_custom_call" | custom-call | flops 1 | bytes 1 | tf_op jit(solution)/shard_map/query_side/pallas_call | solution.py:384
  167.3 3.3 %collective-permute-start.15 = (f32[1,64]{1,0:T(1,128)S(1)}, f32[1,64]{1,0:T(1,128)S(1)}, u32[]{:S(2)}, u32[]{:S(2)}) collective-permute-start(f32[1,64]{1,0:T(1,128)S(1)} %bitcast.82), channel_id=1, source_target_pairs={{0,64},{16,80},{32,96},{48,112},{64,0},{80,16},{96,32},{112,48},{1... | collective-permute-start | bytes 776 | tf_op jit(solution)/shard_map/ppermute | solution.py:75
  175.8 3.6 %all-to-all-start.3 = ((bf16[8,16,4096]{2,1,0:T(8,128)(2,1)}), bf16[8,16,4096]{2,1,0:T(8,128)(2,1)S(1)}, u32[]{:S(2)}, u32[]{:S(2)}) async-start(bf16[8,16,4096]{2,1,0:T(8,128)(2,1)} %bitcast.33), calls=%async_computation.3 | async-start | bytes 2097152 | tf_op jit(solution)/shard_map/all_to_all | solution.py:61
  183.1 6.4 %passage_side.3 = (bf16[64,4096]{1,0:T(8,128)(2,1)S(1)}, bf16[64,4096]{1,0:T(8,128)(2,1)}, bf16[64,4096]{1,0:T(8,128)(2,1)}, bf16[64,4096]{1,0:T(8,128)(2,1)S(1)...) custom-call(bf16[384,512]{1,0:T(8,128)(2,1)S(1)} %copy-done.42, bf16[512,4096]{1,0:T(8,128)(2,1)S(1)} %copy-done.3, ...), custom_call_target="tpu_custom_call" | custom-call | flops 99999997952 | bytes 100000000 | tf_op jit(solution)/shard_map/passage_side/pallas_call | solution.py:432
  190.5 4.7 %all-to-all-done.3 = bf16[8,16,4096]{2,1,0:T(8,128)(2,1)S(1)} async-done(((bf16[8,16,4096]{2,1,0:T(8,128)(2,1)}), bf16[8,16,4096]{2,1,0:T(8,128)(2,1)S(1)}, u32[]{:S(2)}, u32[]{:S(2)}) %all-to-all-start.3) | async-done | bytes 1048608 | tf_op jit(solution)/shard_map/all_to_all | solution.py:61
  196.4 4.2 %collective-permute-done.26 = f32[32,128]{1,0:T(8,128)S(1)} collective-permute-done((f32[32,128]{1,0:T(8,128)S(1)}, f32[32,128]{1,0:T(8,128)S(1)}, u32[]{:S(2)}, u32[]{:S(2)}) %collective-permute-start.26) | collective-permute-done | bytes 16416 | tf_op jit(solution)/shard_map/ppermute | solution.py:53
  200.8 5.4 %collective-permute-done.27 = f32[32,128]{1,0:T(8,128)S(1)} collective-permute-done((f32[32,128]{1,0:T(8,128)S(1)}, f32[32,128]{1,0:T(8,128)S(1)}, u32[]{:S(2)}, u32[]{:S(2)}) %collective-permute-start.27) | collective-permute-done | bytes 16416 | tf_op jit(solution)/shard_map/ppermute | solution.py:55
  217.6 16.3 %collective-permute-done.23 = bf16[64,4096]{1,0:T(8,128)(2,1)S(1)} collective-permute-done((bf16[64,4096]{1,0:T(8,128)(2,1)S(1)}, bf16[64,4096]{1,0:T(8,128)(2,1)S(1)}, u32[]{:S(2)}, u32[]{:S(2)}) %collective-permute-start.23) | collective-permute-done | bytes 524320 | tf_op jit(solution)/shard_map/ppermute | solution.py:21
  237.8 8.3 %collective-permute-done.30 = f32[32,128]{1,0:T(8,128)S(1)} collective-permute-done((f32[32,128]{1,0:T(8,128)S(1)}, f32[32,128]{1,0:T(8,128)S(1)}, u32[]{:S(2)}, u32[]{:S(2)}) %collective-permute-start.30) | collective-permute-done | bytes 16416 | tf_op jit(solution)/shard_map/ppermute | solution.py:53
  256.1 4.4 %finish.3 = bf16[128,4096]{1,0:T(8,128)(2,1)} custom-call(bf16[128,4096]{1,0:T(8,128)(2,1)S(1)} %copy-done.20, f32[1,4096]{1,0:T(1,128)S(1)} %bitcast.61, f32[128,4096]{1,0:T(8,128)S(1)} %passage_side.2.refs_0_, bf16[64,4096]{1,0:T(8,128)(2,1)} %collective-permute-done.20.refs_1_, bf16[64,4096]{1,0:T(8,128)(2,1)} %collective-permute-done.21.refs_2_, ...), custom_call_target="tpu_custom_call" | custom-call | flops 1 | bytes 1 | tf_op jit(solution)/shard_map/finish/pallas_call | solution.py:199
  (252 shorter events, 105.6 us)
Async XLA Ops:
  7.2 54.9 %all-gather.2.cloned.1.call-start = ((), (), s32[]{:S(2)}) async-start(), calls=%async_computation.6 | async-start | bytes 5242880 | tf_op jit(solution)/shard_map/all_gather | solution.py:460
  12.1 31.0 %collective-permute-start.3 = (bf16[64,4096]{1,0:T(8,128)(2,1)S(1)}, bf16[64,4096]{1,0:T(8,128)(2,1)S(1)}, u32[]{:S(2)}, u32[]{:S(2)}) collective-permute-start(bf16[64,4096]{1,0:T(8,128)(2,1)S(1)} %get-tuple-element.67.refs_1_), channel_id=1, source_target_pairs={{0,1},{1,2},{2,3},{3,0},{4,5},{5,6},{6,7},{7,4},{8,9},{9,10},{10,1... | collective-permute-start | bytes 1572872 | tf_op jit(solution)/shard_map/ppermute | solution.py:21
  13.7 29.3 %collective-permute-start.1 = (bf16[64,4096]{1,0:T(8,128)(2,1)S(1)}, bf16[64,4096]{1,0:T(8,128)(2,1)S(1)}, u32[]{:S(2)}, u32[]{:S(2)}) collective-permute-start(bf16[64,4096]{1,0:T(8,128)(2,1)S(1)} %get-tuple-element.67.refs_1_), channel_id=1, source_target_pairs={{0,3},{1,0},{2,1},{3,2},{4,7},{5,4},{6,5},{7,6},{8,11},{9,8},{10,9... | collective-permute-start | bytes 1572872 | tf_op jit(solution)/shard_map/ppermute | solution.py:21
  15.4 27.7 %collective-permute-start.2 = (bf16[64,4096]{1,0:T(8,128)(2,1)S(1)}, bf16[64,4096]{1,0:T(8,128)(2,1)S(1)}, u32[]{:S(2)}, u32[]{:S(2)}) collective-permute-start(bf16[64,4096]{1,0:T(8,128)(2,1)S(1)} %get-tuple-element.68.refs_0_), channel_id=1, source_target_pairs={{0,1},{1,2},{2,3},{3,0},{4,5},{5,6},{6,7},{7,4},{8,9},{9,10},{10,1... | collective-permute-start | bytes 1572872 | tf_op jit(solution)/shard_map/ppermute | solution.py:21
  15.8 27.3 %collective-permute-start = (bf16[64,4096]{1,0:T(8,128)(2,1)S(1)}, bf16[64,4096]{1,0:T(8,128)(2,1)S(1)}, u32[]{:S(2)}, u32[]{:S(2)}) collective-permute-start(bf16[64,4096]{1,0:T(8,128)(2,1)S(1)} %get-tuple-element.68.refs_0_), channel_id=1, source_target_pairs={{0,3},{1,0},{2,1},{3,2},{4,7},{5,4},{6,5},{7,6},{8,11},{9,8},{10,9... | collective-permute-start | bytes 1572872 | tf_op jit(solution)/shard_map/ppermute | solution.py:21
  20.1 22.8 %all-to-all-start = ((s32[32,1,16]{2,1,0:T(1,128)}), s32[32,1,16]{2,1,0:T(1,128)S(1)}, u32[]{:S(2)}, u32[]{:S(2)}) async-start(s32[32,1,16]{2,1,0:T(1,128)} %bitcast.5), calls=%async_computation | async-start | bytes 32768 | tf_op jit(solution)/shard_map/all_to_all | solution.py:478
  47.5 20.8 %all-to-all-start.1 = ((bf16[8,16,4096]{2,1,0:T(8,128)(2,1)}), bf16[8,16,4096]{2,1,0:T(8,128)(2,1)S(1)}, u32[]{:S(2)}, u32[]{:S(2)}) async-start(bf16[8,16,4096]{2,1,0:T(8,128)(2,1)} %bitcast.7), calls=%async_computation.1 | async-start | bytes 2097152 | tf_op jit(solution)/shard_map/all_to_all | solution.py:61
  69.2 53.2 %all-to-all-start.2 = ((bf16[8,48,4096]{2,1,0:T(8,128)(2,1)}), bf16[8,48,4096]{2,1,0:T(8,128)(2,1)S(1)}, u32[]{:S(2)}, u32[]{:S(2)}) async-start(bf16[8,48,4096]{2,1,0:T(8,128)(2,1)} %bitcast.12), calls=%async_computation.2 | async-start | bytes 6291456 | tf_op jit(solution)/shard_map/all_to_all | solution.py:61
  74.1 10.8 %collective-permute-start.8 = (s32[1,128]{1,0:T(1,128)S(1)}, s32[1,128]{1,0:T(1,128)S(1)}, u32[]{:S(2)}, u32[]{:S(2)}) collective-permute-start(s32[1,128]{1,0:T(1,128)S(1)} %broadcast_in_dim.377), channel_id=1, source_target_pairs={{0,3},{1,0},{2,1},{3,2},{4,7},{5,4},{6,5},{7,6},{8,11},{9,8},{10,9... | collective-permute-start | bytes 1544 | tf_op jit(solution)/shard_map/ppermute | solution.py:21
  76.8 7.1 %collective-permute-start.7 = (s32[1,128]{1,0:T(1,128)S(1)}, s32[1,128]{1,0:T(1,128)S(1)}, u32[]{:S(2)}, u32[]{:S(2)}) collective-permute-start(s32[1,128]{1,0:T(1,128)S(1)} %broadcast_in_dim.372), channel_id=1, source_target_pairs={{0,2},{1,3},{2,0},{3,1},{4,6},{5,7},{6,4},{7,5},{8,10},{9,11},{10,... | collective-permute-start | bytes 1544 | tf_op jit(solution)/shard_map/ppermute | solution.py:21
  86.1 14.5 %collective-permute-start.5 = (bf16[64,4096]{1,0:T(8,128)(2,1)}, bf16[64,4096]{1,0:T(8,128)(2,1)}, u32[]{:S(2)}, u32[]{:S(2)}) collective-permute-start(bf16[64,4096]{1,0:T(8,128)(2,1)} %copy-done.30), channel_id=1, source_target_pairs={{0,1},{1,2},{2,3},{3,0},{4,5},{5,6},{6,7},{7,4},{8,9},{9,10},{10,1... | collective-permute-start | bytes 1572872 | tf_op jit(solution)/shard_map/ppermute | solution.py:21
  86.2 14.4 %collective-permute-start.4 = (bf16[64,4096]{1,0:T(8,128)(2,1)}, bf16[64,4096]{1,0:T(8,128)(2,1)}, u32[]{:S(2)}, u32[]{:S(2)}) collective-permute-start(bf16[64,4096]{1,0:T(8,128)(2,1)} %copy-done.36), channel_id=1, source_target_pairs={{0,3},{1,0},{2,1},{3,2},{4,7},{5,4},{6,5},{7,6},{8,11},{9,8},{10,9... | collective-permute-start | bytes 1572872 | tf_op jit(solution)/shard_map/ppermute | solution.py:21
  122.4 53.3 %all-to-all-start.4 = ((bf16[8,48,4096]{2,1,0:T(8,128)(2,1)}), bf16[8,48,4096]{2,1,0:T(8,128)(2,1)}, u32[]{:S(2)}, u32[]{:S(2)}) async-start(bf16[8,48,4096]{2,1,0:T(8,128)(2,1)} %bitcast.35), calls=%async_computation.5 | async-start | bytes 6291456 | tf_op jit(solution)/shard_map/all_to_all | solution.py:61
  126.9 125.5 %reduce-scatter.2.cloned.1.call-start = ((), (), s32[]{:S(2)}) async-start(), calls=%async_computation.7 | async-start | bytes 5242880 | tf_op jit(solution)/shard_map/reduce_scatter | solution.py:538
  163.6 7.0 %collective-permute-start.18 = (f32[1,64]{1,0:T(1,128)S(1)}, f32[1,64]{1,0:T(1,128)S(1)}, u32[]{:S(2)}, u32[]{:S(2)}) collective-permute-start(f32[1,64]{1,0:T(1,128)S(1)} %bitcast.87), channel_id=1, source_target_pairs={{0,112},{16,96},{32,16},{48,0},{64,48},{80,32},{96,80},{112,64},{1... | collective-permute-start | bytes 776 | tf_op jit(solution)/shard_map/ppermute | solution.py:75
  165.5 6.3 %collective-permute-start.17 = (f32[1,64]{1,0:T(1,128)S(1)}, f32[1,64]{1,0:T(1,128)S(1)}, u32[]{:S(2)}, u32[]{:S(2)}) collective-permute-start(f32[1,64]{1,0:T(1,128)S(1)} %bitcast.86), channel_id=1, source_target_pairs={{0,96},{16,112},{32,0},{48,16},{64,32},{80,48},{96,64},{112,80},{1... | collective-permute-start | bytes 776 | tf_op jit(solution)/shard_map/ppermute | solution.py:75
  175.8 19.5 %all-to-all-start.3 = ((bf16[8,16,4096]{2,1,0:T(8,128)(2,1)}), bf16[8,16,4096]{2,1,0:T(8,128)(2,1)S(1)}, u32[]{:S(2)}, u32[]{:S(2)}) async-start(bf16[8,16,4096]{2,1,0:T(8,128)(2,1)} %bitcast.33), calls=%async_computation.3 | async-start | bytes 2097152 | tf_op jit(solution)/shard_map/all_to_all | solution.py:61
  189.5 25.9 %collective-permute-start.19 = (bf16[64,4096]{1,0:T(8,128)(2,1)}, bf16[64,4096]{1,0:T(8,128)(2,1)}, u32[]{:S(2)}, u32[]{:S(2)}) collective-permute-start(bf16[64,4096]{1,0:T(8,128)(2,1)} %get-tuple-element.47), channel_id=1, source_target_pairs={{0,4},{4,8},{8,12},{12,0},{1,5},{5,9},{9,13},{13,1},{2,6},{6,10},{... | collective-permute-start | bytes 1572872 | tf_op jit(solution)/shard_map/ppermute | solution.py:21
  211.0 45.1 %collective-permute-start.21 = (bf16[64,4096]{1,0:T(8,128)(2,1)}, bf16[64,4096]{1,0:T(8,128)(2,1)}, u32[]{:S(2)}, u32[]{:S(2)}) collective-permute-start(bf16[64,4096]{1,0:T(8,128)(2,1)} %get-tuple-element.48), channel_id=1, source_target_pairs={{0,12},{4,0},{8,4},{12,8},{1,13},{5,1},{9,5},{13,9},{2,14},{6,2},{... | collective-permute-start | bytes 1572872 | tf_op jit(solution)/shard_map/ppermute | solution.py:21
  212.1 44.0 %collective-permute-start.22 = (bf16[64,4096]{1,0:T(8,128)(2,1)}, bf16[64,4096]{1,0:T(8,128)(2,1)}, u32[]{:S(2)}, u32[]{:S(2)}) collective-permute-start(bf16[64,4096]{1,0:T(8,128)(2,1)} %get-tuple-element.49), channel_id=1, source_target_pairs={{0,4},{4,8},{8,12},{12,0},{1,5},{5,9},{9,13},{13,1},{2,6},{6,10},{... | collective-permute-start | bytes 1572872 | tf_op jit(solution)/shard_map/ppermute | solution.py:21
  213.1 20.9 %collective-permute-start.23 = (bf16[64,4096]{1,0:T(8,128)(2,1)S(1)}, bf16[64,4096]{1,0:T(8,128)(2,1)S(1)}, u32[]{:S(2)}, u32[]{:S(2)}) collective-permute-start(bf16[64,4096]{1,0:T(8,128)(2,1)S(1)} %get-tuple-element.51), channel_id=1, source_target_pairs={{0,12},{4,0},{8,4},{12,8},{1,13},{5,1},{9,5},{13,9},{2,14},{6,2},{... | collective-permute-start | bytes 1572872 | tf_op jit(solution)/shard_map/ppermute | solution.py:21
  217.4 38.7 %collective-permute-start.20 = (bf16[64,4096]{1,0:T(8,128)(2,1)}, bf16[64,4096]{1,0:T(8,128)(2,1)}, u32[]{:S(2)}, u32[]{:S(2)}) collective-permute-start(bf16[64,4096]{1,0:T(8,128)(2,1)} %add_convert_fusion.1), channel_id=1, source_target_pairs={{0,4},{4,8},{8,12},{12,0},{1,5},{5,9},{9,13},{13,1},{2,6},{6,10},{... | collective-permute-start | bytes 1572872 | tf_op jit(solution)/shard_map/ppermute | solution.py:21
  234.9 21.2 %collective-permute-start.24 = (bf16[64,4096]{1,0:T(8,128)(2,1)}, bf16[64,4096]{1,0:T(8,128)(2,1)}, u32[]{:S(2)}, u32[]{:S(2)}) collective-permute-start(bf16[64,4096]{1,0:T(8,128)(2,1)} %add_convert_fusion), channel_id=1, source_target_pairs={{0,12},{4,0},{8,4},{12,8},{1,13},{5,1},{9,5},{13,9},{2,14},{6,2},{... | collective-permute-start | bytes 1572872 | tf_op jit(solution)/shard_map/ppermute | solution.py:21
  237.2 8.9 %collective-permute-start.30 = (f32[32,128]{1,0:T(8,128)S(1)}, f32[32,128]{1,0:T(8,128)S(1)}, u32[]{:S(2)}, u32[]{:S(2)}) collective-permute-start(f32[32,128]{1,0:T(8,128)S(1)} %add.437), channel_id=1, source_target_pairs={{0,4},{4,0},{8,12},{12,8},{1,5},{5,1},{9,13},{13,9},{2,6},{6,2},{1... | collective-permute-start | bytes 49160 | tf_op jit(solution)/shard_map/ppermute | solution.py:53
  (64 other events, 502.8 us)
Sparse Core Ops, SparseCore 0:
  11.3 50.7 all-gather.1
  172.1 46.0 reduce-scatter.1

commit v4 on v2

--- a/solution.py
+++ b/solution.py
@@ -21,13 +21,17 @@
     return lax.ppermute(value, axis, [(i, (i + step) % RING) for i in range(RING)])
 
 
-def axes_sum(value, axes):
-    for axis in axes:
-        size = lax.axis_size(axis)
-        value = value + lax.ppermute(value, axis, [(i, i ^ 1) for i in range(size)])
-        if size > 2:
-            value = value + lax.ppermute(value, axis, [(i, size - 1 - i) for i in range(size)])
-    return value
+def ring_gather(block, axis):
+    half = block.shape[0] // 2
+    up = shift(block, axis, -1)
+    down = shift(block, axis, 1)
+    return [up, down], [shift(up[:half], axis, -1), shift(down[half:], axis, 1)]
+
+
+def pair_sum(value, axis, turn):
+    size = lax.axis_size(axis)
+    pairs = [(i, size - 1 - i if turn else i ^ 1) for i in range(size)]
+    return value + lax.ppermute(value, axis, pairs)
 
 
 def group_rows(rows, group_count):
@@ -155,7 +159,7 @@
     )(hidden, gain, *terms)
 
 
-def pick_rows(matrix, sources, cost=SMALL):
+def pick_rows(matrix, sources):
     width = sources[0].shape[1]
 
     def body(matrix_ref, *refs):
@@ -168,35 +172,9 @@
         out_specs=columns(matrix.shape[0], width),
         out_shape=jax.ShapeDtypeStruct((matrix.shape[0], width), jnp.bfloat16),
         compiler_params=params(16),
-        cost_estimate=cost,
+        cost_estimate=SMALL,
         name="pick_rows",
     )(matrix, *sources)
-
-
-def pick_into(matrix, sources, shape, at, held=None):
-    width = sources[0].shape[1]
-    groups = shape[0]
-    size = matrix.shape[0] // groups
-
-    def body(matrix_ref, *refs):
-        picked = mxu(matrix_ref[...], joined(refs[: len(sources)])).astype(jnp.bfloat16)
-        refs[-1][...] = picked.reshape(groups, size, picked.shape[1])
-
-    place = pl.BlockSpec((groups, size, tile(width)), lambda i: (0, at // size, i))
-    more = () if held is None else (held,)
-    return pl.pallas_call(
-        body,
-        grid=(width // tile(width),),
-        in_specs=[whole(matrix.shape)]
-        + [columns(s.shape[0], width) for s in sources]
-        + [pl.BlockSpec(memory_space=pl.ANY)] * len(more),
-        out_specs=place,
-        out_shape=jax.ShapeDtypeStruct(shape, jnp.bfloat16),
-        input_output_aliases={1 + len(sources): 0} if more else {},
-        compiler_params=params(16),
-        cost_estimate=SMALL,
-        name="pick_into",
-    )(matrix, *sources, *more)
 
 
 def line_scores(sources, queries, scale):
@@ -358,15 +336,18 @@
     )(near, far, asked_by, log_total, weight, target, queries, *sources)
 
 
-def passage_side(coeff, queries, put, arrived, scale, out_type, pieces):
+def passage_side(coeff, queries, put, arrived, scale, out_type, layout, cost):
     width = queries.shape[1]
-    rows = coeff.shape[0] // pieces
+    sizes = [sum(high - low for low, high in ranges) for ranges in layout]
 
     def body(coeff_ref, query_ref, put_ref, arrived_ref, *out_refs):
         total = mxu(coeff_ref[...], query_ref[...]) + mxu(put_ref[...], arrived_ref[...])
         total = scale * total
-        for i, out_ref in enumerate(out_refs):
-            out_ref[...] = total[i * rows : (i + 1) * rows].astype(out_type)
+        for ranges, out_ref in zip(layout, out_refs):
+            at = 0
+            for low, high in ranges:
+                out_ref[at : at + high - low] = total[low:high].astype(out_type)
+                at += high - low
 
     return pl.pallas_call(
         body,
@@ -377,12 +358,35 @@
             whole(put.shape),
             columns(arrived.shape[0], width),
         ],
-        out_specs=[columns(rows, width)] * pieces,
-        out_shape=[jax.ShapeDtypeStruct((rows, width), out_type)] * pieces,
+        out_specs=[columns(size, width) for size in sizes],
+        out_shape=[jax.ShapeDtypeStruct((size, width), out_type) for size in sizes],
         compiler_params=params(20),
-        cost_estimate=LARGE if pieces > 1 else SMALL,
+        cost_estimate=cost,
         name="passage_side",
     )(coeff, queries, put, arrived)
+
+
+def add_passing(up, passing_low, down, passing_high):
+    half, width = passing_low.shape
+
+    def body(up_ref, low_ref, down_ref, high_ref, up_out, down_out):
+        wide = jnp.float32
+        up_out[...] = (up_ref[...].astype(wide) + low_ref[...].astype(wide)).astype(up.dtype)
+        down_out[...] = (down_ref[...].astype(wide) + high_ref[...].astype(wide)).astype(up.dtype)
+
+    low = pl.BlockSpec((half, tile(width)), lambda i: (0, i))
+    high = pl.BlockSpec((half, tile(width)), lambda i: (1, i))
+    return pl.pallas_call(
+        body,
+        grid=(width // tile(width),),
+        in_specs=[low, low, high, low],
+        out_specs=[low, high],
+        out_shape=[jax.ShapeDtypeStruct(up.shape, up.dtype)] * 2,
+        input_output_aliases={0: 0, 2: 1},
+        compiler_params=params(12),
+        cost_estimate=SMALL,
+        name="add_passing",
+    )(up, passing_low, down, passing_high)
 
 
 def on_device(query_hidden, passage_hidden, norm_gain, query_weight, hneg_ids):
@@ -396,8 +400,7 @@
 
     gain = norm_gain.reshape(1, width)
     p_own = embed(passage_hidden, gain)
-    p_mid = [shift(p_own, "y", -1), shift(p_own, "y", 1)]
-    p_opp = shift(p_own, "y", 2)
+    p_mid, p_opp = ring_gather(p_own, "y")
 
     flat_ids = hneg_ids.reshape(-1)
     id_count = rows * neg_count
@@ -418,24 +421,19 @@
     )
     asked = asked.reshape(group_count, RING, RING, CAP).transpose(0, 2, 1, 3)
     place = jnp.arange(line, dtype=jnp.int32)
-    asked, _ = lax.optimization_barrier((asked, p_mid[0]))
+    asked, _ = lax.optimization_barrier((asked, p_mid))
     asked_own = asked[:, 0].reshape(-1)
     above = jnp.where(asked[:, 3:] < 0, -1, asked[:, 3:] + rows)
-    asked_mid = jnp.concatenate([asked[:, 1:2], above], axis=1)
     opposite = jnp.where(asked[:, 2:3] < 0, -1, asked[:, 2:3] + 2 * rows)
-    asked_far = jnp.concatenate([asked_mid, opposite], axis=1).reshape(-1)
+    asked_far = jnp.concatenate([asked[:, 1:2], above, opposite], axis=1).reshape(-1)
 
     def one_hot(numbers, size):
         return (numbers[:, None] == place[None, :size]).astype(jnp.bfloat16)
 
-    hard_own = group_rows(pick_rows(one_hot(asked_own, rows), [p_own]), group_count)
-    per_owner = RING * CAP
-    shape = (group_count, 3 * per_owner, width)
-    chosen = pick_into(one_hot(asked_mid.reshape(-1), 2 * rows), p_mid, shape, 0)
-    chosen = pick_into(
-        one_hot(asked[:, 2].reshape(-1), rows), [p_opp], shape, 2 * per_owner, chosen
-    )
-    hard_far = group_rows(chosen.reshape(-1, width), group_count)
+    chosen_own = pick_rows(one_hot(asked_own, rows), [p_own])
+    hard_own = group_rows(chosen_own, group_count)
+    chosen_far = pick_rows(one_hot(asked_far, 3 * rows), [*p_mid, *p_opp])
+    hard_far = group_rows(chosen_far, group_count)
 
     q_emb = embed(query_hidden, gain)
     q_line = lax.all_gather(q_emb, "x", axis=0, tiled=True)
@@ -455,7 +453,7 @@
     far_queries = group_rows(leave_far, group_count)
     own_queries = group_rows(leave_own, group_count)
 
-    near = line_scores([p_own, *p_mid, p_opp, hard_own], q_line, scale)
+    near = line_scores([p_own, *p_mid, *p_opp, hard_own], q_line, scale)
     far, part_log = far_scores(near, [hard_far], q_line, asked_by, line, scale)
     part_log = part_log.reshape(RING, rows)
     own_place = jnp.arange(RING, dtype=jnp.int32)[:, None] == x_place
@@ -472,7 +470,7 @@
 
     part, gain_part, slot_coeff, positive, coeff_own, coeff_far = query_side(
         near, far, asked_by, log_total, weight, target, q_line,
-        [p_own, *p_mid, p_opp, hard_own, hard_far], line, scale,
+        [p_own, *p_mid, *p_opp, hard_own, hard_far], line, scale,
     )
     loss_rows = lax.dynamic_slice(log_total - positive, (0, first_row), (1, rows)).reshape(-1)
     query_up = lax.psum_scatter(part, "x", scatter_dimension=0, tiled=True)
@@ -493,17 +491,28 @@
 
     put_own = put_rows(asked_own, got_coeff[:, :first], rows)
     put_far = put_rows(asked_far, got_coeff[:, first:], 3 * rows)
-    above, below, far = passage_side(
-        coeff_far, q_line, put_far, far_queries, scale, jnp.bfloat16, 3
-    )
-    arrived = [shift(above, "y", 1), shift(below, "y", -1), shift(far, "y", 2)]
-    gain_part, own_queries = lax.optimization_barrier((gain_part, own_queries))
-    gain_part = axes_sum(gain_part.reshape(-1, 128), ("c", "x", "z", "y"))
+    half = rows // 2
+    low_1, high_1, low_3, high_3, low_2, high_2 = [(i * half, (i + 1) * half) for i in range(6)]
+    for_above, for_below, pass_up, pass_down = passage_side(
+        coeff_far, q_line, put_far, far_queries, scale, jnp.bfloat16,
+        [[low_1, high_1], [low_3, high_3], [low_2], [high_2]], LARGE,
+    )
+    for_above, for_below = add_passing(
+        for_above, shift(pass_up, "y", 1), for_below, shift(pass_down, "y", -1)
+    )
+    from_below = shift(for_above, "y", 1)
+    from_above = shift(for_below, "y", -1)
+    gain_part, _ = lax.optimization_barrier((gain_part.reshape(-1, 128), for_above))
+    gain_part = pair_sum(gain_part, "c", False)
+    for axis in ("x", "z", "y"):
+        gain_part = pair_sum(pair_sum(gain_part, axis, False), axis, True)
     gain_grad = 2.0 * gain_part.reshape(-1) / norm_gain
 
-    own_part = passage_side(coeff_own, q_line, put_own, own_queries, scale, jnp.float32, 1)[0]
+    own_part = passage_side(
+        coeff_own, q_line, put_own, own_queries, scale, jnp.float32, [[(0, rows)]], SMALL
+    )[0]
     own_part, query_grad = lax.optimization_barrier((own_part, query_grad))
-    passage_grad = finish(passage_hidden, gain, [own_part, *arrived])
+    passage_grad = finish(passage_hidden, gain, [own_part, from_below, from_above])
     return (loss_rows, query_grad, passage_grad, gain_grad)
 
 

time: 275 us -> 248 us (0.902)
  waiting for transfers between devices: 94.7 us -> 69.1 us
  local copies, waits for them, and re-layouts: 44.1 us -> 40.3 us
    ppermute x7, waiting for transfers between devices: 37.1 us -> 17.5 us  [pair_sum(): return value + lax.ppermute(value, axis, pairs)]
    unnamed x117 -> x107, local copies, waits for them, and re-layouts: 39.4 us -> 34.6 us
    ppermute x12 -> x14, waiting for transfers between devices: 37.3 us -> 33.3 us  [shift(): lax.ppermute(value, axis, [(i, (i + step) % RING) for i in range(RING)])]
    ppermute x12 -> x14, starting transfers between devices: 19.2 us -> 22.5 us  [shift(): lax.ppermute(value, axis, [(i, (i + step) % RING) for i in range(RING)])]
    all_to_all x4, waiting for transfers between devices: 11.3 us -> 8.2 us  [group_rows(): return lax.all_to_all(blocks, GROUPS, 0, 0, tiled=True).reshape(rows.shape)]
    pallas_call x3 -> x4, Pallas kernels: 6.42 us -> 9.41 us  [pick_rows(): pl.pallas_call(body, grid=(width // tile(width),), in_specs=[whole(matrix...]
    pallas_call x2 -> x1, Pallas kernels: 6.39 us -> 3.46 us  [add_passing(): pl.pallas_call(body, grid=(width // tile(width),), in_specs=[low, low, hi...]
  transfers between devices with their start and end apart: 33 -> 35, of which waited for: 18 -> 17; matrix products, arithmetic and copies ran while one was open for 5% -> 6% of each run, Pallas kernels for 16% -> 18%
where the time goes in v4:
time: 248 us; the launch traced here: 247 us
  waiting for transfers between devices  69.1 us (28%)
  starting transfers between devices  63.3 us (26%)
  Pallas kernels  51 us (21%)
  local copies, waits for them, and re-layouts  40.3 us (16%)
  between operations  14.8 us (6%)
  other arithmetic  8.57 us (3%)
    unnamed x107, local copies, waits for them, and re-layouts  34.6 us
    ppermute x14, waiting for transfers between devices, shift(): lax.ppermute(value, axis, [(i, (i + step) % RING) for i in range(RING)])  33.3 us
    ppermute x14, starting transfers between devices, shift(): lax.ppermute(value, axis, [(i, (i + step) % RING) for i in range(RING)])  22.5 us
    all_to_all x4, starting transfers between devices, group_rows(): return lax.all_to_all(blocks, GROUPS, 0, 0, tiled=True).reshape(rows.shape)  18.6 us
    ppermute x7, waiting for transfers between devices, pair_sum(): return value + lax.ppermute(value, axis, pairs)  17.5 us
    pallas_call x2, Pallas kernels, passage_side(): pl.pallas_call(body, grid=(width // tile(width),), in_specs=[whole(coeff....  9.82 us
    pallas_call x4, Pallas kernels, pick_rows(): pl.pallas_call(body, grid=(width // tile(width),), in_specs=[whole(matrix...  9.41 us
    ppermute x7, starting transfers between devices, group_table(): lax.ppermute(row, GROUPS, [(z * 2 + c, (z + z_step) % z_count * 2 + (c ^...  8.34 us
  transfers between devices with their start and end apart: 35, of which 17 were waited for; matrix products, arithmetic and copies ran while one was open for 6% of the time, Pallas kernels for 18%

profile of v4, /device:TPU:0, one launch (start us, length us, event | category | flops | bytes accessed | tf_op | source)
XLA Modules:
  0.0 247.0 jit_solution(9028096766090570831)
XLA Ops:
  17.7 8.2 %all-to-all-start = ((s32[32,1,16]{2,1,0:T(1,128)}), s32[32,1,16]{2,1,0:T(1,128)S(1)}, u32[]{:S(2)}, u32[]{:S(2)}) async-start(s32[32,1,16]{2,1,0:T(1,128)} %bitcast.4), calls=%async_computation | async-start | bytes 32768 | tf_op jit(solution)/shard_map/all_to_all | solution.py:419
  25.9 7.2 %all-to-all-done = s32[32,1,16]{2,1,0:T(1,128)S(1)} async-done(((s32[32,1,16]{2,1,0:T(1,128)}), s32[32,1,16]{2,1,0:T(1,128)S(1)}, u32[]{:S(2)}, u32[]{:S(2)}) %all-to-all-start) | async-done | bytes 2080 | tf_op jit(solution)/shard_map/all_to_all | solution.py:419
  33.3 5.4 %collective-permute-done.3.refs_1_.refs_0_ = bf16[128,4096]{1,0:T(8,128)(2,1)S(1)} collective-permute-done((bf16[128,4096]{1,0:T(8,128)(2,1)S(1)}, bf16[128,4096]{1,0:T(8,128)(2,1)S(1)}, u32[]{:S(2)}, u32[]{:S(2)}) %collective-permute-start.3) | collective-permute-done | bytes 1048608 | tf_op jit(solution)/shard_map/ppermute | solution.py:21
  38.7 3.4 %collective-permute-done.4.refs_2_.refs_1_ = bf16[128,4096]{1,0:T(8,128)(2,1)S(1)} collective-permute-done((bf16[128,4096]{1,0:T(8,128)(2,1)S(1)}, bf16[128,4096]{1,0:T(8,128)(2,1)S(1)}, u32[]{:S(2)}, u32[]{:S(2)}) %collective-permute-start.4) | collective-permute-done | bytes 1048608 | tf_op jit(solution)/shard_map/ppermute | solution.py:21
  44.5 5.3 %all-to-all-start.1 = ((bf16[8,16,4096]{2,1,0:T(8,128)(2,1)}), bf16[8,16,4096]{2,1,0:T(8,128)(2,1)}, u32[]{:S(2)}, u32[]{:S(2)}) async-start(bf16[8,16,4096]{2,1,0:T(8,128)(2,1)} %bitcast.50), calls=%async_computation.1 | async-start | bytes 2097152 | tf_op jit(solution)/shard_map/all_to_all | solution.py:39
  54.0 11.3 %collective-permute-done.5.refs_3_.refs_2_ = bf16[64,4096]{1,0:T(8,128)(2,1)} collective-permute-done((bf16[64,4096]{1,0:T(8,128)(2,1)}, bf16[64,4096]{1,0:T(8,128)(2,1)}, u32[]{:S(2)}, u32[]{:S(2)}) %collective-permute-start.5) | collective-permute-done | bytes 524320 | tf_op jit(solution)/shard_map/ppermute | solution.py:21
  67.3 4.0 %pick_rows.7 = bf16[384,4096]{1,0:T(8,128)(2,1)S(1)} custom-call(bf16[384,384]{1,0:T(8,128)(2,1)S(1)} %compare_convert_fusion.matrix_ref, bf16[128,4096]{1,0:T(8,128)(2,1)S(1)} %collective-permute-done.3.refs_1_.refs_0_, bf16[128,4096]{1,0:T(8,128)(2,1)S(1)} %collective-permute-done.4.refs_2_.refs_1_, ...), custom_call_target="tpu_custom_call" | custom-call | flops 1 | bytes 1 | tf_op jit(solution)/shard_map/pick_rows/pallas_call | solution.py:168
  73.0 4.6 %all-to-all-start.2 = ((bf16[8,48,4096]{2,1,0:T(8,128)(2,1)}), bf16[8,48,4096]{2,1,0:T(8,128)(2,1)}, u32[]{:S(2)}, u32[]{:S(2)}) async-start(bf16[8,48,4096]{2,1,0:T(8,128)(2,1)} %bitcast.48), calls=%async_computation.2 | async-start | bytes 6291456 | tf_op jit(solution)/shard_map/all_to_all | solution.py:39
  101.5 5.4 %line_scores.1.near_ref = f32[640,512]{1,0:T(8,128)S(1)} custom-call(bf16[512,4096]{1,0:T(8,128)(2,1)S(1)} %copy-done.1, bf16[128,4096]{1,0:T(8,128)(2,1)S(1)} %embed.3.refs_0_, bf16[128,4096]{1,0:T(8,128)(2,1)S(1)} %collective-permute-done.3.refs_1_.refs_0_, bf16[128,4096]{1,0:T(8,128)(2,1)S(1)} %collective-permute-done.4.refs_2_.refs_1_, ...), custom_call_target="tpu_custom_call" | custom-call | flops 1 | bytes 1 | tf_op jit(solution)/shard_map/line_scores/pallas_call | solution.py:195
  107.9 8.2 %all-to-all-done.2 = bf16[8,48,4096]{2,1,0:T(8,128)(2,1)} async-done(((bf16[8,48,4096]{2,1,0:T(8,128)(2,1)}), bf16[8,48,4096]{2,1,0:T(8,128)(2,1)}, u32[]{:S(2)}, u32[]{:S(2)}) %all-to-all-start.2) | async-done | bytes 3145760 | tf_op jit(solution)/shard_map/all_to_all | solution.py:39
  116.1 4.5 %all-to-all-start.4 = ((bf16[8,48,4096]{2,1,0:T(8,128)(2,1)}), bf16[8,48,4096]{2,1,0:T(8,128)(2,1)}, u32[]{:S(2)}, u32[]{:S(2)}) async-start(bf16[8,48,4096]{2,1,0:T(8,128)(2,1)} %bitcast.49), calls=%async_computation.5 | async-start | bytes 6291456 | tf_op jit(solution)/shard_map/all_to_all | solution.py:39
  125.2 5.3 %far_scores.1 = (f32[384,512]{1,0:T(8,128)S(1)}, f32[1,512]{1,0:T(1,128)S(1)}) custom-call(f32[640,512]{1,0:T(8,128)S(1)} %copy-done.11, bf16[512,512]{1,0:T(8,128)(2,1)S(1)} %copy-done.20, bf16[512,4096]{1,0:T(8,128)(2,1)S(1)} %copy-done.2, bf16[384,4096]{1,0:T(8,128)(2,1)} %bitcast.9.refs_0_.refs_6_), custom_call_target="tpu_custom_call" | custom-call | flops 99999997952 | bytes 100000000 | tf_op jit(solution)/shard_map/far_scores/pallas_call | solution.py:239
  135.7 3.3 %collective-permute-done.9 = f32[8,128]{1,0:T(8,128)S(1)} collective-permute-done((f32[8,128]{1,0:T(8,128)S(1)}, f32[8,128]{1,0:T(8,128)S(1)}, u32[]{:S(2)}, u32[]{:S(2)}) %collective-permute-start.9) | collective-permute-done | bytes 4128 | tf_op jit(solution)/shard_map/ppermute | solution.py:21
  139.1 8.3 %query_side.1 = (bf16[512,4096]{1,0:T(8,128)(2,1)S(1)}, f32[1,4096]{1,0:T(1,128)S(1)}, f32[8,512]{1,0:T(8,128)S(1)}, f32[1,512]{1,0:T(1,128)S(1)}, bf16[128,512]...) custom-call(f32[640,512]{1,0:T(8,128)S(1)} %copy-done.12, f32[384,512]{1,0:T(8,128)S(1)} %get-tuple-element.28.far_ref, ...), custom_call_target="tpu_custom_call" | custom-call | flops 1 | bytes 1 | tf_op jit(solution)/shard_map/query_side/pallas_call | solution.py:305
  166.2 6.5 %passage_side.3 = (bf16[128,4096]{1,0:T(8,128)(2,1)}, bf16[128,4096]{1,0:T(8,128)(2,1)}, bf16[64,4096]{1,0:T(8,128)(2,1)}, bf16[64,4096]{1,0:T(8,128)(2,1)}) custom-call(bf16[384,512]{1,0:T(8,128)(2,1)S(1)} %copy-done.34, bf16[512,4096]{1,0:T(8,128)(2,1)S(1)} %copy-done.4, bf16[384,384]{1,0:T(8,128)(2,1)S(1)} %select_convert_fusion.put_ref, ...), custom_call_target="tpu_custom_call" | custom-call | flops 99999997952 | bytes 100000000 | tf_op jit(solution)/shard_map/passage_side/pallas_call | solution.py:352
  175.9 4.3 %all-to-all-start.3 = ((bf16[8,16,4096]{2,1,0:T(8,128)(2,1)}), bf16[8,16,4096]{2,1,0:T(8,128)(2,1)}, u32[]{:S(2)}, u32[]{:S(2)}) async-start(bf16[8,16,4096]{2,1,0:T(8,128)(2,1)} %bitcast.51), calls=%async_computation.3 | async-start | bytes 2097152 | tf_op jit(solution)/shard_map/all_to_all | solution.py:39
  180.2 7.9 %collective-permute-done.17.low_ref = bf16[64,4096]{1,0:T(8,128)(2,1)S(1)} collective-permute-done((bf16[64,4096]{1,0:T(8,128)(2,1)}, bf16[64,4096]{1,0:T(8,128)(2,1)S(1)}, u32[]{:S(2)}, u32[]{:S(2)}) %collective-permute-start.17) | collective-permute-done | bytes 524320 | tf_op jit(solution)/shard_map/ppermute | solution.py:21
  191.8 3.5 %add_passing.1 = (bf16[128,4096]{1,0:T(8,128)(2,1)}, bf16[128,4096]{1,0:T(8,128)(2,1)}) custom-call(bf16[128,4096]{1,0:T(8,128)(2,1)} %get-tuple-element.38.up_ref, bf16[64,4096]{1,0:T(8,128)(2,1)S(1)} %copy-done.26, bf16[128,4096]{1,0:T(8,128)(2,1)} %get-tuple-element.40.down_ref, ...), custom_call_target="tpu_custom_call", output_to_operand_aliasing={{0}: (0, {}), {1}: (2, {})} | custom-call | flops 1 | bytes 1 | tf_op jit(solution)/shard_map/add_passing/pallas_call | solution.py:379
  200.1 3.3 %collective-permute-done.22 = f32[32,128]{1,0:T(8,128)S(1)} collective-permute-done((f32[32,128]{1,0:T(8,128)S(1)}, f32[32,128]{1,0:T(8,128)S(1)}, u32[]{:S(2)}, u32[]{:S(2)}) %collective-permute-start.22) | collective-permute-done | bytes 16416 | tf_op jit(solution)/shard_map/ppermute | solution.py:34
  205.1 3.3 %collective-permute-done.23 = f32[32,128]{1,0:T(8,128)S(1)} collective-permute-done((f32[32,128]{1,0:T(8,128)S(1)}, f32[32,128]{1,0:T(8,128)S(1)}, u32[]{:S(2)}, u32[]{:S(2)}) %collective-permute-start.23) | collective-permute-done | bytes 16416 | tf_op jit(solution)/shard_map/ppermute | solution.py:34
  208.8 3.3 %collective-permute-done.24 = f32[32,128]{1,0:T(8,128)S(1)} collective-permute-done((f32[32,128]{1,0:T(8,128)S(1)}, f32[32,128]{1,0:T(8,128)S(1)}, u32[]{:S(2)}, u32[]{:S(2)}) %collective-permute-start.24) | collective-permute-done | bytes 16416 | tf_op jit(solution)/shard_map/ppermute | solution.py:34
  213.8 3.3 %collective-permute-done.25 = f32[32,128]{1,0:T(8,128)S(1)} collective-permute-done((f32[32,128]{1,0:T(8,128)S(1)}, f32[32,128]{1,0:T(8,128)S(1)}, u32[]{:S(2)}, u32[]{:S(2)}) %collective-permute-start.25) | collective-permute-done | bytes 16416 | tf_op jit(solution)/shard_map/ppermute | solution.py:34
  224.5 3.4 %passage_side.2.refs_0_ = f32[128,4096]{1,0:T(8,128)S(1)} custom-call(bf16[128,512]{1,0:T(8,128)(2,1)S(1)} %copy-done.32, bf16[512,4096]{1,0:T(8,128)(2,1)S(1)} %copy-done.5, bf16[128,128]{1,0:T(8,128)(2,1)S(1)} %select_convert_fusion.1.put_ref, bf16[128,4096]{1,0:T(8,128)(2,1)} %bitcast.29.arrived_ref), custom_call_target="tpu_custom_call" | custom-call | flops 1 | bytes 1 | tf_op jit(solution)/shard_map/passage_side/pallas_call | solution.py:352
  236.0 4.2 %finish.3 = bf16[128,4096]{1,0:T(8,128)(2,1)} custom-call(bf16[128,4096]{1,0:T(8,128)(2,1)S(1)} %copy-done.18, f32[1,4096]{1,0:T(1,128)S(1)} %bitcast.55, f32[128,4096]{1,0:T(8,128)S(1)} %copy-done.9, bf16[128,4096]{1,0:T(8,128)(2,1)} %collective-permute-done.19.refs_1_, bf16[128,4096]{1,0:T(8,128)(2,1)} %collective-permute-done.20.refs_2_), custom_call_target="tpu_custom_call" | custom-call | flops 1 | bytes 1 | tf_op jit(solution)/shard_map/finish/pallas_call | solution.py:150
  (248 shorter events, 105.2 us)
Async XLA Ops:
  7.2 85.1 %all-gather.2.cloned.1.call-start = ((), (), s32[]{:S(2)}) async-start(), calls=%async_computation.6 | async-start | bytes 5242880 | tf_op jit(solution)/shard_map/all_gather | solution.py:439
  13.1 25.6 %collective-permute-start.3 = (bf16[128,4096]{1,0:T(8,128)(2,1)S(1)}, bf16[128,4096]{1,0:T(8,128)(2,1)S(1)}, u32[]{:S(2)}, u32[]{:S(2)}) collective-permute-start(bf16[128,4096]{1,0:T(8,128)(2,1)S(1)} %embed.3.refs_0_), channel_id=1, source_target_pairs={{0,12},{4,0},{8,4},{12,8},{1,13},{5,1},{9,5},{13,9},{2,14},{6,2},{... | collective-permute-start | bytes 3145736 | tf_op jit(solution)/shard_map/ppermute | solution.py:21
  16.2 25.8 %collective-permute-start.4 = (bf16[128,4096]{1,0:T(8,128)(2,1)S(1)}, bf16[128,4096]{1,0:T(8,128)(2,1)S(1)}, u32[]{:S(2)}, u32[]{:S(2)}) collective-permute-start(bf16[128,4096]{1,0:T(8,128)(2,1)S(1)} %embed.3.refs_0_), channel_id=1, source_target_pairs={{0,4},{4,8},{8,12},{12,0},{1,5},{5,9},{9,13},{13,1},{2,6},{6,10},{... | collective-permute-start | bytes 3145736 | tf_op jit(solution)/shard_map/ppermute | solution.py:21
  17.7 15.4 %all-to-all-start = ((s32[32,1,16]{2,1,0:T(1,128)}), s32[32,1,16]{2,1,0:T(1,128)S(1)}, u32[]{:S(2)}, u32[]{:S(2)}) async-start(s32[32,1,16]{2,1,0:T(1,128)} %bitcast.4), calls=%async_computation | async-start | bytes 32768 | tf_op jit(solution)/shard_map/all_to_all | solution.py:419
  44.5 28.6 %all-to-all-start.1 = ((bf16[8,16,4096]{2,1,0:T(8,128)(2,1)}), bf16[8,16,4096]{2,1,0:T(8,128)(2,1)}, u32[]{:S(2)}, u32[]{:S(2)}) async-start(bf16[8,16,4096]{2,1,0:T(8,128)(2,1)} %bitcast.50), calls=%async_computation.1 | async-start | bytes 2097152 | tf_op jit(solution)/shard_map/all_to_all | solution.py:39
  50.6 14.7 %collective-permute-start.5 = (bf16[64,4096]{1,0:T(8,128)(2,1)}, bf16[64,4096]{1,0:T(8,128)(2,1)}, u32[]{:S(2)}, u32[]{:S(2)}) collective-permute-start(bf16[64,4096]{1,0:T(8,128)(2,1)} %slice.100), channel_id=1, source_target_pairs={{0,12},{4,0},{8,4},{12,8},{1,13},{5,1},{9,5},{13,9},{2,14},{6,2},{... | collective-permute-start | bytes 1572872 | tf_op jit(solution)/shard_map/ppermute | solution.py:21
  51.7 15.6 %collective-permute-start.6 = (bf16[64,4096]{1,0:T(8,128)(2,1)}, bf16[64,4096]{1,0:T(8,128)(2,1)}, u32[]{:S(2)}, u32[]{:S(2)}) collective-permute-start(bf16[64,4096]{1,0:T(8,128)(2,1)} %slice.101), channel_id=1, source_target_pairs={{0,4},{4,8},{8,12},{12,0},{1,5},{5,9},{9,13},{13,1},{2,6},{6,10},{... | collective-permute-start | bytes 1572872 | tf_op jit(solution)/shard_map/ppermute | solution.py:21
  73.0 43.1 %all-to-all-start.2 = ((bf16[8,48,4096]{2,1,0:T(8,128)(2,1)}), bf16[8,48,4096]{2,1,0:T(8,128)(2,1)}, u32[]{:S(2)}, u32[]{:S(2)}) async-start(bf16[8,48,4096]{2,1,0:T(8,128)(2,1)} %bitcast.48), calls=%async_computation.2 | async-start | bytes 6291456 | tf_op jit(solution)/shard_map/all_to_all | solution.py:39
  77.9 8.9 %collective-permute-start = (s32[1,128]{1,0:T(1,128)S(1)}, s32[1,128]{1,0:T(1,128)S(1)}, u32[]{:S(2)}, u32[]{:S(2)}) collective-permute-start(s32[1,128]{1,0:T(1,128)S(1)} %broadcast_in_dim.366), channel_id=1, source_target_pairs={{0,1},{1,2},{2,3},{3,0},{4,5},{5,6},{6,7},{7,4},{8,9},{9,10},{10,1... | collective-permute-start | bytes 1544 | tf_op jit(solution)/shard_map/ppermute | solution.py:21
  79.5 8.7 %collective-permute-start.1 = (s32[1,128]{1,0:T(1,128)S(1)}, s32[1,128]{1,0:T(1,128)S(1)}, u32[]{:S(2)}, u32[]{:S(2)}) collective-permute-start(s32[1,128]{1,0:T(1,128)S(1)} %broadcast_in_dim.371), channel_id=1, source_target_pairs={{0,2},{1,3},{2,0},{3,1},{4,6},{5,7},{6,4},{7,5},{8,10},{9,11},{10,... | collective-permute-start | bytes 1544 | tf_op jit(solution)/shard_map/ppermute | solution.py:21
  82.3 6.8 %collective-permute-start.2 = (s32[1,128]{1,0:T(1,128)S(1)}, s32[1,128]{1,0:T(1,128)S(1)}, u32[]{:S(2)}, u32[]{:S(2)}) collective-permute-start(s32[1,128]{1,0:T(1,128)S(1)} %broadcast_in_dim.376), channel_id=1, source_target_pairs={{0,3},{1,0},{2,1},{3,2},{4,7},{5,4},{6,5},{7,6},{8,11},{9,8},{10,9... | collective-permute-start | bytes 1544 | tf_op jit(solution)/shard_map/ppermute | solution.py:21
  116.1 46.7 %all-to-all-start.4 = ((bf16[8,48,4096]{2,1,0:T(8,128)(2,1)}), bf16[8,48,4096]{2,1,0:T(8,128)(2,1)}, u32[]{:S(2)}, u32[]{:S(2)}) async-start(bf16[8,48,4096]{2,1,0:T(8,128)(2,1)} %bitcast.49), calls=%async_computation.5 | async-start | bytes 6291456 | tf_op jit(solution)/shard_map/all_to_all | solution.py:39
  120.6 109.2 %reduce-scatter.2.cloned.1.call-start = ((), (), s32[]{:S(2)}) async-start(), calls=%async_computation.7 | async-start | bytes 5242880 | tf_op jit(solution)/shard_map/reduce_scatter | solution.py:476
  130.5 5.1 %collective-permute-start.7 = (f32[8,128]{1,0:T(8,128)S(1)}, f32[8,128]{1,0:T(8,128)S(1)}, u32[]{:S(2)}, u32[]{:S(2)}) collective-permute-start(f32[8,128]{1,0:T(8,128)S(1)} %pad_maximum_fusion.1), channel_id=1, source_target_pairs={{0,1},{1,2},{2,3},{3,0},{4,5},{5,6},{6,7},{7,4},{8,9},{9,10},{10,1... | collective-permute-start | bytes 12296 | tf_op jit(solution)/shard_map/ppermute | solution.py:21
  151.3 6.5 %collective-permute-start.10 = (f32[1,64]{1,0:T(1,128)S(1)}, f32[1,64]{1,0:T(1,128)S(1)}, u32[]{:S(2)}, u32[]{:S(2)}) collective-permute-start(f32[1,64]{1,0:T(1,128)S(1)} %bitcast.82), channel_id=1, source_target_pairs={{0,16},{16,0},{32,48},{48,32},{64,80},{80,64},{96,112},{112,96},{1... | collective-permute-start | bytes 776 | tf_op jit(solution)/shard_map/ppermute | solution.py:53
  151.3 8.1 %collective-permute-start.11 = (f32[1,64]{1,0:T(1,128)S(1)}, f32[1,64]{1,0:T(1,128)S(1)}, u32[]{:S(2)}, u32[]{:S(2)}) collective-permute-start(f32[1,64]{1,0:T(1,128)S(1)} %bitcast.81), channel_id=1, source_target_pairs={{0,32},{16,48},{32,64},{48,80},{64,96},{80,112},{96,0},{112,16},{1... | collective-permute-start | bytes 776 | tf_op jit(solution)/shard_map/ppermute | solution.py:53
  153.3 6.4 %collective-permute-start.12 = (f32[1,64]{1,0:T(1,128)S(1)}, f32[1,64]{1,0:T(1,128)S(1)}, u32[]{:S(2)}, u32[]{:S(2)}) collective-permute-start(f32[1,64]{1,0:T(1,128)S(1)} %bitcast.78), channel_id=1, source_target_pairs={{0,48},{16,32},{32,80},{48,64},{64,112},{80,96},{96,16},{112,0},{1... | collective-permute-start | bytes 776 | tf_op jit(solution)/shard_map/ppermute | solution.py:53
  154.5 5.1 %collective-permute-start.13 = (f32[1,64]{1,0:T(1,128)S(1)}, f32[1,64]{1,0:T(1,128)S(1)}, u32[]{:S(2)}, u32[]{:S(2)}) collective-permute-start(f32[1,64]{1,0:T(1,128)S(1)} %bitcast.77), channel_id=1, source_target_pairs={{0,64},{16,80},{32,96},{48,112},{64,0},{80,16},{96,32},{112,48},{1... | collective-permute-start | bytes 776 | tf_op jit(solution)/shard_map/ppermute | solution.py:53
  172.6 15.5 %collective-permute-start.17 = (bf16[64,4096]{1,0:T(8,128)(2,1)}, bf16[64,4096]{1,0:T(8,128)(2,1)S(1)}, u32[]{:S(2)}, u32[]{:S(2)}) collective-permute-start(bf16[64,4096]{1,0:T(8,128)(2,1)} %get-tuple-element.39), channel_id=1, source_target_pairs={{0,4},{4,8},{8,12},{12,0},{1,5},{5,9},{9,13},{13,1},{2,6},{6,10},{... | collective-permute-start | bytes 1572872 | tf_op jit(solution)/shard_map/ppermute | solution.py:21
  173.3 15.6 %collective-permute-start.18 = (bf16[64,4096]{1,0:T(8,128)(2,1)}, bf16[64,4096]{1,0:T(8,128)(2,1)S(1)}, u32[]{:S(2)}, u32[]{:S(2)}) collective-permute-start(bf16[64,4096]{1,0:T(8,128)(2,1)} %get-tuple-element.41), channel_id=1, source_target_pairs={{0,12},{4,0},{8,4},{12,8},{1,13},{5,1},{9,5},{13,9},{2,14},{6,2},{... | collective-permute-start | bytes 1572872 | tf_op jit(solution)/shard_map/ppermute | solution.py:21
  175.9 46.3 %all-to-all-start.3 = ((bf16[8,16,4096]{2,1,0:T(8,128)(2,1)}), bf16[8,16,4096]{2,1,0:T(8,128)(2,1)}, u32[]{:S(2)}, u32[]{:S(2)}) async-start(bf16[8,16,4096]{2,1,0:T(8,128)(2,1)} %bitcast.51), calls=%async_computation.3 | async-start | bytes 2097152 | tf_op jit(solution)/shard_map/all_to_all | solution.py:39
  195.3 39.5 %collective-permute-start.19 = (bf16[128,4096]{1,0:T(8,128)(2,1)}, bf16[128,4096]{1,0:T(8,128)(2,1)}, u32[]{:S(2)}, u32[]{:S(2)}) collective-permute-start(bf16[128,4096]{1,0:T(8,128)(2,1)} %get-tuple-element.42), channel_id=1, source_target_pairs={{0,4},{4,8},{8,12},{12,0},{1,5},{5,9},{9,13},{13,1},{2,6},{6,10},{... | collective-permute-start | bytes 3145736 | tf_op jit(solution)/shard_map/ppermute | solution.py:21
  195.3 39.5 %collective-permute-start.20 = (bf16[128,4096]{1,0:T(8,128)(2,1)}, bf16[128,4096]{1,0:T(8,128)(2,1)}, u32[]{:S(2)}, u32[]{:S(2)}) collective-permute-start(bf16[128,4096]{1,0:T(8,128)(2,1)} %get-tuple-element.43), channel_id=1, source_target_pairs={{0,12},{4,0},{8,4},{12,8},{1,13},{5,1},{9,5},{13,9},{2,14},{6,2},{... | collective-permute-start | bytes 3145736 | tf_op jit(solution)/shard_map/ppermute | solution.py:21
  220.8 8.4 %collective-permute-start.27 = (f32[32,128]{1,0:T(8,128)S(1)}, f32[32,128]{1,0:T(8,128)S(1)}, u32[]{:S(2)}, u32[]{:S(2)}) collective-permute-start(f32[32,128]{1,0:T(8,128)S(1)} %add.379), channel_id=1, source_target_pairs={{0,12},{4,8},{8,4},{12,0},{1,13},{5,9},{9,5},{13,1},{2,14},{6,10},... | collective-permute-start | bytes 49160 | tf_op jit(solution)/shard_map/ppermute | solution.py:34
  (64 other events, 479.8 us)
Sparse Core Ops, SparseCore 0:
  11.2 50.8 all-gather.1
  159.8 43.5 reduce-scatter.1

commit v5 on v4

--- a/solution.py
+++ b/solution.py
@@ -131,14 +131,17 @@
     )(hidden, gain)
 
 
-def finish(hidden, gain, terms):
+def finish(hidden, gain, terms, put=None, arrived=None, scale=1.0):
     rows, width = hidden.shape
     step = rows // 4
+    product = () if put is None else (put, arrived)
 
     def body(hidden_ref, gain_ref, *refs):
         total = refs[0][...].astype(jnp.float32)
-        for ref in refs[1:-1]:
+        for ref in refs[1 : len(terms)]:
             total += ref[...].astype(jnp.float32)
+        if product:
+            total += scale * mxu(refs[-3][...], refs[-2][...])
         values = hidden_ref[...].astype(jnp.float32)
         inverse = inverse_norm(values)
         unit_rows = values * inverse
@@ -147,16 +150,19 @@
         refs[-1][...] = (inverse * (scaled - unit_rows * inner)).astype(jnp.bfloat16)
 
     block = pl.BlockSpec((step, width), lambda i: (i, 0))
+    extra = []
+    if product:
+        extra = [pl.BlockSpec((step, put.shape[1]), lambda i: (i, 0)), whole(arrived.shape)]
     return pl.pallas_call(
         body,
         grid=(rows // step,),
-        in_specs=[block, whole((1, width))] + [block] * len(terms),
+        in_specs=[block, whole((1, width))] + [block] * len(terms) + extra,
         out_specs=block,
         out_shape=jax.ShapeDtypeStruct((rows, width), jnp.bfloat16),
-        compiler_params=params(16),
+        compiler_params=params(20),
         cost_estimate=SMALL,
         name="finish",
-    )(hidden, gain, *terms)
+    )(hidden, gain, *terms, *product)
 
 
 def pick_rows(matrix, sources):
@@ -263,7 +269,7 @@
     slot_count = asked_by.shape[0]
     count = len(sources)
     rows = line // RING
-    cuts = (rows, 3 * rows)
+    cuts = (line,)
 
     def body(near_ref, far_ref, mask_ref, log_ref, weight_ref, target_ref, query_ref, *refs):
         source_refs = refs[:count]
@@ -336,18 +342,20 @@
     )(near, far, asked_by, log_total, weight, target, queries, *sources)
 
 
-def passage_side(coeff, queries, put, arrived, scale, out_type, layout, cost):
+def passage_side(coeff, queries, put, arrived, scale, layout):
     width = queries.shape[1]
     sizes = [sum(high - low for low, high in ranges) for ranges in layout]
-
-    def body(coeff_ref, query_ref, put_ref, arrived_ref, *out_refs):
-        total = mxu(coeff_ref[...], query_ref[...]) + mxu(put_ref[...], arrived_ref[...])
-        total = scale * total
+    own = coeff.shape[0] - put.shape[0]
+
+    def body(coeff_ref, query_ref, put_ref, arrived_ref, own_ref, *out_refs):
+        total = mxu(coeff_ref[own:], query_ref[...]) + mxu(put_ref[...], arrived_ref[...])
+        total = (scale * total).astype(jnp.bfloat16)
         for ranges, out_ref in zip(layout, out_refs):
             at = 0
             for low, high in ranges:
-                out_ref[at : at + high - low] = total[low:high].astype(out_type)
+                out_ref[at : at + high - low] = total[low:high]
                 at += high - low
+        own_ref[...] = scale * mxu(coeff_ref[:own], query_ref[...])
 
     return pl.pallas_call(
         body,
@@ -358,31 +366,39 @@
             whole(put.shape),
             columns(arrived.shape[0], width),
         ],
-        out_specs=[columns(size, width) for size in sizes],
-        out_shape=[jax.ShapeDtypeStruct((size, width), out_type) for size in sizes],
+        out_specs=[columns(own, width)] + [columns(size, width) for size in sizes],
+        out_shape=[jax.ShapeDtypeStruct((own, width), jnp.float32)]
+        + [jax.ShapeDtypeStruct((size, width), jnp.bfloat16) for size in sizes],
         compiler_params=params(20),
-        cost_estimate=cost,
+        cost_estimate=LARGE,
         name="passage_side",
     )(coeff, queries, put, arrived)
 
 
 def add_passing(up, passing_low, down, passing_high):
     half, width = passing_low.shape
+    rows = 2 * half
 
     def body(up_ref, low_ref, down_ref, high_ref, up_out, down_out):
         wide = jnp.float32
-        up_out[...] = (up_ref[...].astype(wide) + low_ref[...].astype(wide)).astype(up.dtype)
-        down_out[...] = (down_ref[...].astype(wide) + high_ref[...].astype(wide)).astype(up.dtype)
-
-    low = pl.BlockSpec((half, tile(width)), lambda i: (0, i))
-    high = pl.BlockSpec((half, tile(width)), lambda i: (1, i))
+        up_out[:half] = (up_ref[:half].astype(wide) + low_ref[...].astype(wide)).astype(up.dtype)
+        up_out[half:] = up_ref[half:]
+        down_out[:half] = down_ref[:half]
+        down_out[half:] = (down_ref[half:].astype(wide) + high_ref[...].astype(wide)).astype(
+            up.dtype
+        )
+
     return pl.pallas_call(
         body,
         grid=(width // tile(width),),
-        in_specs=[low, low, high, low],
-        out_specs=[low, high],
+        in_specs=[
+            columns(rows, width),
+            columns(half, width),
+            columns(rows, width),
+            columns(half, width),
+        ],
+        out_specs=[columns(rows, width)] * 2,
         out_shape=[jax.ShapeDtypeStruct(up.shape, up.dtype)] * 2,
-        input_output_aliases={0: 0, 2: 1},
         compiler_params=params(12),
         cost_estimate=SMALL,
         name="add_passing",
@@ -468,7 +484,7 @@
     target = place[None, :] - first_row
     target = jnp.where((target >= 0) & (target < rows), target, -1)
 
-    part, gain_part, slot_coeff, positive, coeff_own, coeff_far = query_side(
+    part, gain_part, slot_coeff, positive, coeff = query_side(
         near, far, asked_by, log_total, weight, target, q_line,
         [p_own, *p_mid, *p_opp, hard_own, hard_far], line, scale,
     )
@@ -493,26 +509,26 @@
     put_far = put_rows(asked_far, got_coeff[:, first:], 3 * rows)
     half = rows // 2
     low_1, high_1, low_3, high_3, low_2, high_2 = [(i * half, (i + 1) * half) for i in range(6)]
-    for_above, for_below, pass_up, pass_down = passage_side(
-        coeff_far, q_line, put_far, far_queries, scale, jnp.bfloat16,
-        [[low_1, high_1], [low_3, high_3], [low_2], [high_2]], LARGE,
-    )
-    for_above, for_below = add_passing(
-        for_above, shift(pass_up, "y", 1), for_below, shift(pass_down, "y", -1)
-    )
+    own_part, for_above, for_below, pass_up, pass_down = passage_side(
+        coeff, q_line, put_far, far_queries, scale,
+        [[low_1, high_1], [low_3, high_3], [low_2], [high_2]],
+    )
+    passing_low = shift(pass_up, "y", 1)
+    passing_high = shift(pass_down, "y", -1)
+    gain_part = pair_sum(pair_sum(gain_part.reshape(-1, 128), "z", False), "z", True)
+    gain_part, passing_low = lax.optimization_barrier((gain_part, passing_low))
+    for_above, for_below = add_passing(for_above, passing_low, for_below, passing_high)
     from_below = shift(for_above, "y", 1)
     from_above = shift(for_below, "y", -1)
-    gain_part, _ = lax.optimization_barrier((gain_part.reshape(-1, 128), for_above))
+    gain_part, _ = lax.optimization_barrier((gain_part, for_above))
     gain_part = pair_sum(gain_part, "c", False)
-    for axis in ("x", "z", "y"):
-        gain_part = pair_sum(pair_sum(gain_part, axis, False), axis, True)
+    gain_part = pair_sum(pair_sum(gain_part, "x", False), "x", True)
+    gain_part, query_grad = lax.optimization_barrier((gain_part, query_grad))
+    gain_part = pair_sum(pair_sum(gain_part, "y", False), "y", True)
     gain_grad = 2.0 * gain_part.reshape(-1) / norm_gain
-
-    own_part = passage_side(
-        coeff_own, q_line, put_own, own_queries, scale, jnp.float32, [[(0, rows)]], SMALL
-    )[0]
-    own_part, query_grad = lax.optimization_barrier((own_part, query_grad))
-    passage_grad = finish(passage_hidden, gain, [own_part, from_below, from_above])
+    passage_grad = finish(
+        passage_hidden, gain, [own_part, from_below, from_above], put_own, own_queries, scale
+    )
     return (loss_rows, query_grad, passage_grad, gain_grad)
 
 

time: 248 us -> 235 us (0.948)
  waiting for transfers between devices: 69.1 us -> 64.2 us
  local copies, waits for them, and re-layouts: 40.3 us -> 35.5 us
  Pallas kernels: 51 us -> 46.4 us
    unnamed x107 -> x93, local copies, waits for them, and re-layouts: 34.6 us -> 29.7 us
    ppermute x14, waiting for transfers between devices: 33.3 us -> 28.7 us  [shift(): lax.ppermute(value, axis, [(i, (i + step) % RING) for i in range(RING)])]
    pallas_call x2 -> x1, Pallas kernels: 9.82 us -> 6.2 us  [passage_side(): pl.pallas_call(body, grid=(width // tile(width),), in_specs=[whole(coeff....]
  transfers between devices with their start and end apart: 35 -> 35, of which waited for: 17 -> 17; matrix products, arithmetic and copies ran while one was open for 6% -> 6% of each run, Pallas kernels for 18% -> 19%
where the time goes in v5:
time: 235 us; the launch traced here: 233 us
  waiting for transfers between devices  64.2 us (27%)
  starting transfers between devices  63.9 us (27%)
  Pallas kernels  46.4 us (20%)
  local copies, waits for them, and re-layouts  35.5 us (15%)
  between operations  14.8 us (6%)
  other arithmetic  8.59 us (4%)
    unnamed x93, local copies, waits for them, and re-layouts  29.7 us
    ppermute x14, waiting for transfers between devices, shift(): lax.ppermute(value, axis, [(i, (i + step) % RING) for i in range(RING)])  28.7 us
    ppermute x14, starting transfers between devices, shift(): lax.ppermute(value, axis, [(i, (i + step) % RING) for i in range(RING)])  22.5 us
    all_to_all x4, starting transfers between devices, group_rows(): return lax.all_to_all(blocks, GROUPS, 0, 0, tiled=True).reshape(rows.shape)  18.6 us
    ppermute x7, waiting for transfers between devices, pair_sum(): return value + lax.ppermute(value, axis, pairs)  17.2 us
    pallas_call x4, Pallas kernels, pick_rows(): pl.pallas_call(body, grid=(width // tile(width),), in_specs=[whole(matrix...  9.41 us
    ppermute x7, starting transfers between devices, group_table(): lax.ppermute(row, GROUPS, [(z * 2 + c, (z + z_step) % z_count * 2 + (c ^...  8.34 us
    pallas_call x1, Pallas kernels, query_side(): pl.pallas_call(body, grid=(width // tile(width),), in_specs=[whole(near.s...  8.33 us
  transfers between devices with their start and end apart: 35, of which 17 were waited for; matrix products, arithmetic and copies ran while one was open for 6% of the time, Pallas kernels for 19%

profile of v5, /device:TPU:0, one launch (start us, length us, event | category | flops | bytes accessed | tf_op | source)
XLA Modules:
  0.0 233.4 jit_solution(14128492382166793456)
XLA Ops:
  13.1 3.2 %collective-permute-start.3 = (bf16[128,4096]{1,0:T(8,128)(2,1)S(1)}, bf16[128,4096]{1,0:T(8,128)(2,1)S(1)}, u32[]{:S(2)}, u32[]{:S(2)}) collective-permute-start(bf16[128,4096]{1,0:T(8,128)(2,1)S(1)} %embed.3.refs_0_), channel_id=1, source_target_pairs={{0,12},{4,0},{8,4},{12,8},{1,13},{5,1},{9,5},{13,9},{2,14},{6,2},{... | collective-permute-start | bytes 3145736 | tf_op jit(solution)/shard_map/ppermute | solution.py:21
  17.7 8.2 %all-to-all-start = ((s32[32,1,16]{2,1,0:T(1,128)}), s32[32,1,16]{2,1,0:T(1,128)S(1)}, u32[]{:S(2)}, u32[]{:S(2)}) async-start(s32[32,1,16]{2,1,0:T(1,128)} %bitcast.4), calls=%async_computation | async-start | bytes 32768 | tf_op jit(solution)/shard_map/all_to_all | solution.py:435
  25.9 7.2 %all-to-all-done = s32[32,1,16]{2,1,0:T(1,128)S(1)} async-done(((s32[32,1,16]{2,1,0:T(1,128)}), s32[32,1,16]{2,1,0:T(1,128)S(1)}, u32[]{:S(2)}, u32[]{:S(2)}) %all-to-all-start) | async-done | bytes 2080 | tf_op jit(solution)/shard_map/all_to_all | solution.py:435
  33.3 5.4 %collective-permute-done.3.refs_1_.refs_0_ = bf16[128,4096]{1,0:T(8,128)(2,1)S(1)} collective-permute-done((bf16[128,4096]{1,0:T(8,128)(2,1)S(1)}, bf16[128,4096]{1,0:T(8,128)(2,1)S(1)}, u32[]{:S(2)}, u32[]{:S(2)}) %collective-permute-start.3) | collective-permute-done | bytes 1048608 | tf_op jit(solution)/shard_map/ppermute | solution.py:21
  38.7 3.4 %collective-permute-done.4.refs_2_.refs_1_ = bf16[128,4096]{1,0:T(8,128)(2,1)S(1)} collective-permute-done((bf16[128,4096]{1,0:T(8,128)(2,1)S(1)}, bf16[128,4096]{1,0:T(8,128)(2,1)S(1)}, u32[]{:S(2)}, u32[]{:S(2)}) %collective-permute-start.4) | collective-permute-done | bytes 1048608 | tf_op jit(solution)/shard_map/ppermute | solution.py:21
  44.5 5.3 %all-to-all-start.1 = ((bf16[8,16,4096]{2,1,0:T(8,128)(2,1)}), bf16[8,16,4096]{2,1,0:T(8,128)(2,1)}, u32[]{:S(2)}, u32[]{:S(2)}) async-start(bf16[8,16,4096]{2,1,0:T(8,128)(2,1)} %bitcast.50), calls=%async_computation.1 | async-start | bytes 2097152 | tf_op jit(solution)/shard_map/all_to_all | solution.py:39
  54.0 11.2 %collective-permute-done.5.refs_3_.refs_2_ = bf16[64,4096]{1,0:T(8,128)(2,1)} collective-permute-done((bf16[64,4096]{1,0:T(8,128)(2,1)}, bf16[64,4096]{1,0:T(8,128)(2,1)}, u32[]{:S(2)}, u32[]{:S(2)}) %collective-permute-start.5) | collective-permute-done | bytes 524320 | tf_op jit(solution)/shard_map/ppermute | solution.py:21
  67.3 4.0 %pick_rows.7 = bf16[384,4096]{1,0:T(8,128)(2,1)S(1)} custom-call(bf16[384,384]{1,0:T(8,128)(2,1)S(1)} %compare_convert_fusion.matrix_ref, bf16[128,4096]{1,0:T(8,128)(2,1)S(1)} %collective-permute-done.3.refs_1_.refs_0_, bf16[128,4096]{1,0:T(8,128)(2,1)S(1)} %collective-permute-done.4.refs_2_.refs_1_, ...), custom_call_target="tpu_custom_call" | custom-call | flops 1 | bytes 1 | tf_op jit(solution)/shard_map/pick_rows/pallas_call | solution.py:174
  73.0 4.6 %all-to-all-start.2 = ((bf16[8,48,4096]{2,1,0:T(8,128)(2,1)}), bf16[8,48,4096]{2,1,0:T(8,128)(2,1)}, u32[]{:S(2)}, u32[]{:S(2)}) async-start(bf16[8,48,4096]{2,1,0:T(8,128)(2,1)} %bitcast.48), calls=%async_computation.2 | async-start | bytes 6291456 | tf_op jit(solution)/shard_map/all_to_all | solution.py:39
  101.5 5.4 %line_scores.1.near_ref = f32[640,512]{1,0:T(8,128)S(1)} custom-call(bf16[512,4096]{1,0:T(8,128)(2,1)S(1)} %copy-done.1, bf16[128,4096]{1,0:T(8,128)(2,1)S(1)} %embed.3.refs_0_, bf16[128,4096]{1,0:T(8,128)(2,1)S(1)} %collective-permute-done.3.refs_1_.refs_0_, bf16[128,4096]{1,0:T(8,128)(2,1)S(1)} %collective-permute-done.4.refs_2_.refs_1_, ...), custom_call_target="tpu_custom_call" | custom-call | flops 1 | bytes 1 | tf_op jit(solution)/shard_map/line_scores/pallas_call | solution.py:201
  107.9 8.2 %all-to-all-done.2 = bf16[8,48,4096]{2,1,0:T(8,128)(2,1)} async-done(((bf16[8,48,4096]{2,1,0:T(8,128)(2,1)}), bf16[8,48,4096]{2,1,0:T(8,128)(2,1)}, u32[]{:S(2)}, u32[]{:S(2)}) %all-to-all-start.2) | async-done | bytes 3145760 | tf_op jit(solution)/shard_map/all_to_all | solution.py:39
  116.1 4.4 %all-to-all-start.3 = ((bf16[8,48,4096]{2,1,0:T(8,128)(2,1)}), bf16[8,48,4096]{2,1,0:T(8,128)(2,1)}, u32[]{:S(2)}, u32[]{:S(2)}) async-start(bf16[8,48,4096]{2,1,0:T(8,128)(2,1)} %bitcast.49), calls=%async_computation.3 | async-start | bytes 6291456 | tf_op jit(solution)/shard_map/all_to_all | solution.py:39
  125.2 5.3 %far_scores.1 = (f32[384,512]{1,0:T(8,128)S(1)}, f32[1,512]{1,0:T(1,128)S(1)}) custom-call(f32[640,512]{1,0:T(8,128)S(1)} %copy-done.8, bf16[512,512]{1,0:T(8,128)(2,1)S(1)} %copy-done.19, bf16[512,4096]{1,0:T(8,128)(2,1)S(1)} %copy-done.2, bf16[384,4096]{1,0:T(8,128)(2,1)} %bitcast.9.refs_0_.refs_6_), custom_call_target="tpu_custom_call" | custom-call | flops 99999997952 | bytes 100000000 | tf_op jit(solution)/shard_map/far_scores/pallas_call | solution.py:245
  135.7 3.3 %collective-permute-done.9 = f32[8,128]{1,0:T(8,128)S(1)} collective-permute-done((f32[8,128]{1,0:T(8,128)S(1)}, f32[8,128]{1,0:T(8,128)S(1)}, u32[]{:S(2)}, u32[]{:S(2)}) %collective-permute-start.9) | collective-permute-done | bytes 4128 | tf_op jit(solution)/shard_map/ppermute | solution.py:21
  139.1 8.3 %query_side.1 = (bf16[512,4096]{1,0:T(8,128)(2,1)S(1)}, f32[1,4096]{1,0:T(1,128)S(1)}, f32[8,512]{1,0:T(8,128)S(1)}, f32[1,512]{1,0:T(1,128)S(1)}, bf16[512,512]{1,0:T(8,128)(2,1)S(1)}) custom-call(f32[640,512]{1,0:T(8,128)S(1)} %copy-done.9, f32[384,512]{1,0:T(8,128)S(1)} %get-tuple-element.30.far_ref, bf16[512,512]{1,0:T(8,128)(2,1)S(1)} %copy-done.20, ...), custom_call_target="tpu_custom_call" | custom-call | flops 1 | bytes 1 | tf_op jit(solution)/shard_map/query_side/pallas_call | solution.py:311
  165.6 6.2 %passage_side.1 = (f32[128,4096]{1,0:T(8,128)S(1)}, bf16[128,4096]{1,0:T(8,128)(2,1)S(1)}, bf16[128,4096]{1,0:T(8,128)(2,1)S(1)}, bf16[64,4096]{1,0:T(8,128)(2,1)S(1)}, bf16[64,4096]{1,0:T(8,128)(2,1)S(1)}) custom-call(bf16[512,512]{1,0:T(8,128)(2,1)S(1)} %copy-done.27, bf16[512,4096]{1,0:T(8,128)(2,1)S(1)} %copy-done.4, ...), custom_call_target="tpu_custom_call" | custom-call | flops 99999997952 | bytes 100000000 | tf_op jit(solution)/shard_map/passage_side/pallas_call | solution.py:360
  176.7 3.4 %collective-permute-done.10 = f32[32,128]{1,0:T(8,128)S(1)} collective-permute-done((f32[32,128]{1,0:T(8,128)S(1)}, f32[32,128]{1,0:T(8,128)S(1)}, u32[]{:S(2)}, u32[]{:S(2)}) %collective-permute-start.10) | collective-permute-done | bytes 16416 | tf_op jit(solution)/shard_map/ppermute | solution.py:34
  185.1 3.3 %collective-permute-done.19.low_ref = bf16[64,4096]{1,0:T(8,128)(2,1)S(1)} collective-permute-done((bf16[64,4096]{1,0:T(8,128)(2,1)S(1)}, bf16[64,4096]{1,0:T(8,128)(2,1)S(1)}, u32[]{:S(2)}, u32[]{:S(2)}) %collective-permute-start.19) | collective-permute-done | bytes 524320 | tf_op jit(solution)/shard_map/ppermute | solution.py:21
  190.2 3.2 %collective-permute-start.25 = (bf16[128,4096]{1,0:T(8,128)(2,1)}, bf16[128,4096]{1,0:T(8,128)(2,1)}, u32[]{:S(2)}, u32[]{:S(2)}) collective-permute-start(bf16[128,4096]{1,0:T(8,128)(2,1)} %get-tuple-element.47), channel_id=1, source_target_pairs={{0,12},{4,0},{8,4},{12,8},{1,13},{5,1},{9,5},{13,9},{2,14},{6,2},{... | collective-permute-start | bytes 3145736 | tf_op jit(solution)/shard_map/ppermute | solution.py:21
  193.5 4.2 %all-to-all-start.4 = ((bf16[8,16,4096]{2,1,0:T(8,128)(2,1)}), bf16[8,16,4096]{2,1,0:T(8,128)(2,1)}, u32[]{:S(2)}, u32[]{:S(2)}) async-start(bf16[8,16,4096]{2,1,0:T(8,128)(2,1)} %bitcast.51), calls=%async_computation.5 | async-start | bytes 2097152 | tf_op jit(solution)/shard_map/all_to_all | solution.py:39
  199.3 3.4 %collective-permute-done.22 = f32[32,128]{1,0:T(8,128)S(1)} collective-permute-done((f32[32,128]{1,0:T(8,128)S(1)}, f32[32,128]{1,0:T(8,128)S(1)}, u32[]{:S(2)}, u32[]{:S(2)}) %collective-permute-start.22) | collective-permute-done | bytes 16416 | tf_op jit(solution)/shard_map/ppermute | solution.py:34
  204.3 3.3 %collective-permute-done.23 = f32[32,128]{1,0:T(8,128)S(1)} collective-permute-done((f32[32,128]{1,0:T(8,128)S(1)}, f32[32,128]{1,0:T(8,128)S(1)}, u32[]{:S(2)}, u32[]{:S(2)}) %collective-permute-start.23) | collective-permute-done | bytes 16416 | tf_op jit(solution)/shard_map/ppermute | solution.py:34
  213.2 3.1 %collective-permute-done.26 = f32[32,128]{1,0:T(8,128)S(1)} collective-permute-done((f32[32,128]{1,0:T(8,128)S(1)}, f32[32,128]{1,0:T(8,128)S(1)}, u32[]{:S(2)}, u32[]{:S(2)}) %collective-permute-start.26) | collective-permute-done | bytes 16416 | tf_op jit(solution)/shard_map/ppermute | solution.py:34
  221.0 4.9 %finish.3 = bf16[128,4096]{1,0:T(8,128)(2,1)} custom-call(bf16[128,4096]{1,0:T(8,128)(2,1)S(1)} %copy-done.13, f32[1,4096]{1,0:T(1,128)S(1)} %bitcast.55, f32[128,4096]{1,0:T(8,128)S(1)} %copy-done.18, bf16[128,4096]{1,0:T(8,128)(2,1)} %collective-permute-done.24.refs_1_, bf16[128,4096]{1,0:T(8,128)(2,1)} %collective-permute-done.25.refs_2_, ...), custom_call_target="tpu_custom_call" | custom-call | flops 1 | bytes 1 | tf_op jit(solution)/shard_map/finish/pallas_call | solution.py:156
  (233 shorter events, 96.3 us)
Async XLA Ops:
  7.2 85.1 %all-gather.2.cloned.1.call-start = ((), (), s32[]{:S(2)}) async-start(), calls=%async_computation.6 | async-start | bytes 5242880 | tf_op jit(solution)/shard_map/all_gather | solution.py:455
  13.1 25.6 %collective-permute-start.3 = (bf16[128,4096]{1,0:T(8,128)(2,1)S(1)}, bf16[128,4096]{1,0:T(8,128)(2,1)S(1)}, u32[]{:S(2)}, u32[]{:S(2)}) collective-permute-start(bf16[128,4096]{1,0:T(8,128)(2,1)S(1)} %embed.3.refs_0_), channel_id=1, source_target_pairs={{0,12},{4,0},{8,4},{12,8},{1,13},{5,1},{9,5},{13,9},{2,14},{6,2},{... | collective-permute-start | bytes 3145736 | tf_op jit(solution)/shard_map/ppermute | solution.py:21
  16.2 25.8 %collective-permute-start.4 = (bf16[128,4096]{1,0:T(8,128)(2,1)S(1)}, bf16[128,4096]{1,0:T(8,128)(2,1)S(1)}, u32[]{:S(2)}, u32[]{:S(2)}) collective-permute-start(bf16[128,4096]{1,0:T(8,128)(2,1)S(1)} %embed.3.refs_0_), channel_id=1, source_target_pairs={{0,4},{4,8},{8,12},{12,0},{1,5},{5,9},{9,13},{13,1},{2,6},{6,10},{... | collective-permute-start | bytes 3145736 | tf_op jit(solution)/shard_map/ppermute | solution.py:21
  17.7 15.4 %all-to-all-start = ((s32[32,1,16]{2,1,0:T(1,128)}), s32[32,1,16]{2,1,0:T(1,128)S(1)}, u32[]{:S(2)}, u32[]{:S(2)}) async-start(s32[32,1,16]{2,1,0:T(1,128)} %bitcast.4), calls=%async_computation | async-start | bytes 32768 | tf_op jit(solution)/shard_map/all_to_all | solution.py:435
  44.5 28.5 %all-to-all-start.1 = ((bf16[8,16,4096]{2,1,0:T(8,128)(2,1)}), bf16[8,16,4096]{2,1,0:T(8,128)(2,1)}, u32[]{:S(2)}, u32[]{:S(2)}) async-start(bf16[8,16,4096]{2,1,0:T(8,128)(2,1)} %bitcast.50), calls=%async_computation.1 | async-start | bytes 2097152 | tf_op jit(solution)/shard_map/all_to_all | solution.py:39
  50.6 14.7 %collective-permute-start.5 = (bf16[64,4096]{1,0:T(8,128)(2,1)}, bf16[64,4096]{1,0:T(8,128)(2,1)}, u32[]{:S(2)}, u32[]{:S(2)}) collective-permute-start(bf16[64,4096]{1,0:T(8,128)(2,1)} %slice.100), channel_id=1, source_target_pairs={{0,12},{4,0},{8,4},{12,8},{1,13},{5,1},{9,5},{13,9},{2,14},{6,2},{... | collective-permute-start | bytes 1572872 | tf_op jit(solution)/shard_map/ppermute | solution.py:21
  51.8 15.6 %collective-permute-start.6 = (bf16[64,4096]{1,0:T(8,128)(2,1)}, bf16[64,4096]{1,0:T(8,128)(2,1)}, u32[]{:S(2)}, u32[]{:S(2)}) collective-permute-start(bf16[64,4096]{1,0:T(8,128)(2,1)} %slice.101), channel_id=1, source_target_pairs={{0,4},{4,8},{8,12},{12,0},{1,5},{5,9},{9,13},{13,1},{2,6},{6,10},{... | collective-permute-start | bytes 1572872 | tf_op jit(solution)/shard_map/ppermute | solution.py:21
  73.0 43.1 %all-to-all-start.2 = ((bf16[8,48,4096]{2,1,0:T(8,128)(2,1)}), bf16[8,48,4096]{2,1,0:T(8,128)(2,1)}, u32[]{:S(2)}, u32[]{:S(2)}) async-start(bf16[8,48,4096]{2,1,0:T(8,128)(2,1)} %bitcast.48), calls=%async_computation.2 | async-start | bytes 6291456 | tf_op jit(solution)/shard_map/all_to_all | solution.py:39
  77.9 8.9 %collective-permute-start = (s32[1,128]{1,0:T(1,128)S(1)}, s32[1,128]{1,0:T(1,128)S(1)}, u32[]{:S(2)}, u32[]{:S(2)}) collective-permute-start(s32[1,128]{1,0:T(1,128)S(1)} %broadcast_in_dim.366), channel_id=1, source_target_pairs={{0,1},{1,2},{2,3},{3,0},{4,5},{5,6},{6,7},{7,4},{8,9},{9,10},{10,1... | collective-permute-start | bytes 1544 | tf_op jit(solution)/shard_map/ppermute | solution.py:21
  79.5 8.7 %collective-permute-start.1 = (s32[1,128]{1,0:T(1,128)S(1)}, s32[1,128]{1,0:T(1,128)S(1)}, u32[]{:S(2)}, u32[]{:S(2)}) collective-permute-start(s32[1,128]{1,0:T(1,128)S(1)} %broadcast_in_dim.371), channel_id=1, source_target_pairs={{0,2},{1,3},{2,0},{3,1},{4,6},{5,7},{6,4},{7,5},{8,10},{9,11},{10,... | collective-permute-start | bytes 1544 | tf_op jit(solution)/shard_map/ppermute | solution.py:21
  82.3 6.8 %collective-permute-start.2 = (s32[1,128]{1,0:T(1,128)S(1)}, s32[1,128]{1,0:T(1,128)S(1)}, u32[]{:S(2)}, u32[]{:S(2)}) collective-permute-start(s32[1,128]{1,0:T(1,128)S(1)} %broadcast_in_dim.376), channel_id=1, source_target_pairs={{0,3},{1,0},{2,1},{3,2},{4,7},{5,4},{6,5},{7,6},{8,11},{9,8},{10,9... | collective-permute-start | bytes 1544 | tf_op jit(solution)/shard_map/ppermute | solution.py:21
  116.1 46.1 %all-to-all-start.3 = ((bf16[8,48,4096]{2,1,0:T(8,128)(2,1)}), bf16[8,48,4096]{2,1,0:T(8,128)(2,1)}, u32[]{:S(2)}, u32[]{:S(2)}) async-start(bf16[8,48,4096]{2,1,0:T(8,128)(2,1)} %bitcast.49), calls=%async_computation.3 | async-start | bytes 6291456 | tf_op jit(solution)/shard_map/all_to_all | solution.py:39
  120.6 87.1 %reduce-scatter.2.cloned.1.call-start = ((), (), s32[]{:S(2)}) async-start(), calls=%async_computation.7 | async-start | bytes 5242880 | tf_op jit(solution)/shard_map/reduce_scatter | solution.py:492
  130.5 5.1 %collective-permute-start.7 = (f32[8,128]{1,0:T(8,128)S(1)}, f32[8,128]{1,0:T(8,128)S(1)}, u32[]{:S(2)}, u32[]{:S(2)}) collective-permute-start(f32[8,128]{1,0:T(8,128)S(1)} %pad_maximum_fusion.1), channel_id=1, source_target_pairs={{0,1},{1,2},{2,3},{3,0},{4,5},{5,6},{6,7},{7,4},{8,9},{9,10},{10,1... | collective-permute-start | bytes 12296 | tf_op jit(solution)/shard_map/ppermute | solution.py:21
  150.6 6.5 %collective-permute-start.12 = (f32[1,64]{1,0:T(1,128)S(1)}, f32[1,64]{1,0:T(1,128)S(1)}, u32[]{:S(2)}, u32[]{:S(2)}) collective-permute-start(f32[1,64]{1,0:T(1,128)S(1)} %bitcast.82), channel_id=1, source_target_pairs={{0,16},{16,0},{32,48},{48,32},{64,80},{80,64},{96,112},{112,96},{1... | collective-permute-start | bytes 776 | tf_op jit(solution)/shard_map/ppermute | solution.py:53
  150.7 8.1 %collective-permute-start.13 = (f32[1,64]{1,0:T(1,128)S(1)}, f32[1,64]{1,0:T(1,128)S(1)}, u32[]{:S(2)}, u32[]{:S(2)}) collective-permute-start(f32[1,64]{1,0:T(1,128)S(1)} %bitcast.81), channel_id=1, source_target_pairs={{0,32},{16,48},{32,64},{48,80},{64,96},{80,112},{96,0},{112,16},{1... | collective-permute-start | bytes 776 | tf_op jit(solution)/shard_map/ppermute | solution.py:53
  152.7 6.4 %collective-permute-start.14 = (f32[1,64]{1,0:T(1,128)S(1)}, f32[1,64]{1,0:T(1,128)S(1)}, u32[]{:S(2)}, u32[]{:S(2)}) collective-permute-start(f32[1,64]{1,0:T(1,128)S(1)} %bitcast.78), channel_id=1, source_target_pairs={{0,48},{16,32},{32,80},{48,64},{64,112},{80,96},{96,16},{112,0},{1... | collective-permute-start | bytes 776 | tf_op jit(solution)/shard_map/ppermute | solution.py:53
  153.9 5.1 %collective-permute-start.15 = (f32[1,64]{1,0:T(1,128)S(1)}, f32[1,64]{1,0:T(1,128)S(1)}, u32[]{:S(2)}, u32[]{:S(2)}) collective-permute-start(f32[1,64]{1,0:T(1,128)S(1)} %bitcast.77), channel_id=1, source_target_pairs={{0,64},{16,80},{32,96},{48,112},{64,0},{80,16},{96,32},{112,48},{1... | collective-permute-start | bytes 776 | tf_op jit(solution)/shard_map/ppermute | solution.py:53
  173.2 15.2 %collective-permute-start.19 = (bf16[64,4096]{1,0:T(8,128)(2,1)S(1)}, bf16[64,4096]{1,0:T(8,128)(2,1)S(1)}, u32[]{:S(2)}, u32[]{:S(2)}) collective-permute-start(bf16[64,4096]{1,0:T(8,128)(2,1)S(1)} %get-tuple-element.36), channel_id=1, source_target_pairs={{0,4},{4,8},{8,12},{12,0},{1,5},{5,9},{9,13},{13,1},{2,6},{6,10},{... | collective-permute-start | bytes 1572872 | tf_op jit(solution)/shard_map/ppermute | solution.py:21
  173.7 14.6 %collective-permute-start.20 = (bf16[64,4096]{1,0:T(8,128)(2,1)S(1)}, bf16[64,4096]{1,0:T(8,128)(2,1)S(1)}, u32[]{:S(2)}, u32[]{:S(2)}) collective-permute-start(bf16[64,4096]{1,0:T(8,128)(2,1)S(1)} %get-tuple-element.41), channel_id=1, source_target_pairs={{0,12},{4,0},{8,4},{12,8},{1,13},{5,1},{9,5},{13,9},{2,14},{6,2},{... | collective-permute-start | bytes 1572872 | tf_op jit(solution)/shard_map/ppermute | solution.py:21
  190.2 28.0 %collective-permute-start.24 = (bf16[128,4096]{1,0:T(8,128)(2,1)S(1)}, bf16[128,4096]{1,0:T(8,128)(2,1)}, u32[]{:S(2)}, u32[]{:S(2)}) collective-permute-start(bf16[128,4096]{1,0:T(8,128)(2,1)S(1)} %get-tuple-element.42), channel_id=1, source_target_pairs={{0,4},{4,8},{8,12},{12,0},{1,5},{5,9},{9,13},{13,1},{2,6},{6,10},{... | collective-permute-start | bytes 3145736 | tf_op jit(solution)/shard_map/ppermute | solution.py:21
  190.2 28.0 %collective-permute-start.25 = (bf16[128,4096]{1,0:T(8,128)(2,1)}, bf16[128,4096]{1,0:T(8,128)(2,1)}, u32[]{:S(2)}, u32[]{:S(2)}) collective-permute-start(bf16[128,4096]{1,0:T(8,128)(2,1)} %get-tuple-element.47), channel_id=1, source_target_pairs={{0,12},{4,0},{8,4},{12,8},{1,13},{5,1},{9,5},{13,9},{2,14},{6,2},{... | collective-permute-start | bytes 3145736 | tf_op jit(solution)/shard_map/ppermute | solution.py:21
  193.5 24.7 %all-to-all-start.4 = ((bf16[8,16,4096]{2,1,0:T(8,128)(2,1)}), bf16[8,16,4096]{2,1,0:T(8,128)(2,1)}, u32[]{:S(2)}, u32[]{:S(2)}) async-start(bf16[8,16,4096]{2,1,0:T(8,128)(2,1)} %bitcast.51), calls=%async_computation.5 | async-start | bytes 2097152 | tf_op jit(solution)/shard_map/all_to_all | solution.py:39
  216.4 9.6 %collective-permute-start.27 = (f32[32,128]{1,0:T(8,128)S(1)}, f32[32,128]{1,0:T(8,128)S(1)}, u32[]{:S(2)}, u32[]{:S(2)}) collective-permute-start(f32[32,128]{1,0:T(8,128)S(1)} %add.379), channel_id=1, source_target_pairs={{0,12},{4,8},{8,4},{12,0},{1,13},{5,9},{9,5},{13,1},{2,14},{6,10},... | collective-permute-start | bytes 49160 | tf_op jit(solution)/shard_map/ppermute | solution.py:34
  (57 other events, 404.7 us)
Sparse Core Ops, SparseCore 0:
  11.2 50.8 all-gather.1
  159.1 43.5 reduce-scatter.1

commit v6 on v5

--- a/solution.py
+++ b/solution.py
@@ -21,11 +21,12 @@
     return lax.ppermute(value, axis, [(i, (i + step) % RING) for i in range(RING)])
 
 
-def ring_gather(block, axis):
-    half = block.shape[0] // 2
-    up = shift(block, axis, -1)
-    down = shift(block, axis, 1)
-    return [up, down], [shift(up[:half], axis, -1), shift(down[half:], axis, 1)]
+def ring_gather(low, high, axis):
+    up_low = shift(low, axis, -1)
+    down_high = shift(high, axis, 1)
+    up_more = shift(jnp.concatenate([high, up_low], axis=0), axis, -1)
+    down_more = shift(jnp.concatenate([low, down_high], axis=0), axis, 1)
+    return [up_low, up_more, down_more, down_high]
 
 
 def pair_sum(value, axis, turn):
@@ -110,21 +111,33 @@
     return lax.rsqrt(jnp.mean(values * values, axis=-1, keepdims=True) + EPSILON)
 
 
-def embed(hidden, gain):
-    def body(hidden_ref, gain_ref, out_ref):
+def embed(hidden, gain, pieces):
+    def body(hidden_ref, gain_ref, *out_refs):
         values = hidden_ref[...].astype(jnp.float32)
         unit_rows = values * inverse_norm(values)
-        out_ref[...] = (unit_rows * gain_ref[...]).astype(jnp.bfloat16)
+        rounded_rows = (unit_rows * gain_ref[...]).astype(jnp.bfloat16)
+        for i, out_ref in enumerate(out_refs):
+
+            @pl.when(pl.program_id(0) // per_piece == i)
+            def _(out_ref=out_ref):
+                out_ref[...] = rounded_rows
 
     rows, width = hidden.shape
-    step = rows // 4
+    step = min(32, rows // pieces)
+    per_piece = rows // pieces // step
     block = pl.BlockSpec((step, width), lambda i: (i, 0))
+
+    def piece(at):
+        return pl.BlockSpec(
+            (step, width), lambda i: (jnp.clip(i - at * per_piece, 0, per_piece - 1), 0)
+        )
+
     return pl.pallas_call(
         body,
         grid=(rows // step,),
         in_specs=[block, whole((1, width))],
-        out_specs=block,
-        out_shape=jax.ShapeDtypeStruct((rows, width), jnp.bfloat16),
+        out_specs=[piece(at) for at in range(pieces)],
+        out_shape=[jax.ShapeDtypeStruct((rows // pieces, width), jnp.bfloat16)] * pieces,
         compiler_params=params(12),
         cost_estimate=SMALL,
         name="embed",
@@ -415,8 +428,8 @@
     y_place, x_place = lax.axis_index("y"), lax.axis_index("x")
 
     gain = norm_gain.reshape(1, width)
-    p_own = embed(passage_hidden, gain)
-    p_mid, p_opp = ring_gather(p_own, "y")
+    p_own = embed(passage_hidden, gain, 2)
+    p_far = ring_gather(*p_own, "y")
 
     flat_ids = hneg_ids.reshape(-1)
     id_count = rows * neg_count
@@ -437,21 +450,26 @@
     )
     asked = asked.reshape(group_count, RING, RING, CAP).transpose(0, 2, 1, 3)
     place = jnp.arange(line, dtype=jnp.int32)
-    asked, _ = lax.optimization_barrier((asked, p_mid))
+    asked, _ = lax.optimization_barrier((asked, [p_far[0], p_far[-1]]))
     asked_own = asked[:, 0].reshape(-1)
-    above = jnp.where(asked[:, 3:] < 0, -1, asked[:, 3:] + rows)
-    opposite = jnp.where(asked[:, 2:3] < 0, -1, asked[:, 2:3] + 2 * rows)
-    asked_far = jnp.concatenate([asked[:, 1:2], above, opposite], axis=1).reshape(-1)
+    half = rows // 2
+
+    def moved(block, base):
+        return jnp.where(block < 0, -1, block + base + jnp.where(block >= half, half, 0))
+
+    asked_far = jnp.concatenate(
+        [asked[:, 1:2], moved(asked[:, 3:], rows + half), moved(asked[:, 2:3], rows)], axis=1
+    ).reshape(-1)
 
     def one_hot(numbers, size):
         return (numbers[:, None] == place[None, :size]).astype(jnp.bfloat16)
 
-    chosen_own = pick_rows(one_hot(asked_own, rows), [p_own])
+    chosen_own = pick_rows(one_hot(asked_own, rows), p_own)
     hard_own = group_rows(chosen_own, group_count)
-    chosen_far = pick_rows(one_hot(asked_far, 3 * rows), [*p_mid, *p_opp])
+    chosen_far = pick_rows(one_hot(asked_far, 3 * rows), p_far)
     hard_far = group_rows(chosen_far, group_count)
 
-    q_emb = embed(query_hidden, gain)
+    q_emb = embed(query_hidden, gain, 1)[0]
     q_line = lax.all_gather(q_emb, "x", axis=0, tiled=True)
 
     by_x = slot_query.reshape(group_count, RING, RING * CAP).transpose(1, 0, 2)
@@ -469,7 +487,7 @@
     far_queries = group_rows(leave_far, group_count)
     own_queries = group_rows(leave_own, group_count)
 
-    near = line_scores([p_own, *p_mid, *p_opp, hard_own], q_line, scale)
+    near = line_scores([*p_own, *p_far, hard_own], q_line, scale)
     far, part_log = far_scores(near, [hard_far], q_line, asked_by, line, scale)
     part_log = part_log.reshape(RING, rows)
     own_place = jnp.arange(RING, dtype=jnp.int32)[:, None] == x_place
@@ -486,7 +504,7 @@
 
     part, gain_part, slot_coeff, positive, coeff = query_side(
         near, far, asked_by, log_total, weight, target, q_line,
-        [p_own, *p_mid, *p_opp, hard_own, hard_far], line, scale,
+        [*p_own, *p_far, hard_own, hard_far], line, scale,
     )
     loss_rows = lax.dynamic_slice(log_total - positive, (0, first_row), (1, rows)).reshape(-1)
     query_up = lax.psum_scatter(part, "x", scatter_dimension=0, tiled=True)
@@ -507,8 +525,7 @@
 
     put_own = put_rows(asked_own, got_coeff[:, :first], rows)
     put_far = put_rows(asked_far, got_coeff[:, first:], 3 * rows)
-    half = rows // 2
-    low_1, high_1, low_3, high_3, low_2, high_2 = [(i * half, (i + 1) * half) for i in range(6)]
+    low_1, high_1, low_2, low_3, high_2, high_3 = [(i * half, (i + 1) * half) for i in range(6)]
     own_part, for_above, for_below, pass_up, pass_down = passage_side(
         coeff, q_line, put_far, far_queries, scale,
         [[low_1, high_1], [low_3, high_3], [low_2], [high_2]],

time: 235 us -> 228 us (0.970)
  local copies, waits for them, and re-layouts: 35.5 us -> 30.6 us
  Pallas kernels: 46.4 us -> 44 us
    unnamed x93 -> x137, local copies, waits for them, and re-layouts: 29.7 us -> 26.5 us
    ppermute x7, starting transfers between devices: 6.32 us -> 8.84 us  [pair_sum(): return value + lax.ppermute(value, axis, pairs)]
    ppermute x14, starting transfers between devices: 22.5 us -> 19.9 us  [shift(): lax.ppermute(value, axis, [(i, (i + step) % RING) for i in range(RING)])]
    all_to_all x4, waiting for transfers between devices: 8.19 us -> 10.6 us  [group_rows(): return lax.all_to_all(blocks, GROUPS, 0, 0, tiled=True).reshape(rows.shape)]
    all_to_all x4, starting transfers between devices: 18.6 us -> 16.2 us  [group_rows(): return lax.all_to_all(blocks, GROUPS, 0, 0, tiled=True).reshape(rows.shape)]
  transfers between devices with their start and end apart: 35 -> 35, of which waited for: 17 -> 15; matrix products, arithmetic and copies ran while one was open for 6% -> 6% of each run, Pallas kernels for 19% -> 18%
where the time goes in v6:
time: 228 us; the launch traced here: 227 us
  starting transfers between devices  63.6 us (28%)
  waiting for transfers between devices  63.3 us (28%)
  Pallas kernels  44 us (19%)
  local copies, waits for them, and re-layouts  30.6 us (13%)
  between operations  15 us (7%)
  other arithmetic  10.8 us (5%)
    ppermute x14, waiting for transfers between devices, shift(): lax.ppermute(value, axis, [(i, (i + step) % RING) for i in range(RING)])  27.7 us
    unnamed x137, local copies, waits for them, and re-layouts  26.5 us
    ppermute x14, starting transfers between devices, shift(): lax.ppermute(value, axis, [(i, (i + step) % RING) for i in range(RING)])  19.9 us
    ppermute x7, waiting for transfers between devices, pair_sum(): return value + lax.ppermute(value, axis, pairs)  16.5 us
    all_to_all x4, starting transfers between devices, group_rows(): return lax.all_to_all(blocks, GROUPS, 0, 0, tiled=True).reshape(rows.shape)  16.2 us
    all_to_all x4, waiting for transfers between devices, group_rows(): return lax.all_to_all(blocks, GROUPS, 0, 0, tiled=True).reshape(rows.shape)  10.6 us
    ppermute x7, starting transfers between devices, group_table(): lax.ppermute(row, GROUPS, [(z * 2 + c, (z + z_step) % z_count * 2 + (c ^...  10.4 us
    pallas_call x4, Pallas kernels, pick_rows(): pl.pallas_call(body, grid=(width // tile(width),), in_specs=[whole(matrix...  10.3 us
  transfers between devices with their start and end apart: 35, of which 15 were waited for; matrix products, arithmetic and copies ran while one was open for 6% of the time, Pallas kernels for 18%

profile of v6, /device:TPU:0, one launch (start us, length us, event | category | flops | bytes accessed | tf_op | source)
XLA Modules:
  0.0 227.3 jit_solution(710982424204214355)
XLA Ops:
  16.6 8.2 %all-to-all-start = ((s32[32,1,16]{2,1,0:T(1,128)}), s32[32,1,16]{2,1,0:T(1,128)S(1)}, u32[]{:S(2)}, u32[]{:S(2)}) async-start(s32[32,1,16]{2,1,0:T(1,128)} %bitcast.4), calls=%async_computation | async-start | bytes 32768 | tf_op jit(solution)/shard_map/all_to_all | solution.py:448
  24.8 7.2 %all-to-all-done = s32[32,1,16]{2,1,0:T(1,128)S(1)} async-done(((s32[32,1,16]{2,1,0:T(1,128)}), s32[32,1,16]{2,1,0:T(1,128)S(1)}, u32[]{:S(2)}, u32[]{:S(2)}) %all-to-all-start) | async-done | bytes 2080 | tf_op jit(solution)/shard_map/all_to_all | solution.py:448
  34.4 3.2 %collective-permute-start.4 = (bf16[128,4096]{1,0:T(8,128)(2,1)}, bf16[128,4096]{1,0:T(8,128)(2,1)S(1)}, u32[]{:S(2)}, u32[]{:S(2)}) collective-permute-start(bf16[128,4096]{1,0:T(8,128)(2,1)} %pad_maximum_fusion), channel_id=1, source_target_pairs={{0,12},{4,0},{8,4},{12,8},{1,13},{5,1},{9,5},{13,9},{2,14},{6,2},{... | collective-permute-start | bytes 3145736 | tf_op jit(solution)/shard_map/ppermute | solution.py:21
  41.0 3.6 %all-to-all-start.1 = ((bf16[8,16,4096]{2,1,0:T(8,128)(2,1)}), bf16[8,16,4096]{2,1,0:T(8,128)(2,1)S(1)}, u32[]{:S(2)}, u32[]{:S(2)}) async-start(bf16[8,16,4096]{2,1,0:T(8,128)(2,1)} %bitcast.54), calls=%async_computation.1 | async-start | bytes 2097152 | tf_op jit(solution)/shard_map/all_to_all | solution.py:40
  45.1 15.4 %collective-permute-done.4.refs_3_.refs_1_ = bf16[128,4096]{1,0:T(8,128)(2,1)S(1)} collective-permute-done((bf16[128,4096]{1,0:T(8,128)(2,1)}, bf16[128,4096]{1,0:T(8,128)(2,1)S(1)}, u32[]{:S(2)}, u32[]{:S(2)}) %collective-permute-start.4) | collective-permute-done | bytes 1048608 | tf_op jit(solution)/shard_map/ppermute | solution.py:21
  60.5 4.4 %collective-permute-done.6.refs_4_.refs_2_ = bf16[128,4096]{1,0:T(8,128)(2,1)S(1)} collective-permute-done((bf16[128,4096]{1,0:T(8,128)(2,1)}, bf16[128,4096]{1,0:T(8,128)(2,1)S(1)}, u32[]{:S(2)}, u32[]{:S(2)}) %collective-permute-start.6) | collective-permute-done | bytes 1048608 | tf_op jit(solution)/shard_map/ppermute | solution.py:21
  67.0 3.8 %pick_rows.7 = bf16[384,4096]{1,0:T(8,128)(2,1)} custom-call(bf16[384,384]{1,0:T(8,128)(2,1)S(1)} %compare_convert_fusion.matrix_ref, bf16[64,4096]{1,0:T(8,128)(2,1)S(1)} %copy-done.16, bf16[128,4096]{1,0:T(8,128)(2,1)S(1)} %collective-permute-done.4.refs_3_.refs_1_, bf16[128,4096]{1,0:T(8,128)(2,1)S(1)} %collective-permute-done.6.refs_4_.refs_2_, ...), custom_call_target="tpu_custom_call" | custom-call | flops 1 | bytes 1 | tf_op jit(solution)/shard_map/pick_rows/pallas_call | solution.py:187
  71.8 3.8 %all-to-all-start.2 = ((bf16[8,48,4096]{2,1,0:T(8,128)(2,1)}), bf16[8,48,4096]{2,1,0:T(8,128)(2,1)S(1)}, u32[]{:S(2)}, u32[]{:S(2)}) async-start(bf16[8,48,4096]{2,1,0:T(8,128)(2,1)} %bitcast.8), calls=%async_computation.2 | async-start | bytes 6291456 | tf_op jit(solution)/shard_map/all_to_all | solution.py:40
  97.9 4.3 %line_scores.1.near_ref = f32[640,512]{1,0:T(8,128)S(1)} custom-call(bf16[512,4096]{1,0:T(8,128)(2,1)S(1)} %copy-done.1, bf16[64,4096]{1,0:T(8,128)(2,1)S(1)} %copy-done.24, bf16[64,4096]{1,0:T(8,128)(2,1)S(1)} %copy-done.27, bf16[64,4096]{1,0:T(8,128)(2,1)S(1)} %copy-done.17, bf16[128,4096]{1,0:T(8,128)(2,1)S(1)} %copy-done.7, ...), custom_call_target="tpu_custom_call" | custom-call | flops 1 | bytes 1 | tf_op jit(solution)/shard_map/line_scores/pallas_call | solution.py:214
  103.3 10.6 %all-to-all-done.2 = bf16[8,48,4096]{2,1,0:T(8,128)(2,1)S(1)} async-done(((bf16[8,48,4096]{2,1,0:T(8,128)(2,1)}), bf16[8,48,4096]{2,1,0:T(8,128)(2,1)S(1)}, u32[]{:S(2)}, u32[]{:S(2)}) %all-to-all-start.2) | async-done | bytes 3145760 | tf_op jit(solution)/shard_map/all_to_all | solution.py:40
  113.9 4.4 %all-to-all-start.3 = ((bf16[8,48,4096]{2,1,0:T(8,128)(2,1)}), bf16[8,48,4096]{2,1,0:T(8,128)(2,1)}, u32[]{:S(2)}, u32[]{:S(2)}) async-start(bf16[8,48,4096]{2,1,0:T(8,128)(2,1)} %bitcast.50), calls=%async_computation.3 | async-start | bytes 6291456 | tf_op jit(solution)/shard_map/all_to_all | solution.py:40
  123.1 3.7 %far_scores.1 = (f32[384,512]{1,0:T(8,128)S(1)}, f32[1,512]{1,0:T(1,128)S(1)}) custom-call(f32[640,512]{1,0:T(8,128)S(1)} %copy-done.30, bf16[512,512]{1,0:T(8,128)(2,1)S(1)} %copy-done.40, bf16[512,4096]{1,0:T(8,128)(2,1)S(1)} %copy-done.2, bf16[384,4096]{1,0:T(8,128)(2,1)S(1)} %bitcast.48), custom_call_target="tpu_custom_call" | custom-call | flops 99999997952 | bytes 100000000 | tf_op jit(solution)/shard_map/far_scores/pallas_call | solution.py:258
  131.7 3.5 %collective-permute-done.9 = f32[8,128]{1,0:T(8,128)S(1)} collective-permute-done((f32[8,128]{1,0:T(8,128)S(1)}, f32[8,128]{1,0:T(8,128)S(1)}, u32[]{:S(2)}, u32[]{:S(2)}) %collective-permute-start.9) | collective-permute-done | bytes 4128 | tf_op jit(solution)/shard_map/ppermute | solution.py:21
  135.4 7.6 %query_side.1 = (bf16[512,4096]{1,0:T(8,128)(2,1)S(1)}, f32[1,4096]{1,0:T(1,128)S(1)}, f32[8,512]{1,0:T(8,128)S(1)}, f32[1,512]{1,0:T(1,128)S(1)}, bf16[512,512]{1,0:T(8,128)(2,1)S(1)}) custom-call(f32[640,512]{1,0:T(8,128)S(1)} %copy-done.31, f32[384,512]{1,0:T(8,128)S(1)} %get-tuple-element.34.far_ref, bf16[512,512]{1,0:T(8,128)(2,1)S(1)} %copy-done.41, ...), custom_call_target="tpu_custom_call" | custom-call | flops 1 | bytes 1 | tf_op jit(solution)/shard_map/query_side/pallas_call | solution.py:324
  160.7 6.2 %passage_side.1 = (f32[128,4096]{1,0:T(8,128)S(1)}, bf16[128,4096]{1,0:T(8,128)(2,1)S(1)}, bf16[128,4096]{1,0:T(8,128)(2,1)S(1)}, bf16[64,4096]{1,0:T(8,128)(2,1)S(1)}, bf16[64,4096]{1,0:T(8,128)(2,1)S(1)}) custom-call(bf16[512,512]{1,0:T(8,128)(2,1)S(1)} %copy-done.49, bf16[512,4096]{1,0:T(8,128)(2,1)S(1)} %copy-done.4, ...), custom_call_target="tpu_custom_call" | custom-call | flops 99999997952 | bytes 100000000 | tf_op jit(solution)/shard_map/passage_side/pallas_call | solution.py:373
  168.3 3.2 %collective-permute-start.20 = (bf16[64,4096]{1,0:T(8,128)(2,1)S(1)}, bf16[64,4096]{1,0:T(8,128)(2,1)S(1)}, u32[]{:S(2)}, u32[]{:S(2)}) collective-permute-start(bf16[64,4096]{1,0:T(8,128)(2,1)S(1)} %get-tuple-element.45), channel_id=1, source_target_pairs={{0,12},{4,0},{8,4},{12,8},{1,13},{5,1},{9,5},{13,9},{2,14},{6,2},{... | collective-permute-start | bytes 1572872 | tf_op jit(solution)/shard_map/ppermute | solution.py:21
  172.1 3.2 %collective-permute-done.10 = f32[32,128]{1,0:T(8,128)S(1)} collective-permute-done((f32[32,128]{1,0:T(8,128)S(1)}, f32[32,128]{1,0:T(8,128)S(1)}, u32[]{:S(2)}, u32[]{:S(2)}) %collective-permute-start.10) | collective-permute-done | bytes 16416 | tf_op jit(solution)/shard_map/ppermute | solution.py:35
  175.3 4.0 %collective-permute-start.11 = (f32[32,128]{1,0:T(8,128)S(1)}, f32[32,128]{1,0:T(8,128)S(1)}, u32[]{:S(2)}, u32[]{:S(2)}) collective-permute-start(f32[32,128]{1,0:T(8,128)S(1)} %add.358), channel_id=1, source_target_pairs={{0,96},{32,64},{64,32},{96,0},{1,97},{33,65},{65,33},{97,1},{2,98}... | collective-permute-start | bytes 49160 | tf_op jit(solution)/shard_map/ppermute | solution.py:35
  185.8 3.2 %collective-permute-start.25 = (bf16[128,4096]{1,0:T(8,128)(2,1)}, bf16[128,4096]{1,0:T(8,128)(2,1)}, u32[]{:S(2)}, u32[]{:S(2)}) collective-permute-start(bf16[128,4096]{1,0:T(8,128)(2,1)} %get-tuple-element.51), channel_id=1, source_target_pairs={{0,12},{4,0},{8,4},{12,8},{1,13},{5,1},{9,5},{13,9},{2,14},{6,2},{... | collective-permute-start | bytes 3145736 | tf_op jit(solution)/shard_map/ppermute | solution.py:21
  189.0 4.4 %all-to-all-start.4 = ((bf16[8,16,4096]{2,1,0:T(8,128)(2,1)}), bf16[8,16,4096]{2,1,0:T(8,128)(2,1)S(1)}, u32[]{:S(2)}, u32[]{:S(2)}) async-start(bf16[8,16,4096]{2,1,0:T(8,128)(2,1)} %bitcast.31), calls=%async_computation.5 | async-start | bytes 2097152 | tf_op jit(solution)/shard_map/all_to_all | solution.py:40
  195.2 3.3 %collective-permute-done.22 = f32[32,128]{1,0:T(8,128)S(1)} collective-permute-done((f32[32,128]{1,0:T(8,128)S(1)}, f32[32,128]{1,0:T(8,128)S(1)}, u32[]{:S(2)}, u32[]{:S(2)}) %collective-permute-start.22) | collective-permute-done | bytes 16416 | tf_op jit(solution)/shard_map/ppermute | solution.py:35
  199.3 4.2 %collective-permute-done.23 = f32[32,128]{1,0:T(8,128)S(1)} collective-permute-done((f32[32,128]{1,0:T(8,128)S(1)}, f32[32,128]{1,0:T(8,128)S(1)}, u32[]{:S(2)}, u32[]{:S(2)}) %collective-permute-start.23) | collective-permute-done | bytes 16416 | tf_op jit(solution)/shard_map/ppermute | solution.py:35
  207.8 3.2 %collective-permute-done.26 = f32[32,128]{1,0:T(8,128)S(1)} collective-permute-done((f32[32,128]{1,0:T(8,128)S(1)}, f32[32,128]{1,0:T(8,128)S(1)}, u32[]{:S(2)}, u32[]{:S(2)}) %collective-permute-start.26) | collective-permute-done | bytes 16416 | tf_op jit(solution)/shard_map/ppermute | solution.py:35
  215.4 4.5 %finish.3 = bf16[128,4096]{1,0:T(8,128)(2,1)} custom-call(bf16[128,4096]{1,0:T(8,128)(2,1)S(1)} %copy-done.35, f32[1,4096]{1,0:T(1,128)S(1)} %bitcast.58, f32[128,4096]{1,0:T(8,128)S(1)} %copy-done.39, bf16[128,4096]{1,0:T(8,128)(2,1)} %collective-permute-done.24.refs_1_, bf16[128,4096]{1,0:T(8,128)(2,1)} %collective-permute-done.25.refs_2_, ...), custom_call_target="tpu_custom_call" | custom-call | flops 1 | bytes 1 | tf_op jit(solution)/shard_map/finish/pallas_call | solution.py:169
  (277 shorter events, 89.1 us)
Async XLA Ops:
  7.2 81.2 %all-gather.2.cloned.1.call-start = ((), (), s32[]{:S(2)}) async-start(), calls=%async_computation.6 | async-start | bytes 5242880 | tf_op jit(solution)/shard_map/all_gather | solution.py:473
  12.0 20.2 %collective-permute-start.3 = (bf16[64,4096]{1,0:T(8,128)(2,1)S(1)}, bf16[64,4096]{1,0:T(8,128)(2,1)S(1)}, u32[]{:S(2)}, u32[]{:S(2)}) collective-permute-start(bf16[64,4096]{1,0:T(8,128)(2,1)S(1)} %get-tuple-element.30.refs_0_), channel_id=1, source_target_pairs={{0,12},{4,0},{8,4},{12,8},{1,13},{5,1},{9,5},{13,9},{2,14},{6,2},{... | collective-permute-start | bytes 1572872 | tf_op jit(solution)/shard_map/ppermute | solution.py:21
  15.2 17.0 %collective-permute-start.5 = (bf16[64,4096]{1,0:T(8,128)(2,1)S(1)}, bf16[64,4096]{1,0:T(8,128)(2,1)S(1)}, u32[]{:S(2)}, u32[]{:S(2)}) collective-permute-start(bf16[64,4096]{1,0:T(8,128)(2,1)S(1)} %get-tuple-element.31.refs_1_), channel_id=1, source_target_pairs={{0,4},{4,8},{8,12},{12,0},{1,5},{5,9},{9,13},{13,1},{2,6},{6,10},{... | collective-permute-start | bytes 1572872 | tf_op jit(solution)/shard_map/ppermute | solution.py:21
  16.6 15.4 %all-to-all-start = ((s32[32,1,16]{2,1,0:T(1,128)}), s32[32,1,16]{2,1,0:T(1,128)S(1)}, u32[]{:S(2)}, u32[]{:S(2)}) async-start(s32[32,1,16]{2,1,0:T(1,128)} %bitcast.4), calls=%async_computation | async-start | bytes 32768 | tf_op jit(solution)/shard_map/all_to_all | solution.py:448
  34.4 26.0 %collective-permute-start.4 = (bf16[128,4096]{1,0:T(8,128)(2,1)}, bf16[128,4096]{1,0:T(8,128)(2,1)S(1)}, u32[]{:S(2)}, u32[]{:S(2)}) collective-permute-start(bf16[128,4096]{1,0:T(8,128)(2,1)} %pad_maximum_fusion), channel_id=1, source_target_pairs={{0,12},{4,0},{8,4},{12,8},{1,13},{5,1},{9,5},{13,9},{2,14},{6,2},{... | collective-permute-start | bytes 3145736 | tf_op jit(solution)/shard_map/ppermute | solution.py:21
  38.8 26.1 %collective-permute-start.6 = (bf16[128,4096]{1,0:T(8,128)(2,1)}, bf16[128,4096]{1,0:T(8,128)(2,1)S(1)}, u32[]{:S(2)}, u32[]{:S(2)}) collective-permute-start(bf16[128,4096]{1,0:T(8,128)(2,1)} %pad_maximum_fusion.1), channel_id=1, source_target_pairs={{0,4},{4,8},{8,12},{12,0},{1,5},{5,9},{9,13},{13,1},{2,6},{6,10},{... | collective-permute-start | bytes 3145736 | tf_op jit(solution)/shard_map/ppermute | solution.py:21
  41.0 29.8 %all-to-all-start.1 = ((bf16[8,16,4096]{2,1,0:T(8,128)(2,1)}), bf16[8,16,4096]{2,1,0:T(8,128)(2,1)S(1)}, u32[]{:S(2)}, u32[]{:S(2)}) async-start(bf16[8,16,4096]{2,1,0:T(8,128)(2,1)} %bitcast.54), calls=%async_computation.1 | async-start | bytes 2097152 | tf_op jit(solution)/shard_map/all_to_all | solution.py:40
  71.8 42.1 %all-to-all-start.2 = ((bf16[8,48,4096]{2,1,0:T(8,128)(2,1)}), bf16[8,48,4096]{2,1,0:T(8,128)(2,1)S(1)}, u32[]{:S(2)}, u32[]{:S(2)}) async-start(bf16[8,48,4096]{2,1,0:T(8,128)(2,1)} %bitcast.8), calls=%async_computation.2 | async-start | bytes 6291456 | tf_op jit(solution)/shard_map/all_to_all | solution.py:40
  75.9 7.0 %collective-permute-start = (s32[1,128]{1,0:T(1,128)S(1)}, s32[1,128]{1,0:T(1,128)S(1)}, u32[]{:S(2)}, u32[]{:S(2)}) collective-permute-start(s32[1,128]{1,0:T(1,128)S(1)} %broadcast_in_dim.372), channel_id=1, source_target_pairs={{0,1},{1,2},{2,3},{3,0},{4,5},{5,6},{6,7},{7,4},{8,9},{9,10},{10,1... | collective-permute-start | bytes 1544 | tf_op jit(solution)/shard_map/ppermute | solution.py:21
  76.5 7.7 %collective-permute-start.1 = (s32[1,128]{1,0:T(1,128)S(1)}, s32[1,128]{1,0:T(1,128)S(1)}, u32[]{:S(2)}, u32[]{:S(2)}) collective-permute-start(s32[1,128]{1,0:T(1,128)S(1)} %broadcast_in_dim.377), channel_id=1, source_target_pairs={{0,2},{1,3},{2,0},{3,1},{4,6},{5,7},{6,4},{7,5},{8,10},{9,11},{10,... | collective-permute-start | bytes 1544 | tf_op jit(solution)/shard_map/ppermute | solution.py:21
  78.7 6.5 %collective-permute-start.2 = (s32[1,128]{1,0:T(1,128)S(1)}, s32[1,128]{1,0:T(1,128)S(1)}, u32[]{:S(2)}, u32[]{:S(2)}) collective-permute-start(s32[1,128]{1,0:T(1,128)S(1)} %broadcast_in_dim.382), channel_id=1, source_target_pairs={{0,3},{1,0},{2,1},{3,2},{4,7},{5,4},{6,5},{7,6},{8,11},{9,8},{10,9... | collective-permute-start | bytes 1544 | tf_op jit(solution)/shard_map/ppermute | solution.py:21
  113.9 44.4 %all-to-all-start.3 = ((bf16[8,48,4096]{2,1,0:T(8,128)(2,1)}), bf16[8,48,4096]{2,1,0:T(8,128)(2,1)}, u32[]{:S(2)}, u32[]{:S(2)}) async-start(bf16[8,48,4096]{2,1,0:T(8,128)(2,1)} %bitcast.50), calls=%async_computation.3 | async-start | bytes 6291456 | tf_op jit(solution)/shard_map/all_to_all | solution.py:40
  118.4 85.1 %reduce-scatter.2.cloned.1.call-start = ((), (), s32[]{:S(2)}) async-start(), calls=%async_computation.7 | async-start | bytes 5242880 | tf_op jit(solution)/shard_map/reduce_scatter | solution.py:510
  146.1 6.5 %collective-permute-start.12 = (f32[1,64]{1,0:T(1,128)S(1)}, f32[1,64]{1,0:T(1,128)S(1)}, u32[]{:S(2)}, u32[]{:S(2)}) collective-permute-start(f32[1,64]{1,0:T(1,128)S(1)} %bitcast.85), channel_id=1, source_target_pairs={{0,16},{16,0},{32,48},{48,32},{64,80},{80,64},{96,112},{112,96},{1... | collective-permute-start | bytes 776 | tf_op jit(solution)/shard_map/ppermute | solution.py:54
  146.2 8.1 %collective-permute-start.13 = (f32[1,64]{1,0:T(1,128)S(1)}, f32[1,64]{1,0:T(1,128)S(1)}, u32[]{:S(2)}, u32[]{:S(2)}) collective-permute-start(f32[1,64]{1,0:T(1,128)S(1)} %bitcast.84), channel_id=1, source_target_pairs={{0,32},{16,48},{32,64},{48,80},{64,96},{80,112},{96,0},{112,16},{1... | collective-permute-start | bytes 776 | tf_op jit(solution)/shard_map/ppermute | solution.py:54
  148.2 8.5 %collective-permute-start.14 = (f32[1,64]{1,0:T(1,128)S(1)}, f32[1,64]{1,0:T(1,128)S(1)}, u32[]{:S(2)}, u32[]{:S(2)}) collective-permute-start(f32[1,64]{1,0:T(1,128)S(1)} %bitcast.81), channel_id=1, source_target_pairs={{0,48},{16,32},{32,80},{48,64},{64,112},{80,96},{96,16},{112,0},{1... | collective-permute-start | bytes 776 | tf_op jit(solution)/shard_map/ppermute | solution.py:54
  149.4 7.4 %collective-permute-start.15 = (f32[1,64]{1,0:T(1,128)S(1)}, f32[1,64]{1,0:T(1,128)S(1)}, u32[]{:S(2)}, u32[]{:S(2)}) collective-permute-start(f32[1,64]{1,0:T(1,128)S(1)} %bitcast.80), channel_id=1, source_target_pairs={{0,64},{16,80},{32,96},{48,112},{64,0},{80,16},{96,32},{112,48},{1... | collective-permute-start | bytes 776 | tf_op jit(solution)/shard_map/ppermute | solution.py:54
  150.9 5.9 %collective-permute-start.16 = (f32[1,64]{1,0:T(1,128)S(1)}, f32[1,64]{1,0:T(1,128)S(1)}, u32[]{:S(2)}, u32[]{:S(2)}) collective-permute-start(f32[1,64]{1,0:T(1,128)S(1)} %bitcast.78), channel_id=1, source_target_pairs={{0,80},{16,64},{32,112},{48,96},{64,16},{80,0},{96,48},{112,32},{1... | collective-permute-start | bytes 776 | tf_op jit(solution)/shard_map/ppermute | solution.py:54
  168.3 15.4 %collective-permute-start.19 = (bf16[64,4096]{1,0:T(8,128)(2,1)S(1)}, bf16[64,4096]{1,0:T(8,128)(2,1)S(1)}, u32[]{:S(2)}, u32[]{:S(2)}) collective-permute-start(bf16[64,4096]{1,0:T(8,128)(2,1)S(1)} %get-tuple-element.40), channel_id=1, source_target_pairs={{0,4},{4,8},{8,12},{12,0},{1,5},{5,9},{9,13},{13,1},{2,6},{6,10},{... | collective-permute-start | bytes 1572872 | tf_op jit(solution)/shard_map/ppermute | solution.py:21
  168.3 15.4 %collective-permute-start.20 = (bf16[64,4096]{1,0:T(8,128)(2,1)S(1)}, bf16[64,4096]{1,0:T(8,128)(2,1)S(1)}, u32[]{:S(2)}, u32[]{:S(2)}) collective-permute-start(bf16[64,4096]{1,0:T(8,128)(2,1)S(1)} %get-tuple-element.45), channel_id=1, source_target_pairs={{0,12},{4,0},{8,4},{12,8},{1,13},{5,1},{9,5},{13,9},{2,14},{6,2},{... | collective-permute-start | bytes 1572872 | tf_op jit(solution)/shard_map/ppermute | solution.py:21
  185.8 28.0 %collective-permute-start.24 = (bf16[128,4096]{1,0:T(8,128)(2,1)}, bf16[128,4096]{1,0:T(8,128)(2,1)}, u32[]{:S(2)}, u32[]{:S(2)}) collective-permute-start(bf16[128,4096]{1,0:T(8,128)(2,1)} %get-tuple-element.46), channel_id=1, source_target_pairs={{0,4},{4,8},{8,12},{12,0},{1,5},{5,9},{9,13},{13,1},{2,6},{6,10},{... | collective-permute-start | bytes 3145736 | tf_op jit(solution)/shard_map/ppermute | solution.py:21
  185.8 28.0 %collective-permute-start.25 = (bf16[128,4096]{1,0:T(8,128)(2,1)}, bf16[128,4096]{1,0:T(8,128)(2,1)}, u32[]{:S(2)}, u32[]{:S(2)}) collective-permute-start(bf16[128,4096]{1,0:T(8,128)(2,1)} %get-tuple-element.51), channel_id=1, source_target_pairs={{0,12},{4,0},{8,4},{12,8},{1,13},{5,1},{9,5},{13,9},{2,14},{6,2},{... | collective-permute-start | bytes 3145736 | tf_op jit(solution)/shard_map/ppermute | solution.py:21
  189.0 24.7 %all-to-all-start.4 = ((bf16[8,16,4096]{2,1,0:T(8,128)(2,1)}), bf16[8,16,4096]{2,1,0:T(8,128)(2,1)S(1)}, u32[]{:S(2)}, u32[]{:S(2)}) async-start(bf16[8,16,4096]{2,1,0:T(8,128)(2,1)} %bitcast.31), calls=%async_computation.5 | async-start | bytes 2097152 | tf_op jit(solution)/shard_map/all_to_all | solution.py:40
  211.0 8.9 %collective-permute-start.27 = (f32[32,128]{1,0:T(8,128)S(1)}, f32[32,128]{1,0:T(8,128)S(1)}, u32[]{:S(2)}, u32[]{:S(2)}) collective-permute-start(f32[32,128]{1,0:T(8,128)S(1)} %add.387), channel_id=1, source_target_pairs={{0,12},{4,8},{8,4},{12,0},{1,13},{5,9},{9,5},{13,1},{2,14},{6,10},... | collective-permute-start | bytes 49160 | tf_op jit(solution)/shard_map/ppermute | solution.py:35
  (79 other events, 596.9 us)
Sparse Core Ops, SparseCore 0:
  11.3 50.8 all-gather.1
  156.8 41.5 reduce-scatter.1

commit v7 on v6

--- a/solution.py
+++ b/solution.py
@@ -24,9 +24,11 @@
 def ring_gather(low, high, axis):
     up_low = shift(low, axis, -1)
     down_high = shift(high, axis, 1)
-    up_more = shift(jnp.concatenate([high, up_low], axis=0), axis, -1)
-    down_more = shift(jnp.concatenate([low, down_high], axis=0), axis, 1)
-    return [up_low, up_more, down_more, down_high]
+    to_below = jnp.concatenate([high, up_low], axis=0)
+    to_above = jnp.concatenate([low, down_high], axis=0)
+    up_more = shift(to_below, axis, -1)
+    down_more = shift(to_above, axis, 1)
+    return [up_low, up_more, down_more, down_high], [to_below, to_above]
 
 
 def pair_sum(value, axis, turn):
@@ -146,7 +148,7 @@
 
 def finish(hidden, gain, terms, put=None, arrived=None, scale=1.0):
     rows, width = hidden.shape
-    step = rows // 4
+    step = rows // 8
     product = () if put is None else (put, arrived)
 
     def body(hidden_ref, gain_ref, *refs):
@@ -368,7 +370,7 @@
             for low, high in ranges:
                 out_ref[at : at + high - low] = total[low:high]
                 at += high - low
-        own_ref[...] = scale * mxu(coeff_ref[:own], query_ref[...])
+        own_ref[...] = (scale * mxu(coeff_ref[:own], query_ref[...])).astype(jnp.bfloat16)
 
     return pl.pallas_call(
         body,
@@ -380,8 +382,9 @@
             columns(arrived.shape[0], width),
         ],
         out_specs=[columns(own, width)] + [columns(size, width) for size in sizes],
-        out_shape=[jax.ShapeDtypeStruct((own, width), jnp.float32)]
-        + [jax.ShapeDtypeStruct((size, width), jnp.bfloat16) for size in sizes],
+        out_shape=[
+            jax.ShapeDtypeStruct((size, width), jnp.bfloat16) for size in (own, *sizes)
+        ],
         compiler_params=params(20),
         cost_estimate=LARGE,
         name="passage_side",
@@ -429,7 +432,7 @@
 
     gain = norm_gain.reshape(1, width)
     p_own = embed(passage_hidden, gain, 2)
-    p_far = ring_gather(*p_own, "y")
+    p_far, p_sent = ring_gather(*p_own, "y")
 
     flat_ids = hneg_ids.reshape(-1)
     id_count = rows * neg_count
@@ -450,7 +453,7 @@
     )
     asked = asked.reshape(group_count, RING, RING, CAP).transpose(0, 2, 1, 3)
     place = jnp.arange(line, dtype=jnp.int32)
-    asked, _ = lax.optimization_barrier((asked, [p_far[0], p_far[-1]]))
+    asked, query_hidden, _ = lax.optimization_barrier((asked, query_hidden, p_sent))
     asked_own = asked[:, 0].reshape(-1)
     half = rows // 2
 

time: 228 us -> 226 us (level)
  waiting for transfers between devices: 63.3 us -> 57.9 us
  local copies, waits for them, and re-layouts: 30.6 us -> 33.6 us
  Pallas kernels: 44 us -> 46.5 us
    pallas_call x2, Pallas kernels: 6.99 us -> 10.9 us  [finish(): pl.pallas_call(body, grid=(rows // step,), in_specs=[block, whole((1, wid...]
    ppermute x14, waiting for transfers between devices: 27.7 us -> 24.6 us  [shift(): lax.ppermute(value, axis, [(i, (i + step) % RING) for i in range(RING)])]
    unnamed x137 -> x139, local copies, waits for them, and re-layouts: 26.5 us -> 27.7 us
  transfers between devices with their start and end apart: 35 -> 35, of which waited for: 15 -> 14; matrix products, arithmetic and copies ran while one was open for 6% -> 7% of each run, Pallas kernels for 18% -> 20%
where the time goes in v7:
time: 226 us; the launch traced here: 225 us
  starting transfers between devices  63.6 us (28%)
  waiting for transfers between devices  57.9 us (26%)
  Pallas kernels  46.5 us (21%)
  local copies, waits for them, and re-layouts  33.6 us (15%)
  between operations  15.1 us (7%)
  other arithmetic  8.6 us (4%)
    unnamed x139, local copies, waits for them, and re-layouts  27.7 us
    ppermute x14, waiting for transfers between devices, shift(): lax.ppermute(value, axis, [(i, (i + step) % RING) for i in range(RING)])  24.6 us
    ppermute x14, starting transfers between devices, shift(): lax.ppermute(value, axis, [(i, (i + step) % RING) for i in range(RING)])  20.3 us
    all_to_all x4, starting transfers between devices, group_rows(): return lax.all_to_all(blocks, GROUPS, 0, 0, tiled=True).reshape(rows.shape)  16.2 us
    ppermute x7, waiting for transfers between devices, pair_sum(): return value + lax.ppermute(value, axis, pairs)  15.9 us
    pallas_call x2, Pallas kernels, finish(): pl.pallas_call(body, grid=(rows // step,), in_specs=[block, whole((1, wid...  10.9 us
    all_to_all x4, waiting for transfers between devices, group_rows(): return lax.all_to_all(blocks, GROUPS, 0, 0, tiled=True).reshape(rows.shape)  10.6 us
    ppermute x7, starting transfers between devices, group_table(): lax.ppermute(row, GROUPS, [(z * 2 + c, (z + z_step) % z_count * 2 + (c ^...  10.4 us
  transfers between devices with their start and end apart: 35, of which 14 were waited for; matrix products, arithmetic and copies ran while one was open for 7% of the time, Pallas kernels for 20%

profile of v7, /device:TPU:0, one launch (start us, length us, event | category | flops | bytes accessed | tf_op | source)
XLA Modules:
  0.0 225.3 jit_solution(11160599147497485267)
XLA Ops:
  15.5 8.2 %all-to-all-start = ((s32[32,1,16]{2,1,0:T(1,128)}), s32[32,1,16]{2,1,0:T(1,128)S(1)}, u32[]{:S(2)}, u32[]{:S(2)}) async-start(s32[32,1,16]{2,1,0:T(1,128)} %bitcast), calls=%async_computation | async-start | bytes 32768 | tf_op jit(solution)/shard_map/all_to_all | solution.py:451
  25.4 5.5 %all-to-all-done = s32[32,1,16]{2,1,0:T(1,128)S(1)} async-done(((s32[32,1,16]{2,1,0:T(1,128)}), s32[32,1,16]{2,1,0:T(1,128)S(1)}, u32[]{:S(2)}, u32[]{:S(2)}) %all-to-all-start) | async-done | bytes 2080 | tf_op jit(solution)/shard_map/all_to_all | solution.py:451
  35.2 2.9 %collective-permute-start.5 = (bf16[128,4096]{1,0:T(8,128)(2,1)}, bf16[128,4096]{1,0:T(8,128)(2,1)S(1)}, u32[]{:S(2)}, u32[]{:S(2)}) collective-permute-start(bf16[128,4096]{1,0:T(8,128)(2,1)} %constant_dynamic-update-slice_fusion), channel_id=1, source_target_pairs={{0,12},{4,0},{8,4},{12,8},{1,13},{5,1},{9,5},{13,9},{2,14},{6,2},{... | collective-permute-start | bytes 3145736 | tf_op jit(solution)/shard_map/ppermute | solution.py:21
  40.6 3.6 %all-to-all-start.1 = ((bf16[8,16,4096]{2,1,0:T(8,128)(2,1)}), bf16[8,16,4096]{2,1,0:T(8,128)(2,1)S(1)}, u32[]{:S(2)}, u32[]{:S(2)}) async-start(bf16[8,16,4096]{2,1,0:T(8,128)(2,1)} %bitcast.53), calls=%async_computation.1 | async-start | bytes 2097152 | tf_op jit(solution)/shard_map/all_to_all | solution.py:42
  44.7 16.5 %collective-permute-done.6.refs_4_.refs_2_ = bf16[128,4096]{1,0:T(8,128)(2,1)S(1)} collective-permute-done((bf16[128,4096]{1,0:T(8,128)(2,1)}, bf16[128,4096]{1,0:T(8,128)(2,1)S(1)}, u32[]{:S(2)}, u32[]{:S(2)}) %collective-permute-start.6) | collective-permute-done | bytes 1048608 | tf_op jit(solution)/shard_map/ppermute | solution.py:21
  63.7 3.8 %pick_rows.7 = bf16[384,4096]{1,0:T(8,128)(2,1)} custom-call(bf16[384,384]{1,0:T(8,128)(2,1)S(1)} %compare_convert_fusion.matrix_ref, bf16[64,4096]{1,0:T(8,128)(2,1)S(1)} %copy-done.20, bf16[128,4096]{1,0:T(8,128)(2,1)S(1)} %collective-permute-done.5.refs_3_.refs_1_, bf16[128,4096]{1,0:T(8,128)(2,1)S(1)} %collective-permute-done.6.refs_4_.refs_2_, ...), custom_call_target="tpu_custom_call" | custom-call | flops 1 | bytes 1 | tf_op jit(solution)/shard_map/pick_rows/pallas_call | solution.py:189
  68.5 3.8 %all-to-all-start.2 = ((bf16[8,48,4096]{2,1,0:T(8,128)(2,1)}), bf16[8,48,4096]{2,1,0:T(8,128)(2,1)S(1)}, u32[]{:S(2)}, u32[]{:S(2)}) async-start(bf16[8,48,4096]{2,1,0:T(8,128)(2,1)} %bitcast.8), calls=%async_computation.2 | async-start | bytes 6291456 | tf_op jit(solution)/shard_map/all_to_all | solution.py:42
  94.6 4.4 %line_scores.1.near_ref = f32[640,512]{1,0:T(8,128)S(1)} custom-call(bf16[512,4096]{1,0:T(8,128)(2,1)S(1)} %copy-done.1, bf16[64,4096]{1,0:T(8,128)(2,1)S(1)} %copy-done.24, bf16[64,4096]{1,0:T(8,128)(2,1)S(1)} %copy-done.27, bf16[64,4096]{1,0:T(8,128)(2,1)S(1)} %copy-done.21, bf16[128,4096]{1,0:T(8,128)(2,1)S(1)} %copy-done.10, ...), custom_call_target="tpu_custom_call" | custom-call | flops 1 | bytes 1 | tf_op jit(solution)/shard_map/line_scores/pallas_call | solution.py:216
  100.1 10.6 %all-to-all-done.2 = bf16[8,48,4096]{2,1,0:T(8,128)(2,1)S(1)} async-done(((bf16[8,48,4096]{2,1,0:T(8,128)(2,1)}), bf16[8,48,4096]{2,1,0:T(8,128)(2,1)S(1)}, u32[]{:S(2)}, u32[]{:S(2)}) %all-to-all-start.2) | async-done | bytes 3145760 | tf_op jit(solution)/shard_map/all_to_all | solution.py:42
  110.6 4.4 %all-to-all-start.3 = ((bf16[8,48,4096]{2,1,0:T(8,128)(2,1)}), bf16[8,48,4096]{2,1,0:T(8,128)(2,1)}, u32[]{:S(2)}, u32[]{:S(2)}) async-start(bf16[8,48,4096]{2,1,0:T(8,128)(2,1)} %bitcast.50), calls=%async_computation.3 | async-start | bytes 6291456 | tf_op jit(solution)/shard_map/all_to_all | solution.py:42
  119.8 3.7 %far_scores.1 = (f32[384,512]{1,0:T(8,128)S(1)}, f32[1,512]{1,0:T(1,128)S(1)}) custom-call(f32[640,512]{1,0:T(8,128)S(1)} %copy-done.30, bf16[512,512]{1,0:T(8,128)(2,1)S(1)} %copy-done.39, bf16[512,4096]{1,0:T(8,128)(2,1)S(1)} %copy-done.2, bf16[384,4096]{1,0:T(8,128)(2,1)S(1)} %bitcast.48), custom_call_target="tpu_custom_call" | custom-call | flops 99999997952 | bytes 100000000 | tf_op jit(solution)/shard_map/far_scores/pallas_call | solution.py:260
  128.4 3.5 %collective-permute-done.9 = f32[8,128]{1,0:T(8,128)S(1)} collective-permute-done((f32[8,128]{1,0:T(8,128)S(1)}, f32[8,128]{1,0:T(8,128)S(1)}, u32[]{:S(2)}, u32[]{:S(2)}) %collective-permute-start.9) | collective-permute-done | bytes 4128 | tf_op jit(solution)/shard_map/ppermute | solution.py:21
  132.1 7.6 %query_side.1 = (bf16[512,4096]{1,0:T(8,128)(2,1)S(1)}, f32[1,4096]{1,0:T(1,128)S(1)}, f32[8,512]{1,0:T(8,128)S(1)}, f32[1,512]{1,0:T(1,128)S(1)}, bf16[512,512]{1,0:T(8,128)(2,1)S(1)}) custom-call(f32[640,512]{1,0:T(8,128)S(1)} %copy-done.31, f32[384,512]{1,0:T(8,128)S(1)} %get-tuple-element.36.far_ref, bf16[512,512]{1,0:T(8,128)(2,1)S(1)} %copy-done.40, ...), custom_call_target="tpu_custom_call" | custom-call | flops 1 | bytes 1 | tf_op jit(solution)/shard_map/query_side/pallas_call | solution.py:326
  157.2 6.1 %passage_side.1 = (bf16[128,4096]{1,0:T(8,128)(2,1)S(1)}, bf16[128,4096]{1,0:T(8,128)(2,1)S(1)}, bf16[128,4096]{1,0:T(8,128)(2,1)S(1)}, bf16[64,4096]{1,0:T(8,128)(2,1)S(1)}, bf16[64,4096]{1,0:T(8,128)(2,1)S(1)}) custom-call(bf16[512,512]{1,0:T(8,128)(2,1)S(1)} %copy-done.50, bf16[512,4096]{1,0:T(8,128)(2,1)S(1)} %copy-done.4, ...), custom_call_target="tpu_custom_call" | custom-call | flops 99999997952 | bytes 100000000 | tf_op jit(solution)/shard_map/passage_side/pallas_call | solution.py:375
  163.6 3.1 %collective-permute-start.20 = (bf16[64,4096]{1,0:T(8,128)(2,1)S(1)}, bf16[64,4096]{1,0:T(8,128)(2,1)S(1)}, u32[]{:S(2)}, u32[]{:S(2)}) collective-permute-start(bf16[64,4096]{1,0:T(8,128)(2,1)S(1)} %get-tuple-element.47), channel_id=1, source_target_pairs={{0,12},{4,0},{8,4},{12,8},{1,13},{5,1},{9,5},{13,9},{2,14},{6,2},{... | collective-permute-start | bytes 1572872 | tf_op jit(solution)/shard_map/ppermute | solution.py:21
  167.4 3.0 %collective-permute-done.10 = f32[32,128]{1,0:T(8,128)S(1)} collective-permute-done((f32[32,128]{1,0:T(8,128)S(1)}, f32[32,128]{1,0:T(8,128)S(1)}, u32[]{:S(2)}, u32[]{:S(2)}) %collective-permute-start.10) | collective-permute-done | bytes 16416 | tf_op jit(solution)/shard_map/ppermute | solution.py:37
  170.4 3.6 %collective-permute-start.11 = (f32[32,128]{1,0:T(8,128)S(1)}, f32[32,128]{1,0:T(8,128)S(1)}, u32[]{:S(2)}, u32[]{:S(2)}) collective-permute-start(f32[32,128]{1,0:T(8,128)S(1)} %add.358), channel_id=1, source_target_pairs={{0,96},{32,64},{64,32},{96,0},{1,97},{33,65},{65,33},{97,1},{2,98}... | collective-permute-start | bytes 49160 | tf_op jit(solution)/shard_map/ppermute | solution.py:37
  175.7 3.0 %collective-permute-done.19.low_ref = bf16[64,4096]{1,0:T(8,128)(2,1)S(1)} collective-permute-done((bf16[64,4096]{1,0:T(8,128)(2,1)S(1)}, bf16[64,4096]{1,0:T(8,128)(2,1)S(1)}, u32[]{:S(2)}, u32[]{:S(2)}) %collective-permute-start.19) | collective-permute-done | bytes 524320 | tf_op jit(solution)/shard_map/ppermute | solution.py:21
  184.1 4.3 %all-to-all-start.4 = ((bf16[8,16,4096]{2,1,0:T(8,128)(2,1)}), bf16[8,16,4096]{2,1,0:T(8,128)(2,1)S(1)}, u32[]{:S(2)}, u32[]{:S(2)}) async-start(bf16[8,16,4096]{2,1,0:T(8,128)(2,1)} %bitcast.31), calls=%async_computation.5 | async-start | bytes 2097152 | tf_op jit(solution)/shard_map/all_to_all | solution.py:42
  190.5 3.4 %collective-permute-done.22 = f32[32,128]{1,0:T(8,128)S(1)} collective-permute-done((f32[32,128]{1,0:T(8,128)S(1)}, f32[32,128]{1,0:T(8,128)S(1)}, u32[]{:S(2)}, u32[]{:S(2)}) %collective-permute-start.22) | collective-permute-done | bytes 16416 | tf_op jit(solution)/shard_map/ppermute | solution.py:37
  195.1 3.8 %collective-permute-done.23 = f32[32,128]{1,0:T(8,128)S(1)} collective-permute-done((f32[32,128]{1,0:T(8,128)S(1)}, f32[32,128]{1,0:T(8,128)S(1)}, u32[]{:S(2)}, u32[]{:S(2)}) %collective-permute-start.23) | collective-permute-done | bytes 16416 | tf_op jit(solution)/shard_map/ppermute | solution.py:37
  200.1 4.0 %finish.2 = bf16[128,4096]{1,0:T(8,128)(2,1)} custom-call(bf16[128,4096]{1,0:T(8,128)(2,1)S(1)} %copy-done.33, f32[1,4096]{1,0:T(1,128)S(1)} %bitcast.57, bf16[128,4096]{1,0:T(8,128)(2,1)S(1)} %copy-done.43), custom_call_target="tpu_custom_call" | custom-call | flops 1 | bytes 1 | tf_op jit(solution)/shard_map/finish/pallas_call | solution.py:171
  204.7 3.1 %collective-permute-done.26 = f32[32,128]{1,0:T(8,128)S(1)} collective-permute-done((f32[32,128]{1,0:T(8,128)S(1)}, f32[32,128]{1,0:T(8,128)S(1)}, u32[]{:S(2)}, u32[]{:S(2)}) %collective-permute-start.26) | collective-permute-done | bytes 16416 | tf_op jit(solution)/shard_map/ppermute | solution.py:37
  210.9 6.9 %finish.3 = bf16[128,4096]{1,0:T(8,128)(2,1)} custom-call(bf16[128,4096]{1,0:T(8,128)(2,1)S(1)} %copy-done.38, f32[1,4096]{1,0:T(1,128)S(1)} %bitcast.58, bf16[128,4096]{1,0:T(8,128)(2,1)S(1)} %copy-done.45, bf16[128,4096]{1,0:T(8,128)(2,1)} %collective-permute-done.24.refs_1_, bf16[128,4096]{1,0:T(8,128)(2,1)} %collective-permute-done.25.refs_2_, ...), custom_call_target="tpu_custom_call" | custom-call | flops 1 | bytes 1 | tf_op jit(solution)/shard_map/finish/pallas_call | solution.py:171
  (279 shorter events, 87.5 us)
Async XLA Ops:
  10.0 21.1 %collective-permute-start.1 = (bf16[64,4096]{1,0:T(8,128)(2,1)S(1)}, bf16[64,4096]{1,0:T(8,128)(2,1)S(1)}, u32[]{:S(2)}, u32[]{:S(2)}) collective-permute-start(bf16[64,4096]{1,0:T(8,128)(2,1)S(1)} %get-tuple-element.30.refs_1_), channel_id=1, source_target_pairs={{0,4},{4,8},{8,12},{12,0},{1,5},{5,9},{9,13},{13,1},{2,6},{6,10},{... | collective-permute-start | bytes 1572872 | tf_op jit(solution)/shard_map/ppermute | solution.py:21
  11.8 20.3 %collective-permute-start = (bf16[64,4096]{1,0:T(8,128)(2,1)S(1)}, bf16[64,4096]{1,0:T(8,128)(2,1)S(1)}, u32[]{:S(2)}, u32[]{:S(2)}) collective-permute-start(bf16[64,4096]{1,0:T(8,128)(2,1)S(1)} %get-tuple-element.31.refs_0_), channel_id=1, source_target_pairs={{0,12},{4,0},{8,4},{12,8},{1,13},{5,1},{9,5},{13,9},{2,14},{6,2},{... | collective-permute-start | bytes 1572872 | tf_op jit(solution)/shard_map/ppermute | solution.py:21
  15.5 15.5 %all-to-all-start = ((s32[32,1,16]{2,1,0:T(1,128)}), s32[32,1,16]{2,1,0:T(1,128)S(1)}, u32[]{:S(2)}, u32[]{:S(2)}) async-start(s32[32,1,16]{2,1,0:T(1,128)} %bitcast), calls=%async_computation | async-start | bytes 32768 | tf_op jit(solution)/shard_map/all_to_all | solution.py:451
  23.7 61.4 %all-gather.2.cloned.1.call-start = ((), (), s32[]{:S(2)}) async-start(), calls=%async_computation.6 | async-start | bytes 5242880 | tf_op jit(solution)/shard_map/all_gather | solution.py:476
  34.8 26.4 %collective-permute-start.6 = (bf16[128,4096]{1,0:T(8,128)(2,1)}, bf16[128,4096]{1,0:T(8,128)(2,1)S(1)}, u32[]{:S(2)}, u32[]{:S(2)}) collective-permute-start(bf16[128,4096]{1,0:T(8,128)(2,1)} %constant_dynamic-update-slice_fusion.2), channel_id=1, source_target_pairs={{0,4},{4,8},{8,12},{12,0},{1,5},{5,9},{9,13},{13,1},{2,6},{6,10},{... | collective-permute-start | bytes 3145736 | tf_op jit(solution)/shard_map/ppermute | solution.py:21
  35.2 26.0 %collective-permute-start.5 = (bf16[128,4096]{1,0:T(8,128)(2,1)}, bf16[128,4096]{1,0:T(8,128)(2,1)S(1)}, u32[]{:S(2)}, u32[]{:S(2)}) collective-permute-start(bf16[128,4096]{1,0:T(8,128)(2,1)} %constant_dynamic-update-slice_fusion), channel_id=1, source_target_pairs={{0,12},{4,0},{8,4},{12,8},{1,13},{5,1},{9,5},{13,9},{2,14},{6,2},{... | collective-permute-start | bytes 3145736 | tf_op jit(solution)/shard_map/ppermute | solution.py:21
  40.6 26.9 %all-to-all-start.1 = ((bf16[8,16,4096]{2,1,0:T(8,128)(2,1)}), bf16[8,16,4096]{2,1,0:T(8,128)(2,1)S(1)}, u32[]{:S(2)}, u32[]{:S(2)}) async-start(bf16[8,16,4096]{2,1,0:T(8,128)(2,1)} %bitcast.53), calls=%async_computation.1 | async-start | bytes 2097152 | tf_op jit(solution)/shard_map/all_to_all | solution.py:42
  68.5 42.1 %all-to-all-start.2 = ((bf16[8,48,4096]{2,1,0:T(8,128)(2,1)}), bf16[8,48,4096]{2,1,0:T(8,128)(2,1)S(1)}, u32[]{:S(2)}, u32[]{:S(2)}) async-start(bf16[8,48,4096]{2,1,0:T(8,128)(2,1)} %bitcast.8), calls=%async_computation.2 | async-start | bytes 6291456 | tf_op jit(solution)/shard_map/all_to_all | solution.py:42
  72.6 7.0 %collective-permute-start.2 = (s32[1,128]{1,0:T(1,128)S(1)}, s32[1,128]{1,0:T(1,128)S(1)}, u32[]{:S(2)}, u32[]{:S(2)}) collective-permute-start(s32[1,128]{1,0:T(1,128)S(1)} %broadcast_in_dim.373), channel_id=1, source_target_pairs={{0,1},{1,2},{2,3},{3,0},{4,5},{5,6},{6,7},{7,4},{8,9},{9,10},{10,1... | collective-permute-start | bytes 1544 | tf_op jit(solution)/shard_map/ppermute | solution.py:21
  73.3 7.7 %collective-permute-start.3 = (s32[1,128]{1,0:T(1,128)S(1)}, s32[1,128]{1,0:T(1,128)S(1)}, u32[]{:S(2)}, u32[]{:S(2)}) collective-permute-start(s32[1,128]{1,0:T(1,128)S(1)} %broadcast_in_dim.378), channel_id=1, source_target_pairs={{0,2},{1,3},{2,0},{3,1},{4,6},{5,7},{6,4},{7,5},{8,10},{9,11},{10,... | collective-permute-start | bytes 1544 | tf_op jit(solution)/shard_map/ppermute | solution.py:21
  75.4 6.5 %collective-permute-start.4 = (s32[1,128]{1,0:T(1,128)S(1)}, s32[1,128]{1,0:T(1,128)S(1)}, u32[]{:S(2)}, u32[]{:S(2)}) collective-permute-start(s32[1,128]{1,0:T(1,128)S(1)} %broadcast_in_dim.383), channel_id=1, source_target_pairs={{0,3},{1,0},{2,1},{3,2},{4,7},{5,4},{6,5},{7,6},{8,11},{9,8},{10,9... | collective-permute-start | bytes 1544 | tf_op jit(solution)/shard_map/ppermute | solution.py:21
  110.6 44.4 %all-to-all-start.3 = ((bf16[8,48,4096]{2,1,0:T(8,128)(2,1)}), bf16[8,48,4096]{2,1,0:T(8,128)(2,1)}, u32[]{:S(2)}, u32[]{:S(2)}) async-start(bf16[8,48,4096]{2,1,0:T(8,128)(2,1)} %bitcast.50), calls=%async_computation.3 | async-start | bytes 6291456 | tf_op jit(solution)/shard_map/all_to_all | solution.py:42
  115.1 83.8 %reduce-scatter.2.cloned.1.call-start = ((), (), s32[]{:S(2)}) async-start(), calls=%async_computation.7 | async-start | bytes 5242880 | tf_op jit(solution)/shard_map/reduce_scatter | solution.py:513
  142.8 6.5 %collective-permute-start.12 = (f32[1,64]{1,0:T(1,128)S(1)}, f32[1,64]{1,0:T(1,128)S(1)}, u32[]{:S(2)}, u32[]{:S(2)}) collective-permute-start(f32[1,64]{1,0:T(1,128)S(1)} %bitcast.85), channel_id=1, source_target_pairs={{0,16},{16,0},{32,48},{48,32},{64,80},{80,64},{96,112},{112,96},{1... | collective-permute-start | bytes 776 | tf_op jit(solution)/shard_map/ppermute | solution.py:56
  142.9 8.1 %collective-permute-start.13 = (f32[1,64]{1,0:T(1,128)S(1)}, f32[1,64]{1,0:T(1,128)S(1)}, u32[]{:S(2)}, u32[]{:S(2)}) collective-permute-start(f32[1,64]{1,0:T(1,128)S(1)} %bitcast.84), channel_id=1, source_target_pairs={{0,32},{16,48},{32,64},{48,80},{64,96},{80,112},{96,0},{112,16},{1... | collective-permute-start | bytes 776 | tf_op jit(solution)/shard_map/ppermute | solution.py:56
  144.9 8.5 %collective-permute-start.14 = (f32[1,64]{1,0:T(1,128)S(1)}, f32[1,64]{1,0:T(1,128)S(1)}, u32[]{:S(2)}, u32[]{:S(2)}) collective-permute-start(f32[1,64]{1,0:T(1,128)S(1)} %bitcast.81), channel_id=1, source_target_pairs={{0,48},{16,32},{32,80},{48,64},{64,112},{80,96},{96,16},{112,0},{1... | collective-permute-start | bytes 776 | tf_op jit(solution)/shard_map/ppermute | solution.py:56
  146.1 7.4 %collective-permute-start.15 = (f32[1,64]{1,0:T(1,128)S(1)}, f32[1,64]{1,0:T(1,128)S(1)}, u32[]{:S(2)}, u32[]{:S(2)}) collective-permute-start(f32[1,64]{1,0:T(1,128)S(1)} %bitcast.80), channel_id=1, source_target_pairs={{0,64},{16,80},{32,96},{48,112},{64,0},{80,16},{96,32},{112,48},{1... | collective-permute-start | bytes 776 | tf_op jit(solution)/shard_map/ppermute | solution.py:56
  147.6 5.9 %collective-permute-start.16 = (f32[1,64]{1,0:T(1,128)S(1)}, f32[1,64]{1,0:T(1,128)S(1)}, u32[]{:S(2)}, u32[]{:S(2)}) collective-permute-start(f32[1,64]{1,0:T(1,128)S(1)} %bitcast.78), channel_id=1, source_target_pairs={{0,80},{16,64},{32,112},{48,96},{64,16},{80,0},{96,48},{112,32},{1... | collective-permute-start | bytes 776 | tf_op jit(solution)/shard_map/ppermute | solution.py:56
  163.4 15.3 %collective-permute-start.19 = (bf16[64,4096]{1,0:T(8,128)(2,1)S(1)}, bf16[64,4096]{1,0:T(8,128)(2,1)S(1)}, u32[]{:S(2)}, u32[]{:S(2)}) collective-permute-start(bf16[64,4096]{1,0:T(8,128)(2,1)S(1)} %get-tuple-element.42), channel_id=1, source_target_pairs={{0,4},{4,8},{8,12},{12,0},{1,5},{5,9},{9,13},{13,1},{2,6},{6,10},{... | collective-permute-start | bytes 1572872 | tf_op jit(solution)/shard_map/ppermute | solution.py:21
  163.6 15.1 %collective-permute-start.20 = (bf16[64,4096]{1,0:T(8,128)(2,1)S(1)}, bf16[64,4096]{1,0:T(8,128)(2,1)S(1)}, u32[]{:S(2)}, u32[]{:S(2)}) collective-permute-start(bf16[64,4096]{1,0:T(8,128)(2,1)S(1)} %get-tuple-element.47), channel_id=1, source_target_pairs={{0,12},{4,0},{8,4},{12,8},{1,13},{5,1},{9,5},{13,9},{2,14},{6,2},{... | collective-permute-start | bytes 1572872 | tf_op jit(solution)/shard_map/ppermute | solution.py:21
  180.8 28.9 %collective-permute-start.24 = (bf16[128,4096]{1,0:T(8,128)(2,1)}, bf16[128,4096]{1,0:T(8,128)(2,1)}, u32[]{:S(2)}, u32[]{:S(2)}) collective-permute-start(bf16[128,4096]{1,0:T(8,128)(2,1)} %get-tuple-element.48), channel_id=1, source_target_pairs={{0,4},{4,8},{8,12},{12,0},{1,5},{5,9},{9,13},{13,1},{2,6},{6,10},{... | collective-permute-start | bytes 3145736 | tf_op jit(solution)/shard_map/ppermute | solution.py:21
  181.6 28.0 %collective-permute-start.25 = (bf16[128,4096]{1,0:T(8,128)(2,1)}, bf16[128,4096]{1,0:T(8,128)(2,1)}, u32[]{:S(2)}, u32[]{:S(2)}) collective-permute-start(bf16[128,4096]{1,0:T(8,128)(2,1)} %get-tuple-element.53), channel_id=1, source_target_pairs={{0,12},{4,0},{8,4},{12,8},{1,13},{5,1},{9,5},{13,9},{2,14},{6,2},{... | collective-permute-start | bytes 3145736 | tf_op jit(solution)/shard_map/ppermute | solution.py:21
  184.1 25.5 %all-to-all-start.4 = ((bf16[8,16,4096]{2,1,0:T(8,128)(2,1)}), bf16[8,16,4096]{2,1,0:T(8,128)(2,1)S(1)}, u32[]{:S(2)}, u32[]{:S(2)}) async-start(bf16[8,16,4096]{2,1,0:T(8,128)(2,1)} %bitcast.31), calls=%async_computation.5 | async-start | bytes 2097152 | tf_op jit(solution)/shard_map/all_to_all | solution.py:42
  207.8 10.1 %collective-permute-start.27 = (f32[32,128]{1,0:T(8,128)S(1)}, f32[32,128]{1,0:T(8,128)S(1)}, u32[]{:S(2)}, u32[]{:S(2)}) collective-permute-start(f32[32,128]{1,0:T(8,128)S(1)} %add.387), channel_id=1, source_target_pairs={{0,12},{4,8},{8,4},{12,0},{1,13},{5,9},{9,5},{13,1},{2,14},{6,10},... | collective-permute-start | bytes 49160 | tf_op jit(solution)/shard_map/ppermute | solution.py:37
  (79 other events, 729.9 us)
Sparse Core Ops, SparseCore 0:
  34.9 44.7 all-gather.1
  153.4 43.6 reduce-scatter.1

commit v8 on v7

--- a/solution.py
+++ b/solution.py
@@ -100,8 +100,8 @@
     return pl.BlockSpec(shape, lambda i: (0,) * len(shape))
 
 
-def columns(rows, width):
-    return pl.BlockSpec((rows, tile(width)), lambda i: (0, i))
+def columns(rows, width, tiles=1):
+    return pl.BlockSpec((rows, tiles * tile(width)), lambda i: (0, i))
 
 
 def joined(refs):
@@ -148,7 +148,7 @@
 
 def finish(hidden, gain, terms, put=None, arrived=None, scale=1.0):
     rows, width = hidden.shape
-    step = rows // 8
+    step = rows // 2
     product = () if put is None else (put, arrived)
 
     def body(hidden_ref, gain_ref, *refs):
@@ -174,7 +174,7 @@
         in_specs=[block, whole((1, width))] + [block] * len(terms) + extra,
         out_specs=block,
         out_shape=jax.ShapeDtypeStruct((rows, width), jnp.bfloat16),
-        compiler_params=params(20),
+        compiler_params=params(28),
         cost_estimate=SMALL,
         name="finish",
     )(hidden, gain, *terms, *product)
@@ -188,9 +188,9 @@
 
     return pl.pallas_call(
         body,
-        grid=(width // tile(width),),
-        in_specs=[whole(matrix.shape)] + [columns(s.shape[0], width) for s in sources],
-        out_specs=columns(matrix.shape[0], width),
+        grid=(width // (2 * tile(width)),),
+        in_specs=[whole(matrix.shape)] + [columns(s.shape[0], width, 2) for s in sources],
+        out_specs=columns(matrix.shape[0], width, 2),
         out_shape=jax.ShapeDtypeStruct((matrix.shape[0], width), jnp.bfloat16),
         compiler_params=params(16),
         cost_estimate=SMALL,

time: 226 us -> 222 us (0.982)
  Pallas kernels: 46.5 us -> 39.7 us
    pallas_call x2, Pallas kernels: 10.9 us -> 5.71 us  [finish(): pl.pallas_call(body, grid=(rows // step,), in_specs=[block, whole((1, wid...]
  transfers between devices with their start and end apart: 35 -> 35, of which waited for: 14 -> 14; matrix products, arithmetic and copies ran while one was open for 7% -> 7% of each run, Pallas kernels for 20% -> 17%
where the time goes in v8:
time: 222 us; the launch traced here: 221 us
  starting transfers between devices  64 us (29%)
  waiting for transfers between devices  59.2 us (27%)
  Pallas kernels  39.7 us (18%)
  local copies, waits for them, and re-layouts  34.3 us (15%)
  between operations  15.1 us (7%)
  other arithmetic  8.6 us (4%)
    unnamed x139, local copies, waits for them, and re-layouts  28.4 us
    ppermute x14, waiting for transfers between devices, shift(): lax.ppermute(value, axis, [(i, (i + step) % RING) for i in range(RING)])  24.9 us
    ppermute x14, starting transfers between devices, shift(): lax.ppermute(value, axis, [(i, (i + step) % RING) for i in range(RING)])  20.3 us
    ppermute x7, waiting for transfers between devices, pair_sum(): return value + lax.ppermute(value, axis, pairs)  16.6 us
    all_to_all x4, starting transfers between devices, group_rows(): return lax.all_to_all(blocks, GROUPS, 0, 0, tiled=True).reshape(rows.shape)  16.1 us
    all_to_all x4, waiting for transfers between devices, group_rows(): return lax.all_to_all(blocks, GROUPS, 0, 0, tiled=True).reshape(rows.shape)  10.8 us
    ppermute x7, starting transfers between devices, group_table(): lax.ppermute(row, GROUPS, [(z * 2 + c, (z + z_step) % z_count * 2 + (c ^...  10.4 us
    ppermute x7, starting transfers between devices, pair_sum(): return value + lax.ppermute(value, axis, pairs)  8.76 us
  transfers between devices with their start and end apart: 35, of which 14 were waited for; matrix products, arithmetic and copies ran while one was open for 7% of the time, Pallas kernels for 17%

profile of v8, /device:TPU:0, one launch (start us, length us, event | category | flops | bytes accessed | tf_op | source)
XLA Modules:
  0.0 220.8 jit_solution(4793901326737171647)
XLA Ops:
  15.5 8.2 %all-to-all-start = ((s32[32,1,16]{2,1,0:T(1,128)}), s32[32,1,16]{2,1,0:T(1,128)S(1)}, u32[]{:S(2)}, u32[]{:S(2)}) async-start(s32[32,1,16]{2,1,0:T(1,128)} %bitcast), calls=%async_computation | async-start | bytes 32768 | tf_op jit(solution)/shard_map/all_to_all | solution.py:451
  25.4 5.5 %all-to-all-done = s32[32,1,16]{2,1,0:T(1,128)S(1)} async-done(((s32[32,1,16]{2,1,0:T(1,128)}), s32[32,1,16]{2,1,0:T(1,128)S(1)}, u32[]{:S(2)}, u32[]{:S(2)}) %all-to-all-start) | async-done | bytes 2080 | tf_op jit(solution)/shard_map/all_to_all | solution.py:451
  35.2 2.9 %collective-permute-start.5 = (bf16[128,4096]{1,0:T(8,128)(2,1)}, bf16[128,4096]{1,0:T(8,128)(2,1)S(1)}, u32[]{:S(2)}, u32[]{:S(2)}) collective-permute-start(bf16[128,4096]{1,0:T(8,128)(2,1)} %constant_dynamic-update-slice_fusion), channel_id=1, source_target_pairs={{0,12},{4,0},{8,4},{12,8},{1,13},{5,1},{9,5},{13,9},{2,14},{6,2},{... | collective-permute-start | bytes 3145736 | tf_op jit(solution)/shard_map/ppermute | solution.py:21
  40.3 3.6 %all-to-all-start.1 = ((bf16[8,16,4096]{2,1,0:T(8,128)(2,1)}), bf16[8,16,4096]{2,1,0:T(8,128)(2,1)S(1)}, u32[]{:S(2)}, u32[]{:S(2)}) async-start(bf16[8,16,4096]{2,1,0:T(8,128)(2,1)} %bitcast.53), calls=%async_computation.1 | async-start | bytes 2097152 | tf_op jit(solution)/shard_map/all_to_all | solution.py:42
  44.4 16.8 %collective-permute-done.6.refs_4_.refs_2_ = bf16[128,4096]{1,0:T(8,128)(2,1)S(1)} collective-permute-done((bf16[128,4096]{1,0:T(8,128)(2,1)}, bf16[128,4096]{1,0:T(8,128)(2,1)S(1)}, u32[]{:S(2)}, u32[]{:S(2)}) %collective-permute-start.6) | collective-permute-done | bytes 1048608 | tf_op jit(solution)/shard_map/ppermute | solution.py:21
  63.7 3.4 %pick_rows.7 = bf16[384,4096]{1,0:T(8,128)(2,1)} custom-call(bf16[384,384]{1,0:T(8,128)(2,1)S(1)} %compare_convert_fusion.matrix_ref, bf16[64,4096]{1,0:T(8,128)(2,1)S(1)} %copy-done.20, bf16[128,4096]{1,0:T(8,128)(2,1)S(1)} %collective-permute-done.5.refs_3_.refs_1_, bf16[128,4096]{1,0:T(8,128)(2,1)S(1)} %collective-permute-done.6.refs_4_.refs_2_, ...), custom_call_target="tpu_custom_call" | custom-call | flops 1 | bytes 1 | tf_op jit(solution)/shard_map/pick_rows/pallas_call | solution.py:189
  68.1 3.8 %all-to-all-start.2 = ((bf16[8,48,4096]{2,1,0:T(8,128)(2,1)}), bf16[8,48,4096]{2,1,0:T(8,128)(2,1)S(1)}, u32[]{:S(2)}, u32[]{:S(2)}) async-start(bf16[8,48,4096]{2,1,0:T(8,128)(2,1)} %bitcast.8), calls=%async_computation.2 | async-start | bytes 6291456 | tf_op jit(solution)/shard_map/all_to_all | solution.py:42
  94.0 4.3 %line_scores.1.near_ref = f32[640,512]{1,0:T(8,128)S(1)} custom-call(bf16[512,4096]{1,0:T(8,128)(2,1)S(1)} %copy-done.1, bf16[64,4096]{1,0:T(8,128)(2,1)S(1)} %copy-done.24, bf16[64,4096]{1,0:T(8,128)(2,1)S(1)} %copy-done.27, bf16[64,4096]{1,0:T(8,128)(2,1)S(1)} %copy-done.21, bf16[128,4096]{1,0:T(8,128)(2,1)S(1)} %copy-done.10, ...), custom_call_target="tpu_custom_call" | custom-call | flops 1 | bytes 1 | tf_op jit(solution)/shard_map/line_scores/pallas_call | solution.py:216
  99.4 10.8 %all-to-all-done.2 = bf16[8,48,4096]{2,1,0:T(8,128)(2,1)S(1)} async-done(((bf16[8,48,4096]{2,1,0:T(8,128)(2,1)}), bf16[8,48,4096]{2,1,0:T(8,128)(2,1)S(1)}, u32[]{:S(2)}, u32[]{:S(2)}) %all-to-all-start.2) | async-done | bytes 3145760 | tf_op jit(solution)/shard_map/all_to_all | solution.py:42
  110.2 4.4 %all-to-all-start.3 = ((bf16[8,48,4096]{2,1,0:T(8,128)(2,1)}), bf16[8,48,4096]{2,1,0:T(8,128)(2,1)}, u32[]{:S(2)}, u32[]{:S(2)}) async-start(bf16[8,48,4096]{2,1,0:T(8,128)(2,1)} %bitcast.50), calls=%async_computation.3 | async-start | bytes 6291456 | tf_op jit(solution)/shard_map/all_to_all | solution.py:42
  119.4 3.7 %far_scores.1 = (f32[384,512]{1,0:T(8,128)S(1)}, f32[1,512]{1,0:T(1,128)S(1)}) custom-call(f32[640,512]{1,0:T(8,128)S(1)} %copy-done.30, bf16[512,512]{1,0:T(8,128)(2,1)S(1)} %copy-done.39, bf16[512,4096]{1,0:T(8,128)(2,1)S(1)} %copy-done.2, bf16[384,4096]{1,0:T(8,128)(2,1)S(1)} %bitcast.48), custom_call_target="tpu_custom_call" | custom-call | flops 99999997952 | bytes 100000000 | tf_op jit(solution)/shard_map/far_scores/pallas_call | solution.py:260
  123.7 2.7 %collective-permute-start.8 = (f32[8,128]{1,0:T(8,128)S(1)}, f32[8,128]{1,0:T(8,128)S(1)}, u32[]{:S(2)}, u32[]{:S(2)}) collective-permute-start(f32[8,128]{1,0:T(8,128)S(1)} %pad_maximum_fusion.1), channel_id=1, source_target_pairs={{0,3},{1,0},{2,1},{3,2},{4,7},{5,4},{6,5},{7,6},{8,11},{9,8},{10,9... | collective-permute-start | bytes 12296 | tf_op jit(solution)/shard_map/ppermute | solution.py:21
  128.0 3.5 %collective-permute-done.9 = f32[8,128]{1,0:T(8,128)S(1)} collective-permute-done((f32[8,128]{1,0:T(8,128)S(1)}, f32[8,128]{1,0:T(8,128)S(1)}, u32[]{:S(2)}, u32[]{:S(2)}) %collective-permute-start.9) | collective-permute-done | bytes 4128 | tf_op jit(solution)/shard_map/ppermute | solution.py:21
  131.8 7.6 %query_side.1 = (bf16[512,4096]{1,0:T(8,128)(2,1)S(1)}, f32[1,4096]{1,0:T(1,128)S(1)}, f32[8,512]{1,0:T(8,128)S(1)}, f32[1,512]{1,0:T(1,128)S(1)}, bf16[512,512]{1,0:T(8,128)(2,1)S(1)}) custom-call(f32[640,512]{1,0:T(8,128)S(1)} %copy-done.31, f32[384,512]{1,0:T(8,128)S(1)} %get-tuple-element.36.far_ref, bf16[512,512]{1,0:T(8,128)(2,1)S(1)} %copy-done.40, ...), custom_call_target="tpu_custom_call" | custom-call | flops 1 | bytes 1 | tf_op jit(solution)/shard_map/query_side/pallas_call | solution.py:326
  156.8 6.1 %passage_side.1 = (bf16[128,4096]{1,0:T(8,128)(2,1)S(1)}, bf16[128,4096]{1,0:T(8,128)(2,1)S(1)}, bf16[128,4096]{1,0:T(8,128)(2,1)S(1)}, bf16[64,4096]{1,0:T(8,128)(2,1)S(1)}, bf16[64,4096]{1,0:T(8,128)(2,1)S(1)}) custom-call(bf16[512,512]{1,0:T(8,128)(2,1)S(1)} %copy-done.50, bf16[512,4096]{1,0:T(8,128)(2,1)S(1)} %copy-done.4, ...), custom_call_target="tpu_custom_call" | custom-call | flops 99999997952 | bytes 100000000 | tf_op jit(solution)/shard_map/passage_side/pallas_call | solution.py:375
  163.2 3.1 %collective-permute-start.20 = (bf16[64,4096]{1,0:T(8,128)(2,1)S(1)}, bf16[64,4096]{1,0:T(8,128)(2,1)S(1)}, u32[]{:S(2)}, u32[]{:S(2)}) collective-permute-start(bf16[64,4096]{1,0:T(8,128)(2,1)S(1)} %get-tuple-element.47), channel_id=1, source_target_pairs={{0,12},{4,0},{8,4},{12,8},{1,13},{5,1},{9,5},{13,9},{2,14},{6,2},{... | collective-permute-start | bytes 1572872 | tf_op jit(solution)/shard_map/ppermute | solution.py:21
  167.0 3.0 %collective-permute-done.10 = f32[32,128]{1,0:T(8,128)S(1)} collective-permute-done((f32[32,128]{1,0:T(8,128)S(1)}, f32[32,128]{1,0:T(8,128)S(1)}, u32[]{:S(2)}, u32[]{:S(2)}) %collective-permute-start.10) | collective-permute-done | bytes 16416 | tf_op jit(solution)/shard_map/ppermute | solution.py:37
  170.0 3.6 %collective-permute-start.11 = (f32[32,128]{1,0:T(8,128)S(1)}, f32[32,128]{1,0:T(8,128)S(1)}, u32[]{:S(2)}, u32[]{:S(2)}) collective-permute-start(f32[32,128]{1,0:T(8,128)S(1)} %add.358), channel_id=1, source_target_pairs={{0,96},{32,64},{64,32},{96,0},{1,97},{33,65},{65,33},{97,1},{2,98}... | collective-permute-start | bytes 49160 | tf_op jit(solution)/shard_map/ppermute | solution.py:37
  175.3 3.0 %collective-permute-done.19.low_ref = bf16[64,4096]{1,0:T(8,128)(2,1)S(1)} collective-permute-done((bf16[64,4096]{1,0:T(8,128)(2,1)S(1)}, bf16[64,4096]{1,0:T(8,128)(2,1)S(1)}, u32[]{:S(2)}, u32[]{:S(2)}) %collective-permute-start.19) | collective-permute-done | bytes 524320 | tf_op jit(solution)/shard_map/ppermute | solution.py:21
  183.7 4.3 %all-to-all-start.4 = ((bf16[8,16,4096]{2,1,0:T(8,128)(2,1)}), bf16[8,16,4096]{2,1,0:T(8,128)(2,1)S(1)}, u32[]{:S(2)}, u32[]{:S(2)}) async-start(bf16[8,16,4096]{2,1,0:T(8,128)(2,1)} %bitcast.31), calls=%async_computation.5 | async-start | bytes 2097152 | tf_op jit(solution)/shard_map/all_to_all | solution.py:42
  190.1 3.4 %collective-permute-done.22 = f32[32,128]{1,0:T(8,128)S(1)} collective-permute-done((f32[32,128]{1,0:T(8,128)S(1)}, f32[32,128]{1,0:T(8,128)S(1)}, u32[]{:S(2)}, u32[]{:S(2)}) %collective-permute-start.22) | collective-permute-done | bytes 16416 | tf_op jit(solution)/shard_map/ppermute | solution.py:37
  194.7 3.7 %collective-permute-done.23 = f32[32,128]{1,0:T(8,128)S(1)} collective-permute-done((f32[32,128]{1,0:T(8,128)S(1)}, f32[32,128]{1,0:T(8,128)S(1)}, u32[]{:S(2)}, u32[]{:S(2)}) %collective-permute-start.23) | collective-permute-done | bytes 16416 | tf_op jit(solution)/shard_map/ppermute | solution.py:37
  202.2 3.8 %collective-permute-done.26 = f32[32,128]{1,0:T(8,128)S(1)} collective-permute-done((f32[32,128]{1,0:T(8,128)S(1)}, f32[32,128]{1,0:T(8,128)S(1)}, u32[]{:S(2)}, u32[]{:S(2)}) %collective-permute-start.26) | collective-permute-done | bytes 16416 | tf_op jit(solution)/shard_map/ppermute | solution.py:37
  209.6 3.8 %finish.3 = bf16[128,4096]{1,0:T(8,128)(2,1)} custom-call(bf16[128,4096]{1,0:T(8,128)(2,1)S(1)} %copy-done.38, f32[1,4096]{1,0:T(1,128)S(1)} %bitcast.58, bf16[128,4096]{1,0:T(8,128)(2,1)S(1)} %copy-done.45, bf16[128,4096]{1,0:T(8,128)(2,1)} %collective-permute-done.24.refs_1_, bf16[128,4096]{1,0:T(8,128)(2,1)} %collective-permute-done.25.refs_2_, ...), custom_call_target="tpu_custom_call" | custom-call | flops 1 | bytes 1 | tf_op jit(solution)/shard_map/finish/pallas_call | solution.py:171
  (279 shorter events, 86.6 us)
Async XLA Ops:
  10.0 21.1 %collective-permute-start.1 = (bf16[64,4096]{1,0:T(8,128)(2,1)S(1)}, bf16[64,4096]{1,0:T(8,128)(2,1)S(1)}, u32[]{:S(2)}, u32[]{:S(2)}) collective-permute-start(bf16[64,4096]{1,0:T(8,128)(2,1)S(1)} %get-tuple-element.30.refs_1_), channel_id=1, source_target_pairs={{0,4},{4,8},{8,12},{12,0},{1,5},{5,9},{9,13},{13,1},{2,6},{6,10},{... | collective-permute-start | bytes 1572872 | tf_op jit(solution)/shard_map/ppermute | solution.py:21
  11.8 20.3 %collective-permute-start = (bf16[64,4096]{1,0:T(8,128)(2,1)S(1)}, bf16[64,4096]{1,0:T(8,128)(2,1)S(1)}, u32[]{:S(2)}, u32[]{:S(2)}) collective-permute-start(bf16[64,4096]{1,0:T(8,128)(2,1)S(1)} %get-tuple-element.31.refs_0_), channel_id=1, source_target_pairs={{0,12},{4,0},{8,4},{12,8},{1,13},{5,1},{9,5},{13,9},{2,14},{6,2},{... | collective-permute-start | bytes 1572872 | tf_op jit(solution)/shard_map/ppermute | solution.py:21
  15.5 15.5 %all-to-all-start = ((s32[32,1,16]{2,1,0:T(1,128)}), s32[32,1,16]{2,1,0:T(1,128)S(1)}, u32[]{:S(2)}, u32[]{:S(2)}) async-start(s32[32,1,16]{2,1,0:T(1,128)} %bitcast), calls=%async_computation | async-start | bytes 32768 | tf_op jit(solution)/shard_map/all_to_all | solution.py:451
  23.7 61.0 %all-gather.2.cloned.1.call-start = ((), (), s32[]{:S(2)}) async-start(), calls=%async_computation.6 | async-start | bytes 5242880 | tf_op jit(solution)/shard_map/all_gather | solution.py:476
  34.8 26.4 %collective-permute-start.6 = (bf16[128,4096]{1,0:T(8,128)(2,1)}, bf16[128,4096]{1,0:T(8,128)(2,1)S(1)}, u32[]{:S(2)}, u32[]{:S(2)}) collective-permute-start(bf16[128,4096]{1,0:T(8,128)(2,1)} %constant_dynamic-update-slice_fusion.2), channel_id=1, source_target_pairs={{0,4},{4,8},{8,12},{12,0},{1,5},{5,9},{9,13},{13,1},{2,6},{6,10},{... | collective-permute-start | bytes 3145736 | tf_op jit(solution)/shard_map/ppermute | solution.py:21
  35.2 26.0 %collective-permute-start.5 = (bf16[128,4096]{1,0:T(8,128)(2,1)}, bf16[128,4096]{1,0:T(8,128)(2,1)S(1)}, u32[]{:S(2)}, u32[]{:S(2)}) collective-permute-start(bf16[128,4096]{1,0:T(8,128)(2,1)} %constant_dynamic-update-slice_fusion), channel_id=1, source_target_pairs={{0,12},{4,0},{8,4},{12,8},{1,13},{5,1},{9,5},{13,9},{2,14},{6,2},{... | collective-permute-start | bytes 3145736 | tf_op jit(solution)/shard_map/ppermute | solution.py:21
  40.3 26.8 %all-to-all-start.1 = ((bf16[8,16,4096]{2,1,0:T(8,128)(2,1)}), bf16[8,16,4096]{2,1,0:T(8,128)(2,1)S(1)}, u32[]{:S(2)}, u32[]{:S(2)}) async-start(bf16[8,16,4096]{2,1,0:T(8,128)(2,1)} %bitcast.53), calls=%async_computation.1 | async-start | bytes 2097152 | tf_op jit(solution)/shard_map/all_to_all | solution.py:42
  68.1 42.1 %all-to-all-start.2 = ((bf16[8,48,4096]{2,1,0:T(8,128)(2,1)}), bf16[8,48,4096]{2,1,0:T(8,128)(2,1)S(1)}, u32[]{:S(2)}, u32[]{:S(2)}) async-start(bf16[8,48,4096]{2,1,0:T(8,128)(2,1)} %bitcast.8), calls=%async_computation.2 | async-start | bytes 6291456 | tf_op jit(solution)/shard_map/all_to_all | solution.py:42
  72.2 7.0 %collective-permute-start.2 = (s32[1,128]{1,0:T(1,128)S(1)}, s32[1,128]{1,0:T(1,128)S(1)}, u32[]{:S(2)}, u32[]{:S(2)}) collective-permute-start(s32[1,128]{1,0:T(1,128)S(1)} %broadcast_in_dim.373), channel_id=1, source_target_pairs={{0,1},{1,2},{2,3},{3,0},{4,5},{5,6},{6,7},{7,4},{8,9},{9,10},{10,1... | collective-permute-start | bytes 1544 | tf_op jit(solution)/shard_map/ppermute | solution.py:21
  72.9 7.7 %collective-permute-start.3 = (s32[1,128]{1,0:T(1,128)S(1)}, s32[1,128]{1,0:T(1,128)S(1)}, u32[]{:S(2)}, u32[]{:S(2)}) collective-permute-start(s32[1,128]{1,0:T(1,128)S(1)} %broadcast_in_dim.378), channel_id=1, source_target_pairs={{0,2},{1,3},{2,0},{3,1},{4,6},{5,7},{6,4},{7,5},{8,10},{9,11},{10,... | collective-permute-start | bytes 1544 | tf_op jit(solution)/shard_map/ppermute | solution.py:21
  75.0 6.5 %collective-permute-start.4 = (s32[1,128]{1,0:T(1,128)S(1)}, s32[1,128]{1,0:T(1,128)S(1)}, u32[]{:S(2)}, u32[]{:S(2)}) collective-permute-start(s32[1,128]{1,0:T(1,128)S(1)} %broadcast_in_dim.383), channel_id=1, source_target_pairs={{0,3},{1,0},{2,1},{3,2},{4,7},{5,4},{6,5},{7,6},{8,11},{9,8},{10,9... | collective-permute-start | bytes 1544 | tf_op jit(solution)/shard_map/ppermute | solution.py:21
  110.2 44.4 %all-to-all-start.3 = ((bf16[8,48,4096]{2,1,0:T(8,128)(2,1)}), bf16[8,48,4096]{2,1,0:T(8,128)(2,1)}, u32[]{:S(2)}, u32[]{:S(2)}) async-start(bf16[8,48,4096]{2,1,0:T(8,128)(2,1)} %bitcast.50), calls=%async_computation.3 | async-start | bytes 6291456 | tf_op jit(solution)/shard_map/all_to_all | solution.py:42
  114.7 83.8 %reduce-scatter.2.cloned.1.call-start = ((), (), s32[]{:S(2)}) async-start(), calls=%async_computation.7 | async-start | bytes 5242880 | tf_op jit(solution)/shard_map/reduce_scatter | solution.py:513
  142.5 6.5 %collective-permute-start.12 = (f32[1,64]{1,0:T(1,128)S(1)}, f32[1,64]{1,0:T(1,128)S(1)}, u32[]{:S(2)}, u32[]{:S(2)}) collective-permute-start(f32[1,64]{1,0:T(1,128)S(1)} %bitcast.85), channel_id=1, source_target_pairs={{0,16},{16,0},{32,48},{48,32},{64,80},{80,64},{96,112},{112,96},{1... | collective-permute-start | bytes 776 | tf_op jit(solution)/shard_map/ppermute | solution.py:56
  142.6 8.1 %collective-permute-start.13 = (f32[1,64]{1,0:T(1,128)S(1)}, f32[1,64]{1,0:T(1,128)S(1)}, u32[]{:S(2)}, u32[]{:S(2)}) collective-permute-start(f32[1,64]{1,0:T(1,128)S(1)} %bitcast.84), channel_id=1, source_target_pairs={{0,32},{16,48},{32,64},{48,80},{64,96},{80,112},{96,0},{112,16},{1... | collective-permute-start | bytes 776 | tf_op jit(solution)/shard_map/ppermute | solution.py:56
  144.5 8.5 %collective-permute-start.14 = (f32[1,64]{1,0:T(1,128)S(1)}, f32[1,64]{1,0:T(1,128)S(1)}, u32[]{:S(2)}, u32[]{:S(2)}) collective-permute-start(f32[1,64]{1,0:T(1,128)S(1)} %bitcast.81), channel_id=1, source_target_pairs={{0,48},{16,32},{32,80},{48,64},{64,112},{80,96},{96,16},{112,0},{1... | collective-permute-start | bytes 776 | tf_op jit(solution)/shard_map/ppermute | solution.py:56
  145.7 7.4 %collective-permute-start.15 = (f32[1,64]{1,0:T(1,128)S(1)}, f32[1,64]{1,0:T(1,128)S(1)}, u32[]{:S(2)}, u32[]{:S(2)}) collective-permute-start(f32[1,64]{1,0:T(1,128)S(1)} %bitcast.80), channel_id=1, source_target_pairs={{0,64},{16,80},{32,96},{48,112},{64,0},{80,16},{96,32},{112,48},{1... | collective-permute-start | bytes 776 | tf_op jit(solution)/shard_map/ppermute | solution.py:56
  147.2 5.9 %collective-permute-start.16 = (f32[1,64]{1,0:T(1,128)S(1)}, f32[1,64]{1,0:T(1,128)S(1)}, u32[]{:S(2)}, u32[]{:S(2)}) collective-permute-start(f32[1,64]{1,0:T(1,128)S(1)} %bitcast.78), channel_id=1, source_target_pairs={{0,80},{16,64},{32,112},{48,96},{64,16},{80,0},{96,48},{112,32},{1... | collective-permute-start | bytes 776 | tf_op jit(solution)/shard_map/ppermute | solution.py:56
  163.0 15.3 %collective-permute-start.19 = (bf16[64,4096]{1,0:T(8,128)(2,1)S(1)}, bf16[64,4096]{1,0:T(8,128)(2,1)S(1)}, u32[]{:S(2)}, u32[]{:S(2)}) collective-permute-start(bf16[64,4096]{1,0:T(8,128)(2,1)S(1)} %get-tuple-element.42), channel_id=1, source_target_pairs={{0,4},{4,8},{8,12},{12,0},{1,5},{5,9},{9,13},{13,1},{2,6},{6,10},{... | collective-permute-start | bytes 1572872 | tf_op jit(solution)/shard_map/ppermute | solution.py:21
  163.2 15.1 %collective-permute-start.20 = (bf16[64,4096]{1,0:T(8,128)(2,1)S(1)}, bf16[64,4096]{1,0:T(8,128)(2,1)S(1)}, u32[]{:S(2)}, u32[]{:S(2)}) collective-permute-start(bf16[64,4096]{1,0:T(8,128)(2,1)S(1)} %get-tuple-element.47), channel_id=1, source_target_pairs={{0,12},{4,0},{8,4},{12,8},{1,13},{5,1},{9,5},{13,9},{2,14},{6,2},{... | collective-permute-start | bytes 1572872 | tf_op jit(solution)/shard_map/ppermute | solution.py:21
  180.4 27.9 %collective-permute-start.24 = (bf16[128,4096]{1,0:T(8,128)(2,1)}, bf16[128,4096]{1,0:T(8,128)(2,1)}, u32[]{:S(2)}, u32[]{:S(2)}) collective-permute-start(bf16[128,4096]{1,0:T(8,128)(2,1)} %get-tuple-element.48), channel_id=1, source_target_pairs={{0,4},{4,8},{8,12},{12,0},{1,5},{5,9},{9,13},{13,1},{2,6},{6,10},{... | collective-permute-start | bytes 3145736 | tf_op jit(solution)/shard_map/ppermute | solution.py:21
  181.2 27.1 %collective-permute-start.25 = (bf16[128,4096]{1,0:T(8,128)(2,1)}, bf16[128,4096]{1,0:T(8,128)(2,1)}, u32[]{:S(2)}, u32[]{:S(2)}) collective-permute-start(bf16[128,4096]{1,0:T(8,128)(2,1)} %get-tuple-element.53), channel_id=1, source_target_pairs={{0,12},{4,0},{8,4},{12,8},{1,13},{5,1},{9,5},{13,9},{2,14},{6,2},{... | collective-permute-start | bytes 3145736 | tf_op jit(solution)/shard_map/ppermute | solution.py:21
  183.7 24.6 %all-to-all-start.4 = ((bf16[8,16,4096]{2,1,0:T(8,128)(2,1)}), bf16[8,16,4096]{2,1,0:T(8,128)(2,1)S(1)}, u32[]{:S(2)}, u32[]{:S(2)}) async-start(bf16[8,16,4096]{2,1,0:T(8,128)(2,1)} %bitcast.31), calls=%async_computation.5 | async-start | bytes 2097152 | tf_op jit(solution)/shard_map/all_to_all | solution.py:42
  206.1 7.3 %collective-permute-start.27 = (f32[32,128]{1,0:T(8,128)S(1)}, f32[32,128]{1,0:T(8,128)S(1)}, u32[]{:S(2)}, u32[]{:S(2)}) collective-permute-start(f32[32,128]{1,0:T(8,128)S(1)} %add.387), channel_id=1, source_target_pairs={{0,12},{4,8},{8,4},{12,0},{1,13},{5,9},{9,5},{13,1},{2,14},{6,10},... | collective-permute-start | bytes 49160 | tf_op jit(solution)/shard_map/ppermute | solution.py:37
  (79 other events, 720.1 us)
Sparse Core Ops, SparseCore 0:
  34.8 44.7 all-gather.1
  153.1 43.6 reduce-scatter.1

commit v9 on v8

--- a/solution.py
+++ b/solution.py
@@ -374,18 +374,18 @@
 
     return pl.pallas_call(
         body,
-        grid=(width // tile(width),),
+        grid=(width // (2 * tile(width)),),
         in_specs=[
             whole(coeff.shape),
-            columns(queries.shape[0], width),
+            columns(queries.shape[0], width, 2),
             whole(put.shape),
-            columns(arrived.shape[0], width),
+            columns(arrived.shape[0], width, 2),
         ],
-        out_specs=[columns(own, width)] + [columns(size, width) for size in sizes],
+        out_specs=[columns(own, width, 2)] + [columns(size, width, 2) for size in sizes],
         out_shape=[
             jax.ShapeDtypeStruct((size, width), jnp.bfloat16) for size in (own, *sizes)
         ],
-        compiler_params=params(20),
+        compiler_params=params(32),
         cost_estimate=LARGE,
         name="passage_side",
     )(coeff, queries, put, arrived)

time: 222 us -> 222 us (level)
  no operation moved by 1% of the time
where the time goes in v9:
time: 222 us; the launch traced here: 221 us
  starting transfers between devices  64 us (29%)
  waiting for transfers between devices  59.2 us (27%)
  Pallas kernels  39.6 us (18%)
  local copies, waits for them, and re-layouts  34.3 us (15%)
  between operations  15.1 us (7%)
  other arithmetic  8.6 us (4%)
    unnamed x139, local copies, waits for them, and re-layouts  28.4 us
    ppermute x14, waiting for transfers between devices, shift(): lax.ppermute(value, axis, [(i, (i + step) % RING) for i in range(RING)])  24.7 us
    ppermute x14, starting transfers between devices, shift(): lax.ppermute(value, axis, [(i, (i + step) % RING) for i in range(RING)])  20.3 us
    ppermute x7, waiting for transfers between devices, pair_sum(): return value + lax.ppermute(value, axis, pairs)  16.9 us
    all_to_all x4, starting transfers between devices, group_rows(): return lax.all_to_all(blocks, GROUPS, 0, 0, tiled=True).reshape(rows.shape)  16.1 us
    all_to_all x4, waiting for transfers between devices, group_rows(): return lax.all_to_all(blocks, GROUPS, 0, 0, tiled=True).reshape(rows.shape)  10.8 us
    ppermute x7, starting transfers between devices, group_table(): lax.ppermute(row, GROUPS, [(z * 2 + c, (z + z_step) % z_count * 2 + (c ^...  10.4 us
    ppermute x7, starting transfers between devices, pair_sum(): return value + lax.ppermute(value, axis, pairs)  8.73 us
  transfers between devices with their start and end apart: 35, of which 14 were waited for; matrix products, arithmetic and copies ran while one was open for 7% of the time, Pallas kernels for 17%

profile of v9, /device:TPU:0, one launch (start us, length us, event | category | flops | bytes accessed | tf_op | source)
XLA Modules:
  0.0 220.7 jit_solution(16950364148811245261)
XLA Ops:
  15.5 8.2 %all-to-all-start = ((s32[32,1,16]{2,1,0:T(1,128)}), s32[32,1,16]{2,1,0:T(1,128)S(1)}, u32[]{:S(2)}, u32[]{:S(2)}) async-start(s32[32,1,16]{2,1,0:T(1,128)} %bitcast), calls=%async_computation | async-start | bytes 32768 | tf_op jit(solution)/shard_map/all_to_all | solution.py:451
  25.4 5.5 %all-to-all-done = s32[32,1,16]{2,1,0:T(1,128)S(1)} async-done(((s32[32,1,16]{2,1,0:T(1,128)}), s32[32,1,16]{2,1,0:T(1,128)S(1)}, u32[]{:S(2)}, u32[]{:S(2)}) %all-to-all-start) | async-done | bytes 2080 | tf_op jit(solution)/shard_map/all_to_all | solution.py:451
  35.2 2.9 %collective-permute-start.5 = (bf16[128,4096]{1,0:T(8,128)(2,1)}, bf16[128,4096]{1,0:T(8,128)(2,1)S(1)}, u32[]{:S(2)}, u32[]{:S(2)}) collective-permute-start(bf16[128,4096]{1,0:T(8,128)(2,1)} %constant_dynamic-update-slice_fusion), channel_id=1, source_target_pairs={{0,12},{4,0},{8,4},{12,8},{1,13},{5,1},{9,5},{13,9},{2,14},{6,2},{... | collective-permute-start | bytes 3145736 | tf_op jit(solution)/shard_map/ppermute | solution.py:21
  40.3 3.6 %all-to-all-start.1 = ((bf16[8,16,4096]{2,1,0:T(8,128)(2,1)}), bf16[8,16,4096]{2,1,0:T(8,128)(2,1)S(1)}, u32[]{:S(2)}, u32[]{:S(2)}) async-start(bf16[8,16,4096]{2,1,0:T(8,128)(2,1)} %bitcast.53), calls=%async_computation.1 | async-start | bytes 2097152 | tf_op jit(solution)/shard_map/all_to_all | solution.py:42
  44.4 16.8 %collective-permute-done.6.refs_4_.refs_2_ = bf16[128,4096]{1,0:T(8,128)(2,1)S(1)} collective-permute-done((bf16[128,4096]{1,0:T(8,128)(2,1)}, bf16[128,4096]{1,0:T(8,128)(2,1)S(1)}, u32[]{:S(2)}, u32[]{:S(2)}) %collective-permute-start.6) | collective-permute-done | bytes 1048608 | tf_op jit(solution)/shard_map/ppermute | solution.py:21
  63.7 3.4 %pick_rows.7 = bf16[384,4096]{1,0:T(8,128)(2,1)} custom-call(bf16[384,384]{1,0:T(8,128)(2,1)S(1)} %compare_convert_fusion.matrix_ref, bf16[64,4096]{1,0:T(8,128)(2,1)S(1)} %copy-done.20, bf16[128,4096]{1,0:T(8,128)(2,1)S(1)} %collective-permute-done.5.refs_3_.refs_1_, bf16[128,4096]{1,0:T(8,128)(2,1)S(1)} %collective-permute-done.6.refs_4_.refs_2_, ...), custom_call_target="tpu_custom_call" | custom-call | flops 1 | bytes 1 | tf_op jit(solution)/shard_map/pick_rows/pallas_call | solution.py:189
  68.1 3.8 %all-to-all-start.2 = ((bf16[8,48,4096]{2,1,0:T(8,128)(2,1)}), bf16[8,48,4096]{2,1,0:T(8,128)(2,1)S(1)}, u32[]{:S(2)}, u32[]{:S(2)}) async-start(bf16[8,48,4096]{2,1,0:T(8,128)(2,1)} %bitcast.8), calls=%async_computation.2 | async-start | bytes 6291456 | tf_op jit(solution)/shard_map/all_to_all | solution.py:42
  94.0 4.3 %line_scores.1.near_ref = f32[640,512]{1,0:T(8,128)S(1)} custom-call(bf16[512,4096]{1,0:T(8,128)(2,1)S(1)} %copy-done.1, bf16[64,4096]{1,0:T(8,128)(2,1)S(1)} %copy-done.24, bf16[64,4096]{1,0:T(8,128)(2,1)S(1)} %copy-done.27, bf16[64,4096]{1,0:T(8,128)(2,1)S(1)} %copy-done.21, bf16[128,4096]{1,0:T(8,128)(2,1)S(1)} %copy-done.10, ...), custom_call_target="tpu_custom_call" | custom-call | flops 1 | bytes 1 | tf_op jit(solution)/shard_map/line_scores/pallas_call | solution.py:216
  99.4 10.8 %all-to-all-done.2 = bf16[8,48,4096]{2,1,0:T(8,128)(2,1)S(1)} async-done(((bf16[8,48,4096]{2,1,0:T(8,128)(2,1)}), bf16[8,48,4096]{2,1,0:T(8,128)(2,1)S(1)}, u32[]{:S(2)}, u32[]{:S(2)}) %all-to-all-start.2) | async-done | bytes 3145760 | tf_op jit(solution)/shard_map/all_to_all | solution.py:42
  110.2 4.4 %all-to-all-start.3 = ((bf16[8,48,4096]{2,1,0:T(8,128)(2,1)}), bf16[8,48,4096]{2,1,0:T(8,128)(2,1)}, u32[]{:S(2)}, u32[]{:S(2)}) async-start(bf16[8,48,4096]{2,1,0:T(8,128)(2,1)} %bitcast.50), calls=%async_computation.3 | async-start | bytes 6291456 | tf_op jit(solution)/shard_map/all_to_all | solution.py:42
  119.4 3.7 %far_scores.1 = (f32[384,512]{1,0:T(8,128)S(1)}, f32[1,512]{1,0:T(1,128)S(1)}) custom-call(f32[640,512]{1,0:T(8,128)S(1)} %copy-done.30, bf16[512,512]{1,0:T(8,128)(2,1)S(1)} %copy-done.39, bf16[512,4096]{1,0:T(8,128)(2,1)S(1)} %copy-done.2, bf16[384,4096]{1,0:T(8,128)(2,1)S(1)} %bitcast.48), custom_call_target="tpu_custom_call" | custom-call | flops 99999997952 | bytes 100000000 | tf_op jit(solution)/shard_map/far_scores/pallas_call | solution.py:260
  123.7 2.7 %collective-permute-start.8 = (f32[8,128]{1,0:T(8,128)S(1)}, f32[8,128]{1,0:T(8,128)S(1)}, u32[]{:S(2)}, u32[]{:S(2)}) collective-permute-start(f32[8,128]{1,0:T(8,128)S(1)} %pad_maximum_fusion.1), channel_id=1, source_target_pairs={{0,3},{1,0},{2,1},{3,2},{4,7},{5,4},{6,5},{7,6},{8,11},{9,8},{10,9... | collective-permute-start | bytes 12296 | tf_op jit(solution)/shard_map/ppermute | solution.py:21
  128.0 3.5 %collective-permute-done.9 = f32[8,128]{1,0:T(8,128)S(1)} collective-permute-done((f32[8,128]{1,0:T(8,128)S(1)}, f32[8,128]{1,0:T(8,128)S(1)}, u32[]{:S(2)}, u32[]{:S(2)}) %collective-permute-start.9) | collective-permute-done | bytes 4128 | tf_op jit(solution)/shard_map/ppermute | solution.py:21
  131.8 7.6 %query_side.1 = (bf16[512,4096]{1,0:T(8,128)(2,1)S(1)}, f32[1,4096]{1,0:T(1,128)S(1)}, f32[8,512]{1,0:T(8,128)S(1)}, f32[1,512]{1,0:T(1,128)S(1)}, bf16[512,512]{1,0:T(8,128)(2,1)S(1)}) custom-call(f32[640,512]{1,0:T(8,128)S(1)} %copy-done.31, f32[384,512]{1,0:T(8,128)S(1)} %get-tuple-element.36.far_ref, bf16[512,512]{1,0:T(8,128)(2,1)S(1)} %copy-done.40, ...), custom_call_target="tpu_custom_call" | custom-call | flops 1 | bytes 1 | tf_op jit(solution)/shard_map/query_side/pallas_call | solution.py:326
  156.8 6.0 %passage_side.1 = (bf16[128,4096]{1,0:T(8,128)(2,1)S(1)}, bf16[128,4096]{1,0:T(8,128)(2,1)S(1)}, bf16[128,4096]{1,0:T(8,128)(2,1)S(1)}, bf16[64,4096]{1,0:T(8,128)(2,1)S(1)}, bf16[64,4096]{1,0:T(8,128)(2,1)S(1)}) custom-call(bf16[512,512]{1,0:T(8,128)(2,1)S(1)} %copy-done.50, bf16[512,4096]{1,0:T(8,128)(2,1)S(1)} %copy-done.4, ...), custom_call_target="tpu_custom_call" | custom-call | flops 99999997952 | bytes 100000000 | tf_op jit(solution)/shard_map/passage_side/pallas_call | solution.py:375
  163.0 3.1 %collective-permute-start.20 = (bf16[64,4096]{1,0:T(8,128)(2,1)S(1)}, bf16[64,4096]{1,0:T(8,128)(2,1)S(1)}, u32[]{:S(2)}, u32[]{:S(2)}) collective-permute-start(bf16[64,4096]{1,0:T(8,128)(2,1)S(1)} %get-tuple-element.47), channel_id=1, source_target_pairs={{0,12},{4,0},{8,4},{12,8},{1,13},{5,1},{9,5},{13,9},{2,14},{6,2},{... | collective-permute-start | bytes 1572872 | tf_op jit(solution)/shard_map/ppermute | solution.py:21
  166.7 3.1 %collective-permute-done.10 = f32[32,128]{1,0:T(8,128)S(1)} collective-permute-done((f32[32,128]{1,0:T(8,128)S(1)}, f32[32,128]{1,0:T(8,128)S(1)}, u32[]{:S(2)}, u32[]{:S(2)}) %collective-permute-start.10) | collective-permute-done | bytes 16416 | tf_op jit(solution)/shard_map/ppermute | solution.py:37
  169.9 3.8 %collective-permute-start.11 = (f32[32,128]{1,0:T(8,128)S(1)}, f32[32,128]{1,0:T(8,128)S(1)}, u32[]{:S(2)}, u32[]{:S(2)}) collective-permute-start(f32[32,128]{1,0:T(8,128)S(1)} %add.358), channel_id=1, source_target_pairs={{0,96},{32,64},{64,32},{96,0},{1,97},{33,65},{65,33},{97,1},{2,98}... | collective-permute-start | bytes 49160 | tf_op jit(solution)/shard_map/ppermute | solution.py:37
  175.4 2.8 %collective-permute-done.19.low_ref = bf16[64,4096]{1,0:T(8,128)(2,1)S(1)} collective-permute-done((bf16[64,4096]{1,0:T(8,128)(2,1)S(1)}, bf16[64,4096]{1,0:T(8,128)(2,1)S(1)}, u32[]{:S(2)}, u32[]{:S(2)}) %collective-permute-start.19) | collective-permute-done | bytes 524320 | tf_op jit(solution)/shard_map/ppermute | solution.py:21
  183.6 4.4 %all-to-all-start.4 = ((bf16[8,16,4096]{2,1,0:T(8,128)(2,1)}), bf16[8,16,4096]{2,1,0:T(8,128)(2,1)S(1)}, u32[]{:S(2)}, u32[]{:S(2)}) async-start(bf16[8,16,4096]{2,1,0:T(8,128)(2,1)} %bitcast.31), calls=%async_computation.5 | async-start | bytes 2097152 | tf_op jit(solution)/shard_map/all_to_all | solution.py:42
  189.8 3.5 %collective-permute-done.22 = f32[32,128]{1,0:T(8,128)S(1)} collective-permute-done((f32[32,128]{1,0:T(8,128)S(1)}, f32[32,128]{1,0:T(8,128)S(1)}, u32[]{:S(2)}, u32[]{:S(2)}) %collective-permute-start.22) | collective-permute-done | bytes 16416 | tf_op jit(solution)/shard_map/ppermute | solution.py:37
  194.5 3.8 %collective-permute-done.23 = f32[32,128]{1,0:T(8,128)S(1)} collective-permute-done((f32[32,128]{1,0:T(8,128)S(1)}, f32[32,128]{1,0:T(8,128)S(1)}, u32[]{:S(2)}, u32[]{:S(2)}) %collective-permute-start.23) | collective-permute-done | bytes 16416 | tf_op jit(solution)/shard_map/ppermute | solution.py:37
  202.1 3.8 %collective-permute-done.26 = f32[32,128]{1,0:T(8,128)S(1)} collective-permute-done((f32[32,128]{1,0:T(8,128)S(1)}, f32[32,128]{1,0:T(8,128)S(1)}, u32[]{:S(2)}, u32[]{:S(2)}) %collective-permute-start.26) | collective-permute-done | bytes 16416 | tf_op jit(solution)/shard_map/ppermute | solution.py:37
  209.4 3.8 %finish.3 = bf16[128,4096]{1,0:T(8,128)(2,1)} custom-call(bf16[128,4096]{1,0:T(8,128)(2,1)S(1)} %copy-done.38, f32[1,4096]{1,0:T(1,128)S(1)} %bitcast.58, bf16[128,4096]{1,0:T(8,128)(2,1)S(1)} %copy-done.45, bf16[128,4096]{1,0:T(8,128)(2,1)} %collective-permute-done.24.refs_1_, bf16[128,4096]{1,0:T(8,128)(2,1)} %collective-permute-done.25.refs_2_, ...), custom_call_target="tpu_custom_call" | custom-call | flops 1 | bytes 1 | tf_op jit(solution)/shard_map/finish/pallas_call | solution.py:171
  (279 shorter events, 86.3 us)
Async XLA Ops:
  10.0 21.1 %collective-permute-start.1 = (bf16[64,4096]{1,0:T(8,128)(2,1)S(1)}, bf16[64,4096]{1,0:T(8,128)(2,1)S(1)}, u32[]{:S(2)}, u32[]{:S(2)}) collective-permute-start(bf16[64,4096]{1,0:T(8,128)(2,1)S(1)} %get-tuple-element.30.refs_1_), channel_id=1, source_target_pairs={{0,4},{4,8},{8,12},{12,0},{1,5},{5,9},{9,13},{13,1},{2,6},{6,10},{... | collective-permute-start | bytes 1572872 | tf_op jit(solution)/shard_map/ppermute | solution.py:21
  11.8 20.3 %collective-permute-start = (bf16[64,4096]{1,0:T(8,128)(2,1)S(1)}, bf16[64,4096]{1,0:T(8,128)(2,1)S(1)}, u32[]{:S(2)}, u32[]{:S(2)}) collective-permute-start(bf16[64,4096]{1,0:T(8,128)(2,1)S(1)} %get-tuple-element.31.refs_0_), channel_id=1, source_target_pairs={{0,12},{4,0},{8,4},{12,8},{1,13},{5,1},{9,5},{13,9},{2,14},{6,2},{... | collective-permute-start | bytes 1572872 | tf_op jit(solution)/shard_map/ppermute | solution.py:21
  15.5 15.5 %all-to-all-start = ((s32[32,1,16]{2,1,0:T(1,128)}), s32[32,1,16]{2,1,0:T(1,128)S(1)}, u32[]{:S(2)}, u32[]{:S(2)}) async-start(s32[32,1,16]{2,1,0:T(1,128)} %bitcast), calls=%async_computation | async-start | bytes 32768 | tf_op jit(solution)/shard_map/all_to_all | solution.py:451
  23.7 61.0 %all-gather.2.cloned.1.call-start = ((), (), s32[]{:S(2)}) async-start(), calls=%async_computation.6 | async-start | bytes 5242880 | tf_op jit(solution)/shard_map/all_gather | solution.py:476
  34.8 26.4 %collective-permute-start.6 = (bf16[128,4096]{1,0:T(8,128)(2,1)}, bf16[128,4096]{1,0:T(8,128)(2,1)S(1)}, u32[]{:S(2)}, u32[]{:S(2)}) collective-permute-start(bf16[128,4096]{1,0:T(8,128)(2,1)} %constant_dynamic-update-slice_fusion.2), channel_id=1, source_target_pairs={{0,4},{4,8},{8,12},{12,0},{1,5},{5,9},{9,13},{13,1},{2,6},{6,10},{... | collective-permute-start | bytes 3145736 | tf_op jit(solution)/shard_map/ppermute | solution.py:21
  35.2 26.0 %collective-permute-start.5 = (bf16[128,4096]{1,0:T(8,128)(2,1)}, bf16[128,4096]{1,0:T(8,128)(2,1)S(1)}, u32[]{:S(2)}, u32[]{:S(2)}) collective-permute-start(bf16[128,4096]{1,0:T(8,128)(2,1)} %constant_dynamic-update-slice_fusion), channel_id=1, source_target_pairs={{0,12},{4,0},{8,4},{12,8},{1,13},{5,1},{9,5},{13,9},{2,14},{6,2},{... | collective-permute-start | bytes 3145736 | tf_op jit(solution)/shard_map/ppermute | solution.py:21
  40.3 26.8 %all-to-all-start.1 = ((bf16[8,16,4096]{2,1,0:T(8,128)(2,1)}), bf16[8,16,4096]{2,1,0:T(8,128)(2,1)S(1)}, u32[]{:S(2)}, u32[]{:S(2)}) async-start(bf16[8,16,4096]{2,1,0:T(8,128)(2,1)} %bitcast.53), calls=%async_computation.1 | async-start | bytes 2097152 | tf_op jit(solution)/shard_map/all_to_all | solution.py:42
  68.1 42.1 %all-to-all-start.2 = ((bf16[8,48,4096]{2,1,0:T(8,128)(2,1)}), bf16[8,48,4096]{2,1,0:T(8,128)(2,1)S(1)}, u32[]{:S(2)}, u32[]{:S(2)}) async-start(bf16[8,48,4096]{2,1,0:T(8,128)(2,1)} %bitcast.8), calls=%async_computation.2 | async-start | bytes 6291456 | tf_op jit(solution)/shard_map/all_to_all | solution.py:42
  72.2 7.0 %collective-permute-start.2 = (s32[1,128]{1,0:T(1,128)S(1)}, s32[1,128]{1,0:T(1,128)S(1)}, u32[]{:S(2)}, u32[]{:S(2)}) collective-permute-start(s32[1,128]{1,0:T(1,128)S(1)} %broadcast_in_dim.373), channel_id=1, source_target_pairs={{0,1},{1,2},{2,3},{3,0},{4,5},{5,6},{6,7},{7,4},{8,9},{9,10},{10,1... | collective-permute-start | bytes 1544 | tf_op jit(solution)/shard_map/ppermute | solution.py:21
  72.9 7.7 %collective-permute-start.3 = (s32[1,128]{1,0:T(1,128)S(1)}, s32[1,128]{1,0:T(1,128)S(1)}, u32[]{:S(2)}, u32[]{:S(2)}) collective-permute-start(s32[1,128]{1,0:T(1,128)S(1)} %broadcast_in_dim.378), channel_id=1, source_target_pairs={{0,2},{1,3},{2,0},{3,1},{4,6},{5,7},{6,4},{7,5},{8,10},{9,11},{10,... | collective-permute-start | bytes 1544 | tf_op jit(solution)/shard_map/ppermute | solution.py:21
  75.0 6.5 %collective-permute-start.4 = (s32[1,128]{1,0:T(1,128)S(1)}, s32[1,128]{1,0:T(1,128)S(1)}, u32[]{:S(2)}, u32[]{:S(2)}) collective-permute-start(s32[1,128]{1,0:T(1,128)S(1)} %broadcast_in_dim.383), channel_id=1, source_target_pairs={{0,3},{1,0},{2,1},{3,2},{4,7},{5,4},{6,5},{7,6},{8,11},{9,8},{10,9... | collective-permute-start | bytes 1544 | tf_op jit(solution)/shard_map/ppermute | solution.py:21
  110.2 44.4 %all-to-all-start.3 = ((bf16[8,48,4096]{2,1,0:T(8,128)(2,1)}), bf16[8,48,4096]{2,1,0:T(8,128)(2,1)}, u32[]{:S(2)}, u32[]{:S(2)}) async-start(bf16[8,48,4096]{2,1,0:T(8,128)(2,1)} %bitcast.50), calls=%async_computation.3 | async-start | bytes 6291456 | tf_op jit(solution)/shard_map/all_to_all | solution.py:42
  114.7 83.6 %reduce-scatter.2.cloned.1.call-start = ((), (), s32[]{:S(2)}) async-start(), calls=%async_computation.7 | async-start | bytes 5242880 | tf_op jit(solution)/shard_map/reduce_scatter | solution.py:513
  142.5 6.5 %collective-permute-start.12 = (f32[1,64]{1,0:T(1,128)S(1)}, f32[1,64]{1,0:T(1,128)S(1)}, u32[]{:S(2)}, u32[]{:S(2)}) collective-permute-start(f32[1,64]{1,0:T(1,128)S(1)} %bitcast.85), channel_id=1, source_target_pairs={{0,16},{16,0},{32,48},{48,32},{64,80},{80,64},{96,112},{112,96},{1... | collective-permute-start | bytes 776 | tf_op jit(solution)/shard_map/ppermute | solution.py:56
  142.6 8.1 %collective-permute-start.13 = (f32[1,64]{1,0:T(1,128)S(1)}, f32[1,64]{1,0:T(1,128)S(1)}, u32[]{:S(2)}, u32[]{:S(2)}) collective-permute-start(f32[1,64]{1,0:T(1,128)S(1)} %bitcast.84), channel_id=1, source_target_pairs={{0,32},{16,48},{32,64},{48,80},{64,96},{80,112},{96,0},{112,16},{1... | collective-permute-start | bytes 776 | tf_op jit(solution)/shard_map/ppermute | solution.py:56
  144.5 8.5 %collective-permute-start.14 = (f32[1,64]{1,0:T(1,128)S(1)}, f32[1,64]{1,0:T(1,128)S(1)}, u32[]{:S(2)}, u32[]{:S(2)}) collective-permute-start(f32[1,64]{1,0:T(1,128)S(1)} %bitcast.81), channel_id=1, source_target_pairs={{0,48},{16,32},{32,80},{48,64},{64,112},{80,96},{96,16},{112,0},{1... | collective-permute-start | bytes 776 | tf_op jit(solution)/shard_map/ppermute | solution.py:56
  145.7 7.4 %collective-permute-start.15 = (f32[1,64]{1,0:T(1,128)S(1)}, f32[1,64]{1,0:T(1,128)S(1)}, u32[]{:S(2)}, u32[]{:S(2)}) collective-permute-start(f32[1,64]{1,0:T(1,128)S(1)} %bitcast.80), channel_id=1, source_target_pairs={{0,64},{16,80},{32,96},{48,112},{64,0},{80,16},{96,32},{112,48},{1... | collective-permute-start | bytes 776 | tf_op jit(solution)/shard_map/ppermute | solution.py:56
  147.2 5.9 %collective-permute-start.16 = (f32[1,64]{1,0:T(1,128)S(1)}, f32[1,64]{1,0:T(1,128)S(1)}, u32[]{:S(2)}, u32[]{:S(2)}) collective-permute-start(f32[1,64]{1,0:T(1,128)S(1)} %bitcast.78), channel_id=1, source_target_pairs={{0,80},{16,64},{32,112},{48,96},{64,16},{80,0},{96,48},{112,32},{1... | collective-permute-start | bytes 776 | tf_op jit(solution)/shard_map/ppermute | solution.py:56
  162.8 15.3 %collective-permute-start.19 = (bf16[64,4096]{1,0:T(8,128)(2,1)S(1)}, bf16[64,4096]{1,0:T(8,128)(2,1)S(1)}, u32[]{:S(2)}, u32[]{:S(2)}) collective-permute-start(bf16[64,4096]{1,0:T(8,128)(2,1)S(1)} %get-tuple-element.42), channel_id=1, source_target_pairs={{0,4},{4,8},{8,12},{12,0},{1,5},{5,9},{9,13},{13,1},{2,6},{6,10},{... | collective-permute-start | bytes 1572872 | tf_op jit(solution)/shard_map/ppermute | solution.py:21
  163.0 15.2 %collective-permute-start.20 = (bf16[64,4096]{1,0:T(8,128)(2,1)S(1)}, bf16[64,4096]{1,0:T(8,128)(2,1)S(1)}, u32[]{:S(2)}, u32[]{:S(2)}) collective-permute-start(bf16[64,4096]{1,0:T(8,128)(2,1)S(1)} %get-tuple-element.47), channel_id=1, source_target_pairs={{0,12},{4,0},{8,4},{12,8},{1,13},{5,1},{9,5},{13,9},{2,14},{6,2},{... | collective-permute-start | bytes 1572872 | tf_op jit(solution)/shard_map/ppermute | solution.py:21
  180.2 27.9 %collective-permute-start.24 = (bf16[128,4096]{1,0:T(8,128)(2,1)}, bf16[128,4096]{1,0:T(8,128)(2,1)}, u32[]{:S(2)}, u32[]{:S(2)}) collective-permute-start(bf16[128,4096]{1,0:T(8,128)(2,1)} %get-tuple-element.48), channel_id=1, source_target_pairs={{0,4},{4,8},{8,12},{12,0},{1,5},{5,9},{9,13},{13,1},{2,6},{6,10},{... | collective-permute-start | bytes 3145736 | tf_op jit(solution)/shard_map/ppermute | solution.py:21
  181.1 27.1 %collective-permute-start.25 = (bf16[128,4096]{1,0:T(8,128)(2,1)}, bf16[128,4096]{1,0:T(8,128)(2,1)}, u32[]{:S(2)}, u32[]{:S(2)}) collective-permute-start(bf16[128,4096]{1,0:T(8,128)(2,1)} %get-tuple-element.53), channel_id=1, source_target_pairs={{0,12},{4,0},{8,4},{12,8},{1,13},{5,1},{9,5},{13,9},{2,14},{6,2},{... | collective-permute-start | bytes 3145736 | tf_op jit(solution)/shard_map/ppermute | solution.py:21
  183.6 24.6 %all-to-all-start.4 = ((bf16[8,16,4096]{2,1,0:T(8,128)(2,1)}), bf16[8,16,4096]{2,1,0:T(8,128)(2,1)S(1)}, u32[]{:S(2)}, u32[]{:S(2)}) async-start(bf16[8,16,4096]{2,1,0:T(8,128)(2,1)} %bitcast.31), calls=%async_computation.5 | async-start | bytes 2097152 | tf_op jit(solution)/shard_map/all_to_all | solution.py:42
  205.9 7.3 %collective-permute-start.27 = (f32[32,128]{1,0:T(8,128)S(1)}, f32[32,128]{1,0:T(8,128)S(1)}, u32[]{:S(2)}, u32[]{:S(2)}) collective-permute-start(f32[32,128]{1,0:T(8,128)S(1)} %add.387), channel_id=1, source_target_pairs={{0,12},{4,8},{8,4},{12,0},{1,13},{5,9},{9,5},{13,1},{2,14},{6,10},... | collective-permute-start | bytes 49160 | tf_op jit(solution)/shard_map/ppermute | solution.py:37
  (79 other events, 720.4 us)
Sparse Core Ops, SparseCore 0:
  34.8 44.7 all-gather.1
  153.1 43.6 reduce-scatter.1
